TPU v7x, 32 devices: a whole 2x2x4 slice. The times are simulated.
32 devices in a mesh: section: 2 (over y), seq: 4 (over x, core), tensor: 4 (over z).
Axes of the slice: x: 2, y: 2, z: 4, core: 2. Of those that a mesh axis runs over, the one named last changes fastest.
Arguments:
- inputs: bfloat16 [2, 4096, 1024], P(None, ('seq', 'tensor')), may hold values from -6 to 6
- cotangent: bfloat16 [2, 4096, 1024], P(None, ('seq', 'tensor')), may hold values from -6 to 6
- lengths: int32 [2, 4], replicated, may hold values from 1 to 3584, 4096 in all within a row
- w_query: bfloat16 [2, 1024, 1024], P('section', 'seq', 'tensor'), may hold values from -0.1875 to 0.1875
- w_key: bfloat16 [2, 1024, 1024], P('section', 'seq', 'tensor'), may hold values from -0.1875 to 0.1875
- w_value: bfloat16 [2, 1024, 1024], P('section', 'seq', 'tensor'), may hold values from -0.1875 to 0.1875
- w_out: bfloat16 [2, 1024, 1024], P('section', 'tensor', 'seq'), may hold values from -0.75 to 0.75
- w_gate: bfloat16 [2, 1024, 2816], P('section', 'seq', 'tensor'), may hold values from -0.1875 to 0.1875
- w_up: bfloat16 [2, 1024, 2816], P('section', 'seq', 'tensor'), may hold values from -0.1875 to 0.1875
- w_down: bfloat16 [2, 2816, 1024], P('section', 'tensor', 'seq'), may hold values from -0.109375 to 0.109375
- attn_gain: float32 [2, 1024], P('section'), may hold values from 0.5 to 1.5
- mlp_gain: float32 [2, 1024], P('section'), may hold values from 0.5 to 1.5
Outputs:
- layer_out: bfloat16 [2, 2, 4096, 1024], P('section', None, ('seq', 'tensor'))
- input_grad: float32 [2, 2, 4096, 1024], P('section', None, ('seq', 'tensor'))
- grad_query: float32 [2, 1024, 1024], P('section', 'seq', 'tensor')
- grad_key: float32 [2, 1024, 1024], P('section', 'seq', 'tensor')
- grad_value: float32 [2, 1024, 1024], P('section', 'seq', 'tensor')
- grad_out: float32 [2, 1024, 1024], P('section', 'tensor', 'seq')
- grad_gate: float32 [2, 1024, 2816], P('section', 'seq', 'tensor')
- grad_up: float32 [2, 1024, 2816], P('section', 'seq', 'tensor')
- grad_down: float32 [2, 2816, 1024], P('section', 'tensor', 'seq')
- grad_attn_gain: float32 [2, 1024], P('section', ('seq', 'tensor'))
- grad_mlp_gain: float32 [2, 1024], P('section', ('seq', 'tensor'))
Inputs may be any that keep to these rules, and one draw needn't show every extreme that they name: `lengths`: each row lists the 4 documents of one micro-batch's packed row in order; they sum to 4096, and the longest has exactly 3584 tokens.
All inputs are finite; a program needn't handle non-finite values.
Results may differ from a plain program's by a relative error of at most 0.029.
Values may be sent and summed in bfloat16 or wider, within the bound.
A program may use at most 256 MiB of HBM per device.

v0:
```python
import math

import jax
import jax.numpy as jnp
from jax import lax
from jax.sharding import PartitionSpec as P

HS = 64


EPSILON = 1e-05
NEGATIVE = -1e30


def shifted(shard, axis, by):
    peers = lax.axis_size(axis)
    pairs = [(i, i + by) for i in range(peers) if 0 <= i + by < peers]
    return lax.ppermute(shard, axis, pairs)


def product(left, right):
    return jnp.dot(left, right, preferred_element_type=jnp.float32)


def inner_rows(left, right):
    return lax.dot_general(
        left, right, (((0,), (0,)), ((), ())), preferred_element_type=jnp.float32
    )


def against(left, right):
    return lax.dot_general(
        left, right, (((1,), (1,)), ((), ())), preferred_element_type=jnp.float32
    )


def doc_table(length_row, places):
    doc_ends = jnp.cumsum(length_row)
    doc_starts = doc_ends - length_row
    segment = jnp.sum((places[:, None] >= doc_ends[None, :]).astype(jnp.int32), axis=1)
    member = segment[:, None] == jnp.arange(length_row.shape[0], dtype=jnp.int32)[None, :]
    offset = jnp.sum(jnp.where(member, doc_starts[None, :], 0), axis=1)
    return (segment, places - offset)


def rotate(matrix, within, direction):
    row_count = matrix.shape[0]
    head_count = matrix.shape[1] // HS
    half_size = HS // 2
    frequency = jnp.exp(jnp.arange(half_size, dtype=jnp.float32) * (-math.log(10000.0) / half_size))
    angles = within.astype(jnp.float32)[:, None] * frequency[None, :]
    cosine = jnp.cos(angles)[:, None, :]
    sine_part = direction * jnp.sin(angles)[:, None, :]
    paired = matrix.reshape(row_count, head_count, 2, half_size)
    former = paired[:, :, 0, :]
    latter = paired[:, :, 1, :]
    turned = jnp.stack(
        [former * cosine - latter * sine_part, latter * cosine + former * sine_part], axis=2
    )
    return turned.reshape(row_count, head_count * HS)


def norm_rows(values, gain_row):
    inverse = lax.rsqrt(jnp.mean(values * values, axis=-1, keepdims=True) + EPSILON)
    unit_rows = values * inverse
    return (unit_rows, inverse, (unit_rows * gain_row).astype(jnp.bfloat16))


def norm_back(grad_normed, unit_rows, inverse, gain_row):
    shaped = grad_normed * gain_row
    inner = jnp.mean(shaped * unit_rows, axis=-1, keepdims=True)
    return (inverse * (shaped - unit_rows * inner), jnp.sum(grad_normed * unit_rows, axis=0))


def spread(values):
    return lax.all_gather(values, "tensor", axis=0, tiled=True)


def fold_rows(values):
    return lax.psum_scatter(
        values.astype(jnp.bfloat16), "tensor", scatter_dimension=0, tiled=True
    ).astype(jnp.float32)


def allowed_mask(places, segment, key_places, key_segment):
    return (key_places[None, :] <= places[:, None]) & (key_segment[None, :] == segment[:, None])


def project(normed_all, matrices, within, mixin, on_first):
    query_rows = rotate(product(normed_all, matrices[0]), within, 1.0).astype(jnp.bfloat16)
    key_rows = rotate(product(normed_all, matrices[1]), within, 1.0).astype(jnp.bfloat16)
    value_raw = product(normed_all, matrices[2])
    value_rows = jnp.where(
        on_first, value_raw, 0.5 * value_raw + 0.5 * mixin.astype(jnp.float32)
    ).astype(jnp.bfloat16)
    return (query_rows, key_rows, value_rows)


def cycle_attend(query_rows, key_rows, value_rows, places, segment, length_row):
    row_count = query_rows.shape[0]
    head_count = query_rows.shape[1] // HS
    query_heads = query_rows.reshape(row_count, head_count, HS)
    largest = jnp.full((head_count, row_count), NEGATIVE, jnp.float32)
    piece_keys = lax.all_gather(key_rows, "seq", axis=0, tiled=True)
    piece_values = lax.all_gather(value_rows, "seq", axis=0, tiled=True)
    piece_rows = piece_keys.shape[0]
    key_places = jnp.arange(piece_rows, dtype=jnp.int32)
    key_segment = doc_table(length_row, key_places)[0]
    allowed = allowed_mask(places, segment, key_places, key_segment)
    scores = jnp.einsum(
        "qhd,khd->hqk",
        query_heads,
        piece_keys.reshape(piece_rows, head_count, HS),
        preferred_element_type=jnp.float32,
    ) * HS ** (-0.5)
    masked = jnp.where(allowed[None], scores, NEGATIVE)
    newest = jnp.maximum(largest, jnp.max(masked, axis=2))
    weights = jnp.where(allowed[None], jnp.exp(masked - newest[:, :, None]), 0.0)
    totals = jnp.sum(weights, axis=2)
    summed = jnp.einsum(
        "hqk,khd->hqd",
        weights.astype(jnp.bfloat16),
        piece_values.reshape(piece_rows, head_count, HS),
        preferred_element_type=jnp.float32,
    )
    largest, totals, summed = (newest, totals, summed)
    attended = summed / totals[:, :, None]
    return jnp.transpose(attended, (1, 0, 2)).reshape(row_count, head_count * HS)


def forward_layer(residual, mixin, on_first, matrices, gain_pair, places, length_row):
    segment, within = doc_table(length_row, places)
    normed_in = norm_rows(residual, gain_pair[0])[2]
    normed_all = spread(normed_in)
    query_rows, key_rows, value_rows = project(normed_all, matrices, within, mixin, on_first)
    attended = cycle_attend(query_rows, key_rows, value_rows, places, segment, length_row)
    middle = residual + fold_rows(product(attended.astype(jnp.bfloat16), matrices[3]))
    normed_mid = norm_rows(middle, gain_pair[1])[2]
    normed_mid_all = spread(normed_mid)
    gate_rows = product(normed_mid_all, matrices[4])
    up_rows = product(normed_mid_all, matrices[5])
    hidden = (jax.nn.silu(gate_rows) * up_rows).astype(jnp.bfloat16)
    return (middle + fold_rows(product(hidden, matrices[6])), value_rows)


def backward_layer(
    residual, mixin, grad_top, extra_values, on_first, matrices, gain_pair, places, length_row
):
    segment, within = doc_table(length_row, places)
    unit_in, inverse_in, normed_in = norm_rows(residual, gain_pair[0])
    normed_all = spread(normed_in)
    query_rows, key_rows, value_rows = project(normed_all, matrices, within, mixin, on_first)
    all_keys, all_values = (
        lax.all_gather(key_rows, "seq", axis=0, tiled=True),
        lax.all_gather(value_rows, "seq", axis=0, tiled=True),
    )
    row_count = query_rows.shape[0]
    head_count = query_rows.shape[1] // HS
    total_rows = all_keys.shape[0]
    block_count = total_rows // row_count
    query_heads = query_rows.reshape(row_count, head_count, HS)
    key_blocks = all_keys.reshape(block_count, row_count, head_count, HS)
    value_blocks = all_values.reshape(block_count, row_count, head_count, HS)
    block_numbers = jnp.arange(block_count, dtype=jnp.int32)

    def block_scores(block_number, block_keys):
        key_places = block_number * row_count + jnp.arange(row_count, dtype=jnp.int32)
        key_segment = doc_table(length_row, key_places)[0]
        allowed = allowed_mask(places, segment, key_places, key_segment)
        scores = jnp.einsum(
            "qhd,khd->hqk", query_heads, block_keys, preferred_element_type=jnp.float32
        ) * HS ** (-0.5)
        return (allowed, jnp.where(allowed[None], scores, NEGATIVE))

    def first_pass(running, block_item):
        largest, totals, summed = running
        block_number, block_keys, block_values = block_item
        allowed, masked = block_scores(block_number, block_keys)
        newest = jnp.maximum(largest, jnp.max(masked, axis=2))
        rescale = jnp.exp(largest - newest)
        weights = jnp.where(allowed[None], jnp.exp(masked - newest[:, :, None]), 0.0)
        totals = totals * rescale + jnp.sum(weights, axis=2)
        summed = summed * rescale[:, :, None] + jnp.einsum(
            "hqk,khd->hqd",
            weights.astype(jnp.bfloat16),
            block_values,
            preferred_element_type=jnp.float32,
        )
        return ((newest, totals, summed), None)

    start_state = (
        jnp.full((head_count, row_count), NEGATIVE, jnp.float32),
        jnp.zeros((head_count, row_count), jnp.float32),
        jnp.zeros((head_count, row_count, HS), jnp.float32),
    )
    (largest, totals, summed), _ = lax.scan(
        first_pass, start_state, (block_numbers, key_blocks, value_blocks)
    )
    attended = summed / totals[:, :, None]
    attended_low = (
        jnp.transpose(attended, (1, 0, 2)).reshape(row_count, head_count * HS).astype(jnp.bfloat16)
    )
    middle = residual + fold_rows(product(attended_low, matrices[3]))
    unit_mid, inverse_mid, normed_mid = norm_rows(middle, gain_pair[1])
    normed_mid_all = spread(normed_mid)
    gate_rows = product(normed_mid_all, matrices[4])
    up_rows = product(normed_mid_all, matrices[5])
    sigmoid_gate = jax.nn.sigmoid(gate_rows)
    activated = gate_rows * sigmoid_gate
    hidden = (activated * up_rows).astype(jnp.bfloat16)
    grad_top_all = spread(grad_top.astype(jnp.bfloat16))
    grad_w_down = inner_rows(hidden, grad_top_all)
    grad_hidden = against(grad_top_all, matrices[6])
    grad_gate = (
        grad_hidden * up_rows * sigmoid_gate * (1.0 + gate_rows * (1.0 - sigmoid_gate))
    ).astype(jnp.bfloat16)
    grad_up = (grad_hidden * activated).astype(jnp.bfloat16)
    grad_w_gate = inner_rows(normed_mid_all, grad_gate)
    grad_w_up = inner_rows(normed_mid_all, grad_up)
    grad_normed_mid = fold_rows(against(grad_gate, matrices[4]) + against(grad_up, matrices[5]))
    grad_middle, grad_gain_mid = norm_back(grad_normed_mid, unit_mid, inverse_mid, gain_pair[1])
    grad_middle = grad_middle + grad_top
    grad_middle_all = spread(grad_middle.astype(jnp.bfloat16))
    grad_w_out = inner_rows(attended_low, grad_middle_all)
    grad_attended = against(grad_middle_all, matrices[3]).astype(jnp.bfloat16)
    grad_heads = jnp.transpose(grad_attended.reshape(row_count, head_count, HS), (1, 0, 2))
    delta = jnp.sum(grad_heads.astype(jnp.float32) * attended, axis=2)
    scaled_grad = grad_heads.astype(jnp.float32) / totals[:, :, None]
    scaled_high = scaled_grad.astype(jnp.bfloat16)
    scaled_rest = (scaled_grad - scaled_high.astype(jnp.float32)).astype(jnp.bfloat16)
    inverse_totals = 1.0 / totals[:, :, None]

    def second_pass(grad_sum, block_item):
        block_number, block_keys, block_values = block_item
        allowed, masked = block_scores(block_number, block_keys)
        weights = jnp.where(allowed[None], jnp.exp(masked - largest[:, :, None]), 0.0)
        low_weights = weights.astype(jnp.bfloat16)
        along = jnp.einsum(
            "hqd,khd->hqk", grad_heads, block_values, preferred_element_type=jnp.float32
        )
        grad_scores = (weights * inverse_totals * (along - delta[:, :, None])).astype(jnp.bfloat16)
        grad_sum = grad_sum + jnp.einsum(
            "hqk,khd->qhd", grad_scores, block_keys, preferred_element_type=jnp.float32
        ) * HS ** (-0.5)
        block_key_grad = jnp.einsum(
            "hqk,qhd->khd", grad_scores, query_heads, preferred_element_type=jnp.float32
        ) * HS ** (-0.5)
        block_value_grad = jnp.einsum(
            "hqk,hqd->khd", low_weights, scaled_high, preferred_element_type=jnp.float32
        ) + jnp.einsum("hqk,hqd->khd", low_weights, scaled_rest, preferred_element_type=jnp.float32)
        return (grad_sum, (block_key_grad, block_value_grad))

    grad_queries, (grad_keys, grad_values) = lax.scan(
        second_pass,
        jnp.zeros((row_count, head_count, HS), jnp.float32),
        (block_numbers, key_blocks, value_blocks),
    )
    own_keys, own_values = (
        lax.psum_scatter(
            grad_keys.reshape(total_rows, head_count * HS).astype(jnp.bfloat16),
            "seq",
            scatter_dimension=0,
            tiled=True,
        ).astype(jnp.float32),
        lax.psum_scatter(
            grad_values.reshape(total_rows, head_count * HS).astype(jnp.bfloat16),
            "seq",
            scatter_dimension=0,
            tiled=True,
        ).astype(jnp.float32),
    )
    grad_value_raw = jnp.where(on_first, own_values + extra_values, 0.5 * own_values).astype(
        jnp.bfloat16
    )
    send_values = 0.5 * own_values
    grad_query_raw = rotate(grad_queries.reshape(row_count, head_count * HS), within, -1.0).astype(
        jnp.bfloat16
    )
    grad_key_raw = rotate(own_keys, within, -1.0).astype(jnp.bfloat16)
    grad_w_query = inner_rows(normed_all, grad_query_raw)
    grad_w_key = inner_rows(normed_all, grad_key_raw)
    grad_w_value = inner_rows(normed_all, grad_value_raw)
    grad_normed_in = fold_rows(
        against(grad_query_raw, matrices[0])
        + against(grad_key_raw, matrices[1])
        + against(grad_value_raw, matrices[2])
    )
    grad_in, grad_gain_in = norm_back(grad_normed_in, unit_in, inverse_in, gain_pair[0])
    weight_terms = (
        grad_w_query,
        grad_w_key,
        grad_w_value,
        grad_w_out,
        grad_w_gate,
        grad_w_up,
        grad_w_down,
    )
    return (grad_in + grad_middle, send_values, weight_terms, (grad_gain_in, grad_gain_mid))


def on_device(
    inputs,
    cotangent,
    lengths,
    w_query,
    w_key,
    w_value,
    w_out,
    w_gate,
    w_up,
    w_down,
    attn_gain,
    mlp_gain,
):
    section_index = lax.axis_index("section")
    on_first = section_index == 0
    micro_count = inputs.shape[0]
    local_rows = inputs.shape[1]
    model_width = inputs.shape[2]
    group_rows = local_rows * lax.axis_size("tensor")
    head_width = w_query.shape[2]
    row_values = local_rows * model_width
    places = lax.axis_index("seq") * group_rows + jnp.arange(group_rows, dtype=jnp.int32)
    gain_pair = (attn_gain[0], mlp_gain[0])
    gathered = (
        lax.all_gather(w_query[0], "seq", axis=0, tiled=True),
        lax.all_gather(w_key[0], "seq", axis=0, tiled=True),
        lax.all_gather(w_value[0], "seq", axis=0, tiled=True),
        lax.all_gather(w_out[0], "seq", axis=1, tiled=True),
        lax.all_gather(w_gate[0], "seq", axis=0, tiled=True),
        lax.all_gather(w_up[0], "seq", axis=0, tiled=True),
        lax.all_gather(w_down[0], "seq", axis=1, tiled=True),
    )
    recv_rows = jnp.zeros((local_rows, model_width), jnp.bfloat16)
    recv_values = jnp.zeros((group_rows, head_width), jnp.bfloat16)
    kept_inputs = jnp.zeros((micro_count, local_rows, model_width), jnp.bfloat16)
    kept_values = jnp.zeros((micro_count, group_rows, head_width), jnp.bfloat16)
    kept_outputs = jnp.zeros((micro_count, local_rows, model_width), jnp.bfloat16)
    for moment in range(micro_count + 1):
        which = moment - section_index
        usable = (which >= 0) & (which < micro_count)
        slot_index = jnp.clip(which, 0, micro_count - 1)
        own_rows = lax.dynamic_index_in_dim(inputs, slot_index, 0, keepdims=False)
        layer_in = jnp.where(on_first, own_rows, recv_rows)
        length_row = lax.dynamic_index_in_dim(lengths, slot_index, 0, keepdims=False)
        result, value_rows = forward_layer(
            layer_in.astype(jnp.float32),
            recv_values,
            on_first,
            gathered,
            gain_pair,
            places,
            length_row,
        )
        result_low = result.astype(jnp.bfloat16)
        kept_inputs = jnp.where(
            usable,
            lax.dynamic_update_index_in_dim(kept_inputs, layer_in, slot_index, 0),
            kept_inputs,
        )
        kept_values = jnp.where(
            usable,
            lax.dynamic_update_index_in_dim(kept_values, recv_values, slot_index, 0),
            kept_values,
        )
        kept_outputs = jnp.where(
            usable,
            lax.dynamic_update_index_in_dim(kept_outputs, result_low, slot_index, 0),
            kept_outputs,
        )
        if moment < micro_count:
            packed = jnp.concatenate([result_low.reshape(-1), value_rows.reshape(-1)])
            arrived = shifted(packed, "section", 1)
            recv_rows = arrived[:row_values].reshape(local_rows, model_width)
            recv_values = arrived[row_values:].reshape(group_rows, head_width)
    grad_rows_in = jnp.zeros((local_rows, model_width), jnp.float32)
    grad_values_in = jnp.zeros((group_rows, head_width), jnp.float32)
    grad_inputs = jnp.zeros((micro_count, local_rows, model_width), jnp.float32)
    weight_sums = tuple((jnp.zeros(matrix.shape, jnp.float32) for matrix in gathered))
    share_sums = (
        jnp.zeros(w_query[0].shape, jnp.float32),
        jnp.zeros(w_key[0].shape, jnp.float32),
        jnp.zeros(w_value[0].shape, jnp.float32),
        jnp.zeros(w_out[0].shape, jnp.float32),
        jnp.zeros(w_gate[0].shape, jnp.float32),
        jnp.zeros(w_up[0].shape, jnp.float32),
        jnp.zeros(w_down[0].shape, jnp.float32),
    )
    gain_sums = (jnp.zeros((model_width,), jnp.float32), jnp.zeros((model_width,), jnp.float32))
    for moment in range(micro_count + 1):
        which = moment - (1 - section_index)
        usable = (which >= 0) & (which < micro_count)
        slot_index = jnp.clip(which, 0, micro_count - 1)
        matrices = (
            lax.all_gather(w_query[0], "seq", axis=0, tiled=True),
            lax.all_gather(w_key[0], "seq", axis=0, tiled=True),
            lax.all_gather(w_value[0], "seq", axis=0, tiled=True),
            lax.all_gather(w_out[0], "seq", axis=1, tiled=True),
            lax.all_gather(w_gate[0], "seq", axis=0, tiled=True),
            lax.all_gather(w_up[0], "seq", axis=0, tiled=True),
            lax.all_gather(w_down[0], "seq", axis=1, tiled=True),
        )
        layer_in = lax.dynamic_index_in_dim(kept_inputs, slot_index, 0, keepdims=False).astype(
            jnp.float32
        )
        mixin = lax.dynamic_index_in_dim(kept_values, slot_index, 0, keepdims=False)
        length_row = lax.dynamic_index_in_dim(lengths, slot_index, 0, keepdims=False)
        own_grad = lax.dynamic_index_in_dim(cotangent, slot_index, 0, keepdims=False).astype(
            jnp.float32
        )
        grad_top = jnp.where(usable, jnp.where(on_first, grad_rows_in, own_grad), 0.0)
        extra_values = jnp.where(usable & on_first, grad_values_in, 0.0)
        grad_in, send_values, weight_terms, gain_terms = backward_layer(
            layer_in,
            mixin,
            grad_top,
            extra_values,
            on_first,
            matrices,
            gain_pair,
            places,
            length_row,
        )
        gain_sums = (gain_sums[0] + gain_terms[0], gain_sums[1] + gain_terms[1])
        weight_sums = tuple((total + term for total, term in zip(weight_sums, weight_terms)))
        grad_inputs = jnp.where(
            usable,
            lax.dynamic_update_index_in_dim(grad_inputs, grad_in, slot_index, 0),
            grad_inputs,
        )
        if moment < micro_count:
            packed = jnp.concatenate([grad_in.reshape(-1), send_values.reshape(-1)])
            arrived = shifted(packed.astype(jnp.bfloat16), "section", -1).astype(packed.dtype)
            grad_rows_in = arrived[:row_values].reshape(local_rows, model_width)
            grad_values_in = arrived[row_values:].reshape(group_rows, head_width)
    share_sums = (
        lax.psum_scatter(
            weight_sums[0].astype(jnp.bfloat16), "seq", scatter_dimension=0, tiled=True
        ).astype(jnp.float32),
        lax.psum_scatter(
            weight_sums[1].astype(jnp.bfloat16), "seq", scatter_dimension=0, tiled=True
        ).astype(jnp.float32),
        lax.psum_scatter(
            weight_sums[2].astype(jnp.bfloat16), "seq", scatter_dimension=0, tiled=True
        ).astype(jnp.float32),
        lax.psum_scatter(
            weight_sums[3].astype(jnp.bfloat16), "seq", scatter_dimension=1, tiled=True
        ).astype(jnp.float32),
        lax.psum_scatter(
            weight_sums[4].astype(jnp.bfloat16), "seq", scatter_dimension=0, tiled=True
        ).astype(jnp.float32),
        lax.psum_scatter(
            weight_sums[5].astype(jnp.bfloat16), "seq", scatter_dimension=0, tiled=True
        ).astype(jnp.float32),
        lax.psum_scatter(
            weight_sums[6].astype(jnp.bfloat16), "seq", scatter_dimension=1, tiled=True
        ).astype(jnp.float32),
    )
    gain_shares = (
        lax.psum_scatter(gain_sums[0], ("seq", "tensor"), scatter_dimension=0, tiled=True),
        lax.psum_scatter(gain_sums[1], ("seq", "tensor"), scatter_dimension=0, tiled=True),
    )
    return (
        kept_outputs[None],
        grad_inputs[None],
        share_sums[0][None],
        share_sums[1][None],
        share_sums[2][None],
        share_sums[3][None],
        share_sums[4][None],
        share_sums[5][None],
        share_sums[6][None],
        gain_shares[0][None],
        gain_shares[1][None],
    )


def solution(mesh):
    in_specs = (
        P(None, ("seq", "tensor"), None),
        P(None, ("seq", "tensor"), None),
        P(),
        P("section", "seq", "tensor"),
        P("section", "seq", "tensor"),
        P("section", "seq", "tensor"),
        P("section", "tensor", "seq"),
        P("section", "seq", "tensor"),
        P("section", "seq", "tensor"),
        P("section", "tensor", "seq"),
        P("section", None),
        P("section", None),
    )
    out_specs = (
        P("section", None, ("seq", "tensor"), None),
        P("section", None, ("seq", "tensor"), None),
        P("section", "seq", "tensor"),
        P("section", "seq", "tensor"),
        P("section", "seq", "tensor"),
        P("section", "tensor", "seq"),
        P("section", "seq", "tensor"),
        P("section", "seq", "tensor"),
        P("section", "tensor", "seq"),
        P("section", ("seq", "tensor")),
        P("section", ("seq", "tensor")),
    )
    return jax.shard_map(
        on_device, mesh=mesh, in_specs=in_specs, out_specs=out_specs, check_vma=False
    )
```

profile of v0, /device:TPU:0, one launch (start us, length us, event | category | flops | bytes accessed | tf_op | source)
XLA Modules:
  0.0 3431.2 jit_solution(17130129245580188511)
XLA Ops:
  41.5 17.9 all-gather.41.cloned.1.call-done
  86.4 27.6 fusion.144
  114.0 23.0 fusion.147
  141.1 26.8 divide_convert_fusion.2
  170.6 42.4 %reduce-scatter.29.cloned.1.call-done = bf16[256,1024]{1,0:T(8,128)(2,1)} async-done(((bf16[1024,1024]{1,0:T(8,128)(2,1)}), bf16[256,1024]{1,0:T(8,128)(2,1)}) %reduce-scatter.29.cloned.1.call-update) | async-done | bytes 524304 | tf_op jit(solution)/shard_map/reduce_scatter | solution.py:80
  218.2 14.8 all-gather.101.cloned.1.call-done
  232.9 48.1 %all-gather.47.cloned.1.call-done = bf16[1024,1024]{1,0:T(8,128)(2,1)} async-done(((bf16[256,1024]{1,0:T(8,128)(2,1)}), bf16[1024,1024]{1,0:T(8,128)(2,1)}) %all-gather.47.cloned.1.call-update) | async-done | bytes 2097168 | tf_op jit(solution)/shard_map/all_gather | solution.py:76
  286.3 14.2 all-gather.105.cloned.1.call-done
  300.5 20.8 all-gather.103.cloned.1.call-done
  331.6 41.7 %reduce-scatter.31.cloned.1.call-done = bf16[256,1024]{1,0:T(8,128)(2,1)} async-done(((bf16[1024,1024]{1,0:T(8,128)(2,1)}), bf16[256,1024]{1,0:T(8,128)(2,1)}) %reduce-scatter.31.cloned.1.call-update) | async-done | bytes 524304 | tf_op jit(solution)/shard_map/reduce_scatter | solution.py:80
  382.7 20.2 collective-permute-done
  409.1 46.8 %all-gather.49.cloned.1.call-done = bf16[1024,1024]{1,0:T(8,128)(2,1)} async-done(((bf16[256,1024]{1,0:T(8,128)(2,1)}), bf16[1024,1024]{1,0:T(8,128)(2,1)}) %all-gather.49.cloned.1.call-update) | async-done | bytes 2097168 | tf_op jit(solution)/shard_map/all_gather | solution.py:76
  470.1 13.3 all-gather.51.cloned.1.call-done
  483.4 28.9 fusion.145
  512.2 22.9 fusion.149
  539.2 27.5 divide_convert_fusion.1
  570.4 43.7 %reduce-scatter.33.cloned.1.call-done = bf16[256,1024]{1,0:T(8,128)(2,1)} async-done(((bf16[1024,1024]{1,0:T(8,128)(2,1)}), bf16[256,1024]{1,0:T(8,128)(2,1)}) %reduce-scatter.33.cloned.1.call-update) | async-done | bytes 524304 | tf_op jit(solution)/shard_map/reduce_scatter | solution.py:80
  617.5 45.4 %all-gather.55.cloned.1.call-done = bf16[1024,1024]{1,0:T(8,128)(2,1)} async-done(((bf16[256,1024]{1,0:T(8,128)(2,1)}), bf16[1024,1024]{1,0:T(8,128)(2,1)}) %all-gather.55.cloned.1.call-update) | async-done | bytes 2097168 | tf_op jit(solution)/shard_map/all_gather | solution.py:76
  678.6 40.4 %reduce-scatter.35.cloned.1.call-done = bf16[256,1024]{1,0:T(8,128)(2,1)} async-done(((bf16[1024,1024]{1,0:T(8,128)(2,1)}), bf16[256,1024]{1,0:T(8,128)(2,1)}) %reduce-scatter.35.cloned.1.call-update) | async-done | bytes 524304 | tf_op jit(solution)/shard_map/reduce_scatter | solution.py:80
  725.9 21.5 collective-permute-done.1
  755.2 47.0 %all-gather.65.cloned.1.call-done = bf16[1024,1024]{1,0:T(8,128)(2,1)} async-done(((bf16[256,1024]{1,0:T(8,128)(2,1)}), bf16[1024,1024]{1,0:T(8,128)(2,1)}) %all-gather.65.cloned.1.call-update) | async-done | bytes 2097168 | tf_op jit(solution)/shard_map/all_gather | solution.py:76
  815.0 33.4 all-gather.57.cloned.1.call-done
  879.1 16.7 all-gather.69.cloned.1.call-done
  909.9 110.8 %while.102 = (s32[]{:T(128)}, f32[4,1024]{1,0:T(4,128)S(1)}, f32[4,1024]{1,0:T(4,128)S(1)}, f32[4,1024,64]{1,2,0:T(8,128)S(1)}, s32[4]{0:T(128)S(1)}, /*index=5*...) while((s32[]{:T(128)}, f32[4,1024]{1,0:T(4,128)S(1)}, ...), condition=%wide.region_39.40_spmd.clone, body=%wide.region_35.39_spmd.clone.sunk | while | flops 1132233728 | bytes 125599976 | solution.py:196
  1021.4 28.3 fusion.146
  1052.8 23.6 fusion.151
  1080.6 26.8 divide_convert_fusion
  1111.2 42.6 %reduce-scatter.37.cloned.1.call-done = bf16[256,1024]{1,0:T(8,128)(2,1)} async-done(((bf16[1024,1024]{1,0:T(8,128)(2,1)}), bf16[256,1024]{1,0:T(8,128)(2,1)}) %reduce-scatter.37.cloned.1.call-update) | async-done | bytes 524304 | tf_op jit(solution)/shard_map/reduce_scatter | solution.py:80
  1160.7 42.5 %all-gather.77.cloned.1.call-done = bf16[1024,1024]{1,0:T(8,128)(2,1)} async-done(((bf16[256,1024]{1,0:T(8,128)(2,1)}), bf16[1024,1024]{1,0:T(8,128)(2,1)}) %all-gather.77.cloned.1.call-update) | async-done | bytes 2097168 | tf_op jit(solution)/shard_map/all_gather | solution.py:76
  1211.7 38.2 %all-gather.73.cloned.1.call-done = bf16[1024,1024]{1,0:T(8,128)(2,1)} async-done(((bf16[256,1024]{1,0:T(8,128)(2,1)}), bf16[1024,1024]{1,0:T(8,128)(2,1)}) %all-gather.73.cloned.1.call-update) | async-done | bytes 2097168 | tf_op jit(solution)/shard_map/all_gather | solution.py:76
  1258.7 37.4 %all-gather.71.cloned.1.call-done = bf16[1024,1024]{1,0:T(8,128)(2,1)} async-done(((bf16[256,1024]{1,0:T(8,128)(2,1)}), bf16[1024,1024]{1,0:T(8,128)(2,1)}) %all-gather.71.cloned.1.call-update) | async-done | bytes 2097168 | tf_op jit(solution)/shard_map/all_gather | solution.py:76
  1327.6 16.1 all-gather.81.cloned.1.call-done
  1357.7 110.3 %while.104 = (s32[]{:T(128)}, f32[4,1024]{1,0:T(4,128)S(1)}, f32[4,1024]{1,0:T(4,128)S(1)}, f32[4,1024,64]{1,2,0:T(8,128)S(1)}, s32[4]{0:T(128)S(1)}, /*index=5*...) while((s32[]{:T(128)}, f32[4,1024]{1,0:T(4,128)S(1)}, ...), condition=%wide.region_61.62_spmd.clone, body=%wide.region_57.61_spmd.clone.sunk | while | flops 1132233728 | bytes 125599976 | solution.py:196
  1471.4 44.0 %reduce-scatter.51.cloned.1.call-done = bf16[256,1024]{1,0:T(8,128)(2,1)} async-done(((bf16[1024,1024]{1,0:T(8,128)(2,1)}), bf16[256,1024]{1,0:T(8,128)(2,1)}) %reduce-scatter.51.cloned.1.call-update) | async-done | bytes 524304 | tf_op jit(solution)/shard_map/reduce_scatter | solution.py:80
  1520.3 45.3 %all-gather.75.cloned.1.call-done = bf16[1024,1024]{1,0:T(8,128)(2,1)} async-done(((bf16[256,1024]{1,0:T(8,128)(2,1)}), bf16[1024,1024]{1,0:T(8,128)(2,1)}) %all-gather.75.cloned.1.call-update) | async-done | bytes 2097168 | tf_op jit(solution)/shard_map/all_gather | solution.py:76
  1572.8 199.4 %while.103 = (s32[]{:T(128)}, f32[1024,4,64]{0,2,1:T(8,128)}, bf16[4,1024,4,64]{1,3,2,0:T(8,128)(2,1)}, bf16[4,1024,4,64]{1,3,2,0:T(8,128)(2,1)}, bf16[4,1024,4,...) while((s32[]{:T(128)}, f32[1024,4,64]{0,2,1:T(8,128)}, ...), condition=%wide.region_47.48_spmd.clone, body=%wide.region_45.47_spmd.clone.sunk | while | flops 3301192704 | bytes 232899024 | solution.py:253
  1789.5 18.5 reduce-scatter.45.cloned.1.call-done
  1815.7 26.3 reduce-scatter.47.cloned.1.call-done
  1847.8 43.9 %reduce-scatter.49.cloned.1.call-done = bf16[256,1024]{1,0:T(8,128)(2,1)} async-done(((bf16[1024,1024]{1,0:T(8,128)(2,1)}), bf16[256,1024]{1,0:T(8,128)(2,1)}) %reduce-scatter.49.cloned.1.call-update) | async-done | bytes 524304 | tf_op jit(solution)/shard_map/reduce_scatter | solution.py:80
  1901.0 25.6 collective-permute-done.2
  1951.2 37.3 %all-gather.85.cloned.1.call-done = bf16[1024,1024]{1,0:T(8,128)(2,1)} async-done(((bf16[256,1024]{1,0:T(8,128)(2,1)}), bf16[1024,1024]{1,0:T(8,128)(2,1)}) %all-gather.85.cloned.1.call-update) | async-done | bytes 2097168 | tf_op jit(solution)/shard_map/all_gather | solution.py:76
  1997.3 37.9 %all-gather.83.cloned.1.call-done = bf16[1024,1024]{1,0:T(8,128)(2,1)} async-done(((bf16[256,1024]{1,0:T(8,128)(2,1)}), bf16[1024,1024]{1,0:T(8,128)(2,1)}) %all-gather.83.cloned.1.call-update) | async-done | bytes 2097168 | tf_op jit(solution)/shard_map/all_gather | solution.py:76
  2066.9 16.0 all-gather.93.cloned.1.call-done
  2097.1 110.4 %while.106 = (s32[]{:T(128)}, f32[4,1024]{1,0:T(4,128)S(1)}, f32[4,1024]{1,0:T(4,128)S(1)}, f32[4,1024,64]{1,2,0:T(8,128)S(1)}, s32[4]{0:T(128)S(1)}, /*index=5*...) while((s32[]{:T(128)}, f32[4,1024]{1,0:T(4,128)S(1)}, ...), condition=%wide.region_83.84_spmd.clone, body=%wide.region_79.83_spmd.clone.sunk | while | flops 1132233728 | bytes 125599976 | solution.py:196
  2210.8 43.9 %reduce-scatter.61.cloned.1.call-done = bf16[256,1024]{1,0:T(8,128)(2,1)} async-done(((bf16[1024,1024]{1,0:T(8,128)(2,1)}), bf16[256,1024]{1,0:T(8,128)(2,1)}) %reduce-scatter.61.cloned.1.call-update) | async-done | bytes 524304 | tf_op jit(solution)/shard_map/reduce_scatter | solution.py:80
  2259.7 45.3 %all-gather.87.cloned.1.call-done = bf16[1024,1024]{1,0:T(8,128)(2,1)} async-done(((bf16[256,1024]{1,0:T(8,128)(2,1)}), bf16[1024,1024]{1,0:T(8,128)(2,1)}) %all-gather.87.cloned.1.call-update) | async-done | bytes 2097168 | tf_op jit(solution)/shard_map/all_gather | solution.py:76
  2312.2 198.1 %while.105 = (s32[]{:T(128)}, f32[1024,4,64]{0,2,1:T(8,128)}, bf16[4,1024,4,64]{1,3,2,0:T(8,128)(2,1)}, bf16[4,1024,4,64]{1,3,2,0:T(8,128)(2,1)}, bf16[4,1024,4,...) while((s32[]{:T(128)}, f32[1024,4,64]{0,2,1:T(8,128)}, ...), condition=%wide.region_69.70_spmd.clone, body=%wide.region_67.69_spmd.clone.sunk | while | flops 3301192704 | bytes 232899024 | solution.py:253
  2532.8 13.2 reduce-scatter.55.cloned.1.call-done
  2553.7 26.3 reduce-scatter.57.cloned.1.call-done
  2588.7 43.0 %reduce-scatter.59.cloned.1.call-done = bf16[256,1024]{1,0:T(8,128)(2,1)} async-done(((bf16[1024,1024]{1,0:T(8,128)(2,1)}), bf16[256,1024]{1,0:T(8,128)(2,1)}) %reduce-scatter.59.cloned.1.call-update) | async-done | bytes 524304 | tf_op jit(solution)/shard_map/reduce_scatter | solution.py:80
  2637.6 25.7 collective-permute-done.3
  2689.0 36.7 %all-gather.95.cloned.1.call-done = bf16[1024,1024]{1,0:T(8,128)(2,1)} async-done(((bf16[256,1024]{1,0:T(8,128)(2,1)}), bf16[1024,1024]{1,0:T(8,128)(2,1)}) %all-gather.95.cloned.1.call-update) | async-done | bytes 2097168 | tf_op jit(solution)/shard_map/all_gather | solution.py:76
  2737.6 42.7 %reduce-scatter.63.cloned.1.call-done = bf16[256,1024]{1,0:T(8,128)(2,1)} async-done(((bf16[1024,1024]{1,0:T(8,128)(2,1)}), bf16[256,1024]{1,0:T(8,128)(2,1)}) %reduce-scatter.63.cloned.1.call-update) | async-done | bytes 524304 | tf_op jit(solution)/shard_map/reduce_scatter | solution.py:80
  2786.3 44.3 %all-gather.99.cloned.1.call-done = bf16[1024,1024]{1,0:T(8,128)(2,1)} async-done(((bf16[256,1024]{1,0:T(8,128)(2,1)}), bf16[1024,1024]{1,0:T(8,128)(2,1)}) %all-gather.99.cloned.1.call-update) | async-done | bytes 2097168 | tf_op jit(solution)/shard_map/all_gather | solution.py:76
  2837.8 199.6 %while.107 = (s32[]{:T(128)}, f32[1024,4,64]{0,2,1:T(8,128)}, bf16[4,1024,4,64]{1,3,2,0:T(8,128)(2,1)}, bf16[4,1024,4,64]{1,3,2,0:T(8,128)(2,1)}, bf16[4,1024,4,...) while((s32[]{:T(128)}, f32[1024,4,64]{0,2,1:T(8,128)}, ...), condition=%wide.region_91.92_spmd.clone, body=%wide.region_89.91_spmd.clone.sunk | while | flops 3301192704 | bytes 232899024 | solution.py:253
  3159.5 23.6 reduce-scatter.79.cloned.1.call-done
  3184.9 28.2 reduce-scatter.81.cloned.1.call-done
  3215.1 28.0 reduce-scatter.83.cloned.1.call-done
  3245.0 22.4 reduce-scatter.77.cloned.1.call-done
  3269.1 22.4 reduce-scatter.71.cloned.1.call-done
  3293.1 22.6 reduce-scatter.73.cloned.1.call-done
  3317.3 22.6 reduce-scatter.75.cloned.1.call-done
  3341.5 44.7 %reduce-scatter.69.cloned.1.call-done = bf16[256,1024]{1,0:T(8,128)(2,1)} async-done(((bf16[1024,1024]{1,0:T(8,128)(2,1)}), bf16[256,1024]{1,0:T(8,128)(2,1)}) %reduce-scatter.69.cloned.1.call-update) | async-done | bytes 524304 | tf_op jit(solution)/shard_map/reduce_scatter | solution.py:80
  3387.7 32.6 all-reduce.2
  (1389 shorter events, 1590.6 us)
Async XLA Ops:
  7.2 52.2 %all-gather.41.cloned.1.call-start = ((), (), s32[]{:S(2)}) async-start(), calls=%async_computation.28 | async-start | bytes 2621440 | tf_op jit(solution)/shard_map/all_gather | solution.py:76
  10.6 75.8 %all-gather.43.cloned.1.call-start = ((), (), s32[]{:S(2)}) async-start(), calls=%async_computation.29 | async-start | bytes 2621440 | tf_op jit(solution)/shard_map/all_gather | solution.py:104
  63.9 73.1 %all-gather.45.cloned.1.call-start = ((), (), s32[]{:S(2)}) async-start(), calls=%async_computation.30 | async-start | bytes 2621440 | tf_op jit(solution)/shard_map/all_gather | solution.py:105
  85.7 127.3 %reduce-scatter.29.cloned.1.call-start = ((), (), s32[]{:S(2)}) async-start(), calls=%async_computation.31 | async-start | bytes 2621440 | tf_op jit(solution)/shard_map/reduce_scatter | solution.py:80
  170.0 63.0 %all-gather.101.cloned.1.call-start = ((), (), s32[]{:S(2)}) async-start(), calls=%async_computation.86 | async-start | bytes 1802240 | tf_op jit(solution)/shard_map/all_gather | solution.py:330
  170.6 110.4 %all-gather.47.cloned.1.call-start = ((), (), s32[]{:S(2)}) async-start(), calls=%async_computation.32 | async-start | bytes 2621440 | tf_op jit(solution)/shard_map/all_gather | solution.py:76
  216.5 84.0 %all-gather.105.cloned.1.call-start = ((), (), s32[]{:S(2)}) async-start(), calls=%async_computation.88 | async-start | bytes 1802240 | tf_op jit(solution)/shard_map/all_gather | solution.py:332
  217.2 104.0 %all-gather.103.cloned.1.call-start = ((), (), s32[]{:S(2)}) async-start(), calls=%async_computation.87 | async-start | bytes 1802240 | tf_op jit(solution)/shard_map/all_gather | solution.py:331
  218.0 155.4 %reduce-scatter.31.cloned.1.call-start = ((), (), s32[]{:S(2)}) async-start(), calls=%async_computation.33 | async-start | bytes 2621440 | tf_op jit(solution)/shard_map/reduce_scatter | solution.py:80
  329.3 126.5 %all-gather.49.cloned.1.call-start = ((), (), s32[]{:S(2)}) async-start(), calls=%async_computation.34 | async-start | bytes 2621440 | tf_op jit(solution)/shard_map/all_gather | solution.py:76
  377.0 25.9 collective-permute-start
  409.0 74.3 %all-gather.51.cloned.1.call-start = ((), (), s32[]{:S(2)}) async-start(), calls=%async_computation.35 | async-start | bytes 2621440 | tf_op jit(solution)/shard_map/all_gather | solution.py:104
  461.9 73.3 %all-gather.53.cloned.1.call-start = ((), (), s32[]{:S(2)}) async-start(), calls=%async_computation.36 | async-start | bytes 2621440 | tf_op jit(solution)/shard_map/all_gather | solution.py:105
  467.9 146.2 %reduce-scatter.33.cloned.1.call-start = ((), (), s32[]{:S(2)}) async-start(), calls=%async_computation.37 | async-start | bytes 2621440 | tf_op jit(solution)/shard_map/reduce_scatter | solution.py:80
  569.9 93.0 %all-gather.55.cloned.1.call-start = ((), (), s32[]{:S(2)}) async-start(), calls=%async_computation.38 | async-start | bytes 2621440 | tf_op jit(solution)/shard_map/all_gather | solution.py:76
  617.5 101.5 %reduce-scatter.35.cloned.1.call-start = ((), (), s32[]{:S(2)}) async-start(), calls=%async_computation.39 | async-start | bytes 2621440 | tf_op jit(solution)/shard_map/reduce_scatter | solution.py:80
  676.2 126.0 %all-gather.65.cloned.1.call-start = ((), (), s32[]{:S(2)}) async-start(), calls=%async_computation.46 | async-start | bytes 2621440 | tf_op jit(solution)/shard_map/all_gather | solution.py:76
  754.5 93.8 %all-gather.57.cloned.1.call-start = ((), (), s32[]{:S(2)}) async-start(), calls=%async_computation.40 | async-start | bytes 2621440 | tf_op jit(solution)/shard_map/all_gather | solution.py:76
  755.1 115.9 %all-gather.67.cloned.1.call-start = ((), (), s32[]{:S(2)}) async-start(), calls=%async_computation.47 | async-start | bytes 2621440 | tf_op jit(solution)/shard_map/all_gather | solution.py:154
  807.4 88.4 %all-gather.69.cloned.1.call-start = ((), (), s32[]{:S(2)}) async-start(), calls=%async_computation.48 | async-start | bytes 2621440 | tf_op jit(solution)/shard_map/all_gather | solution.py:155
  814.7 206.1 %all-gather.59.cloned.1.call-start = ((), (), s32[]{:S(2)}) async-start(), calls=%async_computation.41 | async-start | bytes 2621440 | tf_op jit(solution)/shard_map/all_gather | solution.py:104
  853.6 222.8 %all-gather.61.cloned.1.call-start = ((), (), s32[]{:S(2)}) async-start(), calls=%async_computation.42 | async-start | bytes 2621440 | tf_op jit(solution)/shard_map/all_gather | solution.py:105
  859.0 250.7 %reduce-scatter.41.cloned.1.call-start = ((), (), s32[]{:S(2)}) async-start(), calls=%async_computation.49 | async-start | bytes 2621440 | tf_op jit(solution)/shard_map/reduce_scatter | solution.py:80
  1052.7 101.0 %reduce-scatter.37.cloned.1.call-start = ((), (), s32[]{:S(2)}) async-start(), calls=%async_computation.43 | async-start | bytes 2621440 | tf_op jit(solution)/shard_map/reduce_scatter | solution.py:80
  1109.6 93.6 %all-gather.77.cloned.1.call-start = ((), (), s32[]{:S(2)}) async-start(), calls=%async_computation.57 | async-start | bytes 2621440 | tf_op jit(solution)/shard_map/all_gather | solution.py:76
  1157.8 92.2 %all-gather.73.cloned.1.call-start = ((), (), s32[]{:S(2)}) async-start(), calls=%async_computation.51 | async-start | bytes 2621440 | tf_op jit(solution)/shard_map/all_gather | solution.py:76
  1158.5 137.6 %all-gather.71.cloned.1.call-start = ((), (), s32[]{:S(2)}) async-start(), calls=%async_computation.50 | async-start | bytes 2621440 | tf_op jit(solution)/shard_map/all_gather | solution.py:76
  1160.6 158.8 %all-gather.79.cloned.1.call-start = ((), (), s32[]{:S(2)}) async-start(), calls=%async_computation.58 | async-start | bytes 2621440 | tf_op jit(solution)/shard_map/all_gather | solution.py:154
  1208.4 135.2 %all-gather.81.cloned.1.call-start = ((), (), s32[]{:S(2)}) async-start(), calls=%async_computation.59 | async-start | bytes 2621440 | tf_op jit(solution)/shard_map/all_gather | solution.py:155
  1211.1 260.3 %reduce-scatter.43.cloned.1.call-start = ((), (), s32[]{:S(2)}) async-start(), calls=%async_computation.52 | async-start | bytes 2621440 | tf_op jit(solution)/shard_map/reduce_scatter | solution.py:80
  1308.1 207.3 %reduce-scatter.51.cloned.1.call-start = ((), (), s32[]{:S(2)}) async-start(), calls=%async_computation.60 | async-start | bytes 2621440 | tf_op jit(solution)/shard_map/reduce_scatter | solution.py:80
  1471.3 94.3 %all-gather.75.cloned.1.call-start = ((), (), s32[]{:S(2)}) async-start(), calls=%async_computation.53 | async-start | bytes 2621440 | tf_op jit(solution)/shard_map/all_gather | solution.py:76
  1520.2 287.7 %reduce-scatter.45.cloned.1.call-start = ((), (), s32[]{:S(2)}) async-start(), calls=%async_computation.54 | async-start | bytes 2621440 | tf_op jit(solution)/shard_map/reduce_scatter | solution.py:259
  1777.7 64.3 %reduce-scatter.47.cloned.1.call-start = ((), (), s32[]{:S(2)}) async-start(), calls=%async_computation.55 | async-start | bytes 2621440 | tf_op jit(solution)/shard_map/reduce_scatter | solution.py:265
  1789.4 102.3 %reduce-scatter.49.cloned.1.call-start = ((), (), s32[]{:S(2)}) async-start(), calls=%async_computation.56 | async-start | bytes 2621440 | tf_op jit(solution)/shard_map/reduce_scatter | solution.py:80
  1847.7 94.0 %all-gather.89.cloned.1.call-start = ((), (), s32[]{:S(2)}) async-start(), calls=%async_computation.68 | async-start | bytes 2621440 | tf_op jit(solution)/shard_map/all_gather | solution.py:76
  1896.3 92.2 %all-gather.85.cloned.1.call-start = ((), (), s32[]{:S(2)}) async-start(), calls=%async_computation.62 | async-start | bytes 2621440 | tf_op jit(solution)/shard_map/all_gather | solution.py:76
  1896.9 138.3 %all-gather.83.cloned.1.call-start = ((), (), s32[]{:S(2)}) async-start(), calls=%async_computation.61 | async-start | bytes 2621440 | tf_op jit(solution)/shard_map/all_gather | solution.py:76
  1899.7 26.8 collective-permute-start.2
  1931.1 127.7 %all-gather.91.cloned.1.call-start = ((), (), s32[]{:S(2)}) async-start(), calls=%async_computation.69 | async-start | bytes 2621440 | tf_op jit(solution)/shard_map/all_gather | solution.py:154
  1948.0 134.9 %all-gather.93.cloned.1.call-start = ((), (), s32[]{:S(2)}) async-start(), calls=%async_computation.70 | async-start | bytes 2621440 | tf_op jit(solution)/shard_map/all_gather | solution.py:155
  1950.9 259.9 %reduce-scatter.53.cloned.1.call-start = ((), (), s32[]{:S(2)}) async-start(), calls=%async_computation.63 | async-start | bytes 2621440 | tf_op jit(solution)/shard_map/reduce_scatter | solution.py:80
  2047.2 207.5 %reduce-scatter.61.cloned.1.call-start = ((), (), s32[]{:S(2)}) async-start(), calls=%async_computation.71 | async-start | bytes 2621440 | tf_op jit(solution)/shard_map/reduce_scatter | solution.py:80
  2210.8 94.3 %all-gather.87.cloned.1.call-start = ((), (), s32[]{:S(2)}) async-start(), calls=%async_computation.64 | async-start | bytes 2621440 | tf_op jit(solution)/shard_map/all_gather | solution.py:76
  2259.6 286.4 %reduce-scatter.55.cloned.1.call-start = ((), (), s32[]{:S(2)}) async-start(), calls=%async_computation.65 | async-start | bytes 2621440 | tf_op jit(solution)/shard_map/reduce_scatter | solution.py:259
  2515.7 64.3 %reduce-scatter.57.cloned.1.call-start = ((), (), s32[]{:S(2)}) async-start(), calls=%async_computation.66 | async-start | bytes 2621440 | tf_op jit(solution)/shard_map/reduce_scatter | solution.py:265
  2529.9 101.7 %reduce-scatter.59.cloned.1.call-start = ((), (), s32[]{:S(2)}) async-start(), calls=%async_computation.67 | async-start | bytes 2621440 | tf_op jit(solution)/shard_map/reduce_scatter | solution.py:80
  2587.6 91.3 %all-gather.97.cloned.1.call-start = ((), (), s32[]{:S(2)}) async-start(), calls=%async_computation.73 | async-start | bytes 2621440 | tf_op jit(solution)/shard_map/all_gather | solution.py:76
  2588.2 137.4 %all-gather.95.cloned.1.call-start = ((), (), s32[]{:S(2)}) async-start(), calls=%async_computation.72 | async-start | bytes 2621440 | tf_op jit(solution)/shard_map/all_gather | solution.py:76
  2636.3 26.9 collective-permute-start.3
  2669.9 110.3 %reduce-scatter.63.cloned.1.call-start = ((), (), s32[]{:S(2)}) async-start(), calls=%async_computation.74 | async-start | bytes 2621440 | tf_op jit(solution)/shard_map/reduce_scatter | solution.py:80
  2737.5 93.1 %all-gather.99.cloned.1.call-start = ((), (), s32[]{:S(2)}) async-start(), calls=%async_computation.75 | async-start | bytes 2621440 | tf_op jit(solution)/shard_map/all_gather | solution.py:76
  2785.5 269.4 %all-gather.63.cloned.1.call-start = ((), (), s32[]{:S(2)}) async-start(), calls=%async_computation.44 | async-start | bytes 2621440 | tf_op jit(solution)/shard_map/all_gather | solution.py:76
  2786.3 323.1 %reduce-scatter.65.cloned.1.call-start = ((), (), s32[]{:S(2)}) async-start(), calls=%async_computation.76 | async-start | bytes 2621440 | tf_op jit(solution)/shard_map/reduce_scatter | solution.py:259
  3042.9 85.3 %reduce-scatter.67.cloned.1.call-start = ((), (), s32[]{:S(2)}) async-start(), calls=%async_computation.77 | async-start | bytes 2621440 | tf_op jit(solution)/shard_map/reduce_scatter | solution.py:265
  3054.8 99.0 %reduce-scatter.39.cloned.1.call-start = ((), (), s32[]{:S(2)}) async-start(), calls=%async_computation.45 | async-start | bytes 2621440 | tf_op jit(solution)/shard_map/reduce_scatter | solution.py:80
  3067.7 115.3 %reduce-scatter.79.cloned.1.call-start = ((), (), s32[]{:S(2)}) async-start(), calls=%async_computation.83 | async-start | bytes 1802240 | tf_op jit(solution)/shard_map/reduce_scatter | solution.py:449
  3076.2 137.0 %reduce-scatter.81.cloned.1.call-start = ((), (), s32[]{:S(2)}) async-start(), calls=%async_computation.84 | async-start | bytes 1802240 | tf_op jit(solution)/shard_map/reduce_scatter | solution.py:452
  3083.1 160.0 %reduce-scatter.83.cloned.1.call-start = ((), (), s32[]{:S(2)}) async-start(), calls=%async_computation.85 | async-start | bytes 1802240 | tf_op jit(solution)/shard_map/reduce_scatter | solution.py:455
  3094.8 172.7 %reduce-scatter.77.cloned.1.call-start = ((), (), s32[]{:S(2)}) async-start(), calls=%async_computation.82 | async-start | bytes 655360 | tf_op jit(solution)/shard_map/reduce_scatter | solution.py:446
  3106.0 185.4 %reduce-scatter.71.cloned.1.call-start = ((), (), s32[]{:S(2)}) async-start(), calls=%async_computation.79 | async-start | bytes 655360 | tf_op jit(solution)/shard_map/reduce_scatter | solution.py:437
  3115.1 200.6 %reduce-scatter.73.cloned.1.call-start = ((), (), s32[]{:S(2)}) async-start(), calls=%async_computation.80 | async-start | bytes 655360 | tf_op jit(solution)/shard_map/reduce_scatter | solution.py:440
  3124.2 215.7 %reduce-scatter.75.cloned.1.call-start = ((), (), s32[]{:S(2)}) async-start(), calls=%async_computation.81 | async-start | bytes 655360 | tf_op jit(solution)/shard_map/reduce_scatter | solution.py:443
  3133.1 253.1 %reduce-scatter.69.cloned.1.call-start = ((), (), s32[]{:S(2)}) async-start(), calls=%async_computation.78 | async-start | bytes 2621440 | tf_op jit(solution)/shard_map/reduce_scatter | solution.py:80
  (347 other events, 7861.4 us)
Sparse Core Ops, SparseCore 0:
  10.7 48.6 all-gather.40
  64.0 21.2 all-gather.42
  87.5 22.5 all-gather.44
  170.1 42.8 reduce-scatter.28
  214.5 18.4 all-gather.100
  235.0 45.9 all-gather.46
  282.6 17.7 all-gather.104
  302.1 19.0 all-gather.102
  329.4 43.8 reduce-scatter.30
  409.1 46.6 all-gather.48
  462.0 21.2 all-gather.50
  485.4 22.5 all-gather.52
  570.0 44.0 reduce-scatter.32
  617.6 45.2 all-gather.54
  676.3 42.5 reduce-scatter.34
  754.6 47.5 all-gather.64
  803.6 44.6 all-gather.56
  849.7 21.2 all-gather.66
  873.2 22.5 all-gather.68
  897.2 22.5 all-gather.58
  922.0 22.5 all-gather.60
  1052.9 43.9 reduce-scatter.40
  1109.7 43.9 reduce-scatter.36
  1157.9 45.2 all-gather.76
  1205.3 44.6 all-gather.72
  1251.4 44.6 all-gather.70
  1298.1 21.2 all-gather.78
  1321.0 22.5 all-gather.80
  1345.9 43.8 reduce-scatter.42
  1471.4 43.9 reduce-scatter.50
  1520.3 45.2 all-gather.74
  1777.8 30.1 reduce-scatter.44
  1810.5 31.4 reduce-scatter.46
  1847.8 43.8 reduce-scatter.48
  1896.4 45.2 all-gather.88
  1943.8 44.6 all-gather.84
  1990.6 44.6 all-gather.82
  2037.5 21.2 all-gather.90
  2060.3 22.5 all-gather.92
  2085.9 43.8 reduce-scatter.52
  2210.8 43.8 reduce-scatter.60
  2259.7 45.2 all-gather.86
  2515.8 30.1 reduce-scatter.54
  2548.5 31.4 reduce-scatter.56
  2587.7 43.8 reduce-scatter.58
  2633.6 45.2 all-gather.96
  2680.9 44.6 all-gather.94
  2737.6 42.5 reduce-scatter.62
  2785.6 44.9 all-gather.98
  2832.2 44.6 all-gather.62
  3043.0 30.0 reduce-scatter.64
  3075.7 31.3 reduce-scatter.66
  3109.9 43.8 reduce-scatter.38
  3156.4 26.6 reduce-scatter.78
  3185.8 27.3 reduce-scatter.80
  3215.7 27.3 reduce-scatter.82
  3245.7 21.6 reduce-scatter.76
  3269.8 21.6 reduce-scatter.70
  3294.0 21.6 reduce-scatter.72
  3318.2 21.6 reduce-scatter.74
  3342.2 43.8 reduce-scatter.68
where the time goes:
time: 3440 us; the launch traced here: 3430 us
  waiting for transfers between devices  1610 us (47%)
  matrix products  1090 us (32%)
  other arithmetic  357 us (10%)
  local copies, waits for them, and re-layouts  258 us (8%)
  blocking collectives  63.1 us (2%)
    all_gather x18, waiting for transfers between devices, spread(): return lax.all_gather(values, 'tensor', axis=0, tiled=True)  623 us
    reduce_scatter x15, waiting for transfers between devices, fold_rows(): lax.psum_scatter(values.astype(jnp.bfloat16), 'tensor', scatter_dimension...  485 us
    dot_general x24, matrix products, block_scores(): jnp.einsum('qhd,khd->hqk', query_heads, block_keys, preferred_element_typ...  143 us
    dot_general x12, matrix products, second_pass(): jnp.einsum('hqd,khd->hqk', grad_heads, block_values, preferred_element_ty...  134 us
    dot_general x12, matrix products, second_pass(): jnp.einsum('hqk,hqd->khd', low_weights, scaled_rest, preferred_element_ty...  119 us
    dot_general x12, matrix products, second_pass(): jnp.einsum('hqk,hqd->khd', low_weights, scaled_high, preferred_element_ty...  118 us
    dot_general x36, matrix products, product(): return jnp.dot(left, right, preferred_element_type=jnp.float32)  115 us
    reduce_sum x12, other arithmetic, first_pass(): totals = totals * rescale + jnp.sum(weights, axis=2)  98.9 us
  transfers between devices with their start and end apart: 65, of which 54 were waited for; matrix products, arithmetic and copies ran while one was open for 31% of the time, Pallas kernels for 0%

commit v1 on v0

--- a/solution.py
+++ b/solution.py
@@ -1,8 +1,11 @@
+import functools
 import math
 
 import jax
 import jax.numpy as jnp
 from jax import lax
+from jax.experimental import pallas as pl
+from jax.experimental.pallas import tpu as pltpu
 from jax.sharding import PartitionSpec as P
 
 HS = 64
@@ -475,6 +478,946 @@
     )
 
 
+MESH_ID = pl.DeviceIdType.MESH
+LOW = jnp.bfloat16
+F32 = jnp.float32
+ORDERS = ((1, 2, 4), (2, 4, 1), (4, 1, 2))
+LEVELS = ((0,), (1, 2, 4), (3, 5, 6), (7,))
+NT = (((1,), (1,)), ((), ()))
+NN = (((1,), (0,)), ((), ()))
+TN = (((0,), (0,)), ((), ()))
+VMEM_BYTES = 60 * 2**20
+
+
+def dot(left, right, dims=NN):
+    return lax.dot_general(left, right, dims, preferred_element_type=F32)
+
+
+def flip(value, bit):
+    if isinstance(bit, int):
+        return 1 - value if bit else value
+    return value + bit - 2 * value * bit
+
+
+def spot():
+    y, s, z = lax.axis_index("section"), lax.axis_index("seq"), lax.axis_index("tensor")
+    return (y, lax.div(s, 2), lax.rem(s, 2), lax.div(z, 2), lax.rem(z, 2))
+
+
+def device(at):
+    y, x, c, h, p = at
+    return (y, 2 * x + c, 2 * h + p)
+
+
+def moved(at, mask, core=0):
+    y, x, c, h, p = at
+    if isinstance(mask, int):
+        bits = (mask & 1, (mask >> 1) & 1, mask >> 2)
+    else:
+        bits = (lax.rem(mask, 2), lax.rem(lax.div(mask, 2), 2), lax.div(mask, 4))
+    return (flip(y, bits[1]), flip(x, bits[0]), flip(c, core), h, flip(p, bits[2]))
+
+
+def far_role(at):
+    return flip(at[0], at[2])
+
+
+def lane_of(at):
+    return 2 * flip(at[3], far_role(at)) + at[4]
+
+
+def block_of(at):
+    return (2 * at[1] + at[2]) * 4 + lane_of(at)
+
+
+def level_mask(level, i):
+    if level == 0:
+        return 0 * i
+    if level == 1:
+        return 1 + i + lax.div(i, 2)
+    if level == 2:
+        return 3 + i + lax.div(i + 1, 2)
+    return 0 * i + 7
+
+
+def last_bit(k, mask):
+    return [bit for bit in ORDERS[k] if bit & mask][-1]
+
+
+def parts_of(rows):
+    units = rows // 16
+    small = units // 3
+    sizes = (16 * (units - 2 * small), 16 * small, 16 * small)
+    return ((0, sizes[0]), (sizes[0], sizes[1]), (sizes[0] + sizes[1], sizes[2]))
+
+
+def remote(src, dst, send, recv, at):
+    return pltpu.make_async_remote_copy(
+        src_ref=src, dst_ref=dst, send_sem=send, recv_sem=recv, device_id=device(at), device_id_type=MESH_ID
+    )
+
+
+def greet(at):
+    barrier = pltpu.get_barrier_semaphore()
+    for mask, core in ((1, 0), (2, 0), (4, 0), (0, 1)):
+        pl.semaphore_signal(barrier, inc=1, device_id=device(moved(at, mask, core)), device_id_type=MESH_ID)
+    pl.semaphore_wait(barrier, 4)
+
+
+def gather(at, buf, sems, on_block):
+    send, recv, csend, crecv = sems
+    parts = parts_of(buf.shape[1])
+
+    def rows(mask, k, core=0):
+        return buf.at[block_of(moved(at, mask, core)), pl.ds(*parts[k])]
+
+    def hop(k, target):
+        bit = last_bit(k, target)
+        ref = rows(target ^ bit, k)
+        return remote(ref, ref, send.at[k, target], recv.at[k, target], moved(at, bit))
+
+    def arrival(k, target):
+        ref = rows(target, k)
+        return remote(ref, ref, send.at[k, target], recv.at[k, target], moved(at, last_bit(k, target)))
+
+    def across(mask, core=0):
+        ref = buf.at[block_of(moved(at, mask, core))]
+        return remote(ref, ref, csend.at[mask], crecv.at[mask], moved(at, 0, 1))
+
+    def visit(level, core):
+        def one(i, none):
+            on_block(block_of(moved(at, level_mask(level, i), core)))
+            return none
+
+        lax.fori_loop(0, len(LEVELS[level]), one, 0)
+
+    for i in range(3):
+        for k in range(3):
+            hop(k, ORDERS[k][i]).start()
+    across(0).start()
+    visit(0, 0)
+    across(0, 1).wait_recv()
+    visit(0, 1)
+    for level in (1, 2, 3):
+        for mask in LEVELS[level]:
+            for k in range(3):
+                arrival(k, mask).wait_recv()
+                place = ORDERS[k].index(last_bit(k, mask))
+                for bit in ORDERS[k][place + 1 :]:
+                    hop(k, mask | bit).start()
+            across(mask).start()
+        visit(level, 0)
+        for mask in LEVELS[level]:
+            across(mask, 1).wait_recv()
+        visit(level, 1)
+    for k in range(3):
+        for target in range(1, 8):
+            hop(k, target).wait_send()
+    for mask in range(8):
+        across(mask).wait_send()
+
+
+def scatter(at, total, boxes, sems, partial, copy=None):
+    own, out_c, in_c, rin = boxes
+    send, recv, csend, crecv = sems
+    parts = parts_of(total.shape[0])
+
+    def hop(k, target):
+        rows = pl.ds(*parts[k])
+        return remote(
+            own.at[target - 1, rows],
+            rin.at[target - 1, rows],
+            send.at[k, target],
+            recv.at[k, target],
+            moved(at, last_bit(k, target)),
+        )
+
+    def across(mask):
+        return remote(out_c.at[mask], in_c.at[mask], csend.at[mask], crecv.at[mask], moved(at, 0, 1))
+
+    def emit(level):
+        def one(i, none):
+            mask = level_mask(level, i)
+            out_c[mask] = partial(block_of(moved(at, mask, 1))).astype(LOW)
+            return none
+
+        lax.fori_loop(0, len(LEVELS[level]), one, 0)
+        for mask in LEVELS[level]:
+            across(mask).start()
+
+    def keep(level):
+        for mask in LEVELS[level]:
+            across(mask).wait_recv()
+
+        def one(i, none):
+            mask = level_mask(level, i)
+            mine = partial(block_of(moved(at, mask))) + in_c[mask].astype(F32)
+            if level == 0:
+                total[...] = mine
+            else:
+                own[mask - 1] = mine.astype(LOW)
+            return none
+
+        lax.fori_loop(0, len(LEVELS[level]), one, 0)
+        for mask in LEVELS[level]:
+            for k in range(3):
+                if mask & ORDERS[k][2]:
+                    hop(k, mask).start()
+
+    def arrived(k, target):
+        hop(k, target).wait_recv()
+        return rin[target - 1, pl.ds(*parts[k])].astype(F32)
+
+    emit(3)
+    emit(2)
+    keep(3)
+    keep(2)
+    emit(1)
+    keep(1)
+    if copy is not None:
+        copy.wait()
+    emit(0)
+    keep(0)
+    for mask_of in (lambda a, b: a | b, lambda a, b: b):
+        for k in range(3):
+            first, second, third = ORDERS[k]
+            mask, rows = mask_of(first, second), pl.ds(*parts[k])
+            own[mask - 1, rows] = (own[mask - 1, rows].astype(F32) + arrived(k, mask | third)).astype(LOW)
+            hop(k, mask).start()
+    for k in range(3):
+        first, second, third = ORDERS[k]
+        rows = pl.ds(*parts[k])
+        own[first - 1, rows] = (
+            own[first - 1, rows].astype(F32) + arrived(k, first | third) + arrived(k, first | second)
+        ).astype(LOW)
+        hop(k, first).start()
+    for k in range(3):
+        first, second, third = ORDERS[k]
+        rows = pl.ds(*parts[k])
+        total[rows] = total[rows] + arrived(k, third) + arrived(k, second) + arrived(k, first)
+    for k in range(3):
+        for target in range(1, 8):
+            hop(k, target).wait_send()
+    for mask in range(8):
+        across(mask).wait_send()
+
+
+def unit_of(values):
+    inverse = lax.rsqrt(jnp.mean(values * values, axis=-1, keepdims=True) + EPSILON)
+    return (values * inverse, inverse)
+
+
+def back_of(grad_normed, values, gain_row):
+    unit, inverse = unit_of(values)
+    shaped = grad_normed * gain_row
+    inner = jnp.mean(shaped * unit, axis=-1, keepdims=True)
+    return (inverse * (shaped - unit * inner), jnp.sum(grad_normed * unit, axis=0, keepdims=True))
+
+
+def span(b, rows):
+    return pl.ds(pl.multiple_of(b * rows, rows), rows)
+
+
+def turned(top, bottom, cosine, sine):
+    return (top * cosine - bottom * sine, bottom * cosine + top * sine)
+
+
+def project_block(b, buf, w_ref, cos_ref, sin_ref, mix_ref, qkv_ref):
+    rows, half = buf.shape[1], HS // 2
+    cols = span(b, rows)
+    raw = dot(w_ref[...], buf[b], NT)
+    cosine, sine = cos_ref[:, cols], sin_ref[:, cols]
+    for first, scale in ((0, HS**-0.5), (HS, 1.0)):
+        a, bb = turned(raw[first : first + half], raw[first + half : first + HS], cosine, sine)
+        qkv_ref[first : first + half, cols] = (a.astype(LOW) * scale).astype(LOW)
+        qkv_ref[first + half : first + HS, cols] = (bb.astype(LOW) * scale).astype(LOW)
+    value = raw[2 * HS :]
+    if mix_ref is not None:
+        value = 0.5 * value + 0.5 * mix_ref[:, cols].astype(F32)
+    qkv_ref[2 * HS :, cols] = value.astype(LOW)
+
+
+def save(buf, out, sem):
+    return pltpu.make_async_copy(buf, out, sem)
+
+
+def first_kernel(x_ref, gain_ref, w_ref, cos_ref, sin_ref, qkv_ref, normed_ref, buf, ag_sems, sem):
+    at = spot()
+    greet(at)
+    buf[block_of(at)] = (unit_of(x_ref[...].astype(F32))[0] * gain_ref[...]).astype(LOW)
+    gather(at, buf, ag_sems, lambda b: project_block(b, buf, w_ref, cos_ref, sin_ref, None, qkv_ref))
+    copy = save(buf, normed_ref, sem)
+    copy.start()
+    copy.wait()
+
+
+def up_block(b, buf, f_ref, hidden_ref, one_ref, two_ref):
+    rows = span(b, buf.shape[1])
+    x = buf[b]
+    gate, up = dot(x, f_ref[0], NT), dot(x, f_ref[1], NT)
+    sigmoid = 1.0 / (1.0 + jnp.exp(-gate))
+    activated = gate * sigmoid
+    hidden_ref[rows] = (activated * up).astype(LOW)
+    one_ref[rows] = (up * sigmoid * (1.0 + gate * (1.0 - sigmoid))).astype(LOW)
+    two_ref[rows] = activated.astype(LOW)
+
+
+def middle_kernel(
+    att_ref, x_ref, wo_ref, f_ref, gain_mid_ref, gain_in_ref, w_ref, cos_ref, sin_ref, mix_ref,
+    middle_ref, out_ref, hidden_ref, one_ref, two_ref, qkv_ref, nmid_ref, normed_ref,
+    buf, total, own, out_c, in_c, rin, ag_sems, rs_sems, sem,
+):
+    at = spot()
+    rows = x_ref.shape[0]
+    greet(at)
+    boxes = (own, out_c, in_c, rin)
+    scatter(at, total, boxes, rs_sems, lambda b: dot(att_ref[span(b, rows)], wo_ref[...]))
+    middle = x_ref[...].astype(F32) + total[...]
+    middle_ref[...] = middle
+    buf[block_of(at)] = (unit_of(middle)[0] * gain_mid_ref[...]).astype(LOW)
+    gather(at, buf, ag_sems, lambda b: up_block(b, buf, f_ref, hidden_ref, one_ref, two_ref))
+    copy = save(buf, nmid_ref, sem)
+    copy.start()
+    scatter(at, total, boxes, rs_sems, lambda b: dot(hidden_ref[span(b, rows)], f_ref[2]), copy)
+    out = (middle_ref[...] + total[...]).astype(LOW)
+    out_ref[...] = out
+    buf[block_of(at)] = (unit_of(out.astype(F32))[0] * gain_in_ref[...]).astype(LOW)
+    gather(at, buf, ag_sems, lambda b: project_block(b, buf, w_ref, cos_ref, sin_ref, mix_ref, qkv_ref))
+    copy = save(buf, normed_ref, sem)
+    copy.start()
+    copy.wait()
+
+
+def down_back(
+    at, top, buf, total, boxes, ag_sems, rs_sems, sem, f_ref, one_ref, two_ref, wo_ref, gain_ref, middle_ref,
+    dgate_ref, dup_ref, dmid_ref, gain_grad_ref, dout_ref, top_all_ref, dmid_all_ref,
+):
+    rows = buf.shape[1]
+    buf[block_of(at)] = top.astype(LOW)
+
+    def hidden_back(b):
+        here = span(b, rows)
+        grad = dot(buf[b], f_ref[2], NT)
+        dgate_ref[here] = (grad * one_ref[here].astype(F32)).astype(LOW)
+        dup_ref[here] = (grad * two_ref[here].astype(F32)).astype(LOW)
+
+    gather(at, buf, ag_sems, hidden_back)
+    copy = save(buf, top_all_ref, sem)
+    copy.start()
+
+    def partial(b):
+        here = span(b, rows)
+        return dot(dgate_ref[here], f_ref[0]) + dot(dup_ref[here], f_ref[1])
+
+    scatter(at, total, boxes, rs_sems, partial, copy)
+    grad, gain_grad = back_of(total[...], middle_ref[...], gain_ref[...])
+    gain_grad_ref[...] = gain_grad
+    grad = grad + top
+    dmid_ref[...] = grad
+    buf[block_of(at)] = grad.astype(LOW)
+
+    def out_back(b):
+        dout_ref[:, span(b, rows)] = dot(wo_ref[...], buf[b], NT).astype(LOW)
+
+    gather(at, buf, ag_sems, out_back)
+    copy = save(buf, dmid_all_ref, sem)
+    copy.start()
+    copy.wait()
+
+
+def turn_kernel(
+    att_ref, x_ref, wo_ref, f_ref, gain_ref, top_ref,
+    out_ref, hidden_ref, dgate_ref, dup_ref, dmid_ref, gain_grad_ref, dout_ref, nmid_ref, top_all_ref, dmid_all_ref,
+    buf, total, own, out_c, in_c, rin, middle_ref, one_ref, two_ref, ag_sems, rs_sems, sem,
+):
+    at = spot()
+    rows = x_ref.shape[0]
+    greet(at)
+    boxes = (own, out_c, in_c, rin)
+    scatter(at, total, boxes, rs_sems, lambda b: dot(att_ref[span(b, rows)], wo_ref[...]))
+    middle = x_ref[...].astype(F32) + total[...]
+    middle_ref[...] = middle
+    buf[block_of(at)] = (unit_of(middle)[0] * gain_ref[...]).astype(LOW)
+    gather(at, buf, ag_sems, lambda b: up_block(b, buf, f_ref, hidden_ref, one_ref, two_ref))
+    copy = save(buf, nmid_ref, sem)
+    copy.start()
+    scatter(at, total, boxes, rs_sems, lambda b: dot(hidden_ref[span(b, rows)], f_ref[2]), copy)
+    out_ref[...] = (middle_ref[...] + total[...]).astype(LOW)
+    down_back(
+        at, top_ref[...].astype(F32), buf, total, boxes, ag_sems, rs_sems, sem, f_ref, one_ref, two_ref, wo_ref,
+        gain_ref, middle_ref, dgate_ref, dup_ref, dmid_ref, gain_grad_ref, dout_ref, top_all_ref, dmid_all_ref,
+    )
+
+
+def input_back(at, dqkv_ref, w_ref, x_ref, gain_ref, dmid_ref, gain_grad_ref, total, boxes, rs_sems):
+    rows = total.shape[0]
+    scatter(at, total, boxes, rs_sems, lambda b: dot(dqkv_ref[:, span(b, rows)], w_ref[...], TN))
+    grad, gain_grad = back_of(total[...], x_ref[...].astype(F32), gain_ref[...])
+    gain_grad_ref[...] = gain_grad
+    return grad + dmid_ref[...]
+
+
+def lower_kernel(
+    dqkv_ref, x_ref, w_ref, gain_in_ref, dmid_above_ref, f_ref, one_ref, two_ref, wo_ref, gain_mid_ref, middle_ref,
+    grad_ref, gain_in_grad_ref, dgate_ref, dup_ref, dmid_ref, gain_mid_grad_ref, dout_ref, top_all_ref, dmid_all_ref,
+    buf, total, own, out_c, in_c, rin, ag_sems, rs_sems, sem,
+):
+    at = spot()
+    greet(at)
+    boxes = (own, out_c, in_c, rin)
+    grad = input_back(at, dqkv_ref, w_ref, x_ref, gain_in_ref, dmid_above_ref, gain_in_grad_ref, total, boxes, rs_sems)
+    grad_ref[...] = grad
+    down_back(
+        at, grad_ref[...], buf, total, boxes, ag_sems, rs_sems, sem, f_ref, one_ref, two_ref, wo_ref, gain_mid_ref,
+        middle_ref, dgate_ref, dup_ref, dmid_ref, gain_mid_grad_ref, dout_ref, top_all_ref, dmid_all_ref,
+    )
+
+
+def last_kernel(
+    dqkv_ref, x_ref, w_ref, gain_ref, dmid_ref, grad_ref, gain_grad_ref, total, own, out_c, in_c, rin, rs_sems
+):
+    at = spot()
+    greet(at)
+    boxes = (own, out_c, in_c, rin)
+    grad_ref[...] = input_back(at, dqkv_ref, w_ref, x_ref, gain_ref, dmid_ref, gain_grad_ref, total, boxes, rs_sems)
+
+
+VMEM_SPEC = pl.BlockSpec(memory_space=pltpu.VMEM)
+ANY_SPEC = pl.BlockSpec(memory_space=pl.ANY)
+
+
+def links():
+    dma = pltpu.SemaphoreType.DMA
+    return (dma((3, 8)), dma((3, 8)), dma((8,)), dma((8,)))
+
+
+def sum_boxes(rows, width):
+    return [
+        pltpu.VMEM((rows, width), F32),
+        pltpu.VMEM((7, rows, width), LOW),
+        pltpu.VMEM((8, rows, width), LOW),
+        pltpu.VMEM((8, rows, width), LOW),
+        pltpu.VMEM((7, rows, width), LOW),
+    ]
+
+
+def reach(kernel, number, args, outs, scratch, name):
+    return pl.pallas_call(
+        kernel,
+        out_shape=[jax.ShapeDtypeStruct(shape, dtype) for shape, dtype, _ in outs],
+        in_specs=[VMEM_SPEC] * len(args),
+        out_specs=[ANY_SPEC if far else VMEM_SPEC for _, _, far in outs],
+        scratch_shapes=scratch,
+        compiler_params=pltpu.CompilerParams(
+            collective_id=number, has_side_effects=True, vmem_limit_bytes=VMEM_BYTES
+        ),
+        name=name,
+    )(*args)
+
+
+def head_homes(at, j):
+    y, x, c, h, p = at
+    return ((j % 2, j // 2, j % 2, h, p), (1 - j % 2, j // 2, j % 2, 1 - h, p))
+
+
+def shard_homes(at):
+    y, x, c, h, p = at
+    half = flip(h, far_role(at))
+    return [(layer, (layer, i // 2, i % 2, half, p)) for layer in range(2) for i in range(4)]
+
+
+def weights_kernel(a_ref, f_ref, a_all, f_all, send, recv, local):
+    at = spot()
+    y, x, c, h, p = at
+    s = 2 * x + c
+    near = 1 - far_role(at)
+    barrier = pltpu.get_barrier_semaphore()
+    mine = []
+    for layer, home in shard_homes(at):
+        is_me = near * (1 - flip(y, layer)) * (1 - jnp.minimum(jnp.abs(s - (2 * home[1] + home[2])), 1))
+        mine.append(is_me)
+
+        @pl.when(is_me == 0)
+        def _():
+            pl.semaphore_signal(barrier, inc=1, device_id=device(home), device_id_type=MESH_ID)
+
+    pl.semaphore_wait(barrier, 8 - near)
+    wide = a_ref.shape[-1]
+    cols = pl.ds(pl.multiple_of(s * wide, wide), wide)
+
+    def pair(j):
+        heads, units = pl.ds(j * HS, HS), pl.ds(j * (f_ref.shape[1] // 4), f_ref.shape[1] // 4)
+        return ((a_ref.at[:, heads], a_all.at[y, :, :, cols]), (f_ref.at[:, units], f_all.at[y, :, :, cols]))
+
+    for other in (1, 0):
+        for j in range(4):
+            home = head_homes(at, j)[other]
+            for i, (src, dst) in enumerate(pair(j)):
+                index = 4 * other + j
+                copy = remote(src, dst, send.at[i, index], recv.at[i, y, s], home)
+                if other:
+                    copy.start()
+                else:
+                    is_me = near * (1 - jnp.minimum(jnp.abs(s - j), 1))
+
+                    @pl.when(is_me == 0)
+                    def _():
+                        copy.start()
+
+                    @pl.when(is_me == 1)
+                    def _():
+                        pltpu.make_async_copy(src, dst, local.at[i]).start()
+
+    for layer in range(2):
+        for k in range(4):
+            is_me = mine[4 * layer + k]
+            place = pl.ds(k * wide, wide)
+            for i, all_ref in enumerate((a_all, f_all)):
+                dst = all_ref.at[layer, :, :, place]
+
+                @pl.when(is_me == 0)
+                def _():
+                    remote(dst, dst, send.at[i, 0], recv.at[i, layer, k], at).wait_recv()
+
+                @pl.when(is_me == 1)
+                def _():
+                    pltpu.make_async_copy(dst, dst, local.at[i]).wait()
+
+    for other in (1, 0):
+        for j in range(4):
+            for i, (src, dst) in enumerate(pair(j)):
+                copy = remote(src, dst, send.at[i, 4 * other + j], recv.at[i, y, s], at)
+                if other:
+                    copy.wait_send()
+                else:
+                    is_me = near * (1 - jnp.minimum(jnp.abs(s - j), 1))
+
+                    @pl.when(is_me == 0)
+                    def _():
+                        copy.wait_send()
+
+
+def grads_kernel(a_ref, f_ref, a_in, f_in, send, recv, local):
+    at = spot()
+    y, x, c, h, p = at
+    s = 2 * x + c
+    near = 1 - far_role(at)
+    wide = a_in.shape[-1]
+    barrier = pltpu.get_barrier_semaphore()
+    for other in (0, 1):
+        for j in range(4):
+            home = head_homes(at, j)[other]
+            if other:
+                pl.semaphore_signal(barrier, inc=1, device_id=device(home), device_id_type=MESH_ID)
+            else:
+
+                @pl.when(near * (1 - jnp.minimum(jnp.abs(s - j), 1)) == 0)
+                def _():
+                    pl.semaphore_signal(barrier, inc=1, device_id=device(home), device_id_type=MESH_ID)
+
+    pl.semaphore_wait(barrier, 8 - near)
+    role = far_role(at)
+    for n, (layer, home) in enumerate(shard_homes(at)):
+        k = 2 * home[1] + home[2]
+        is_me = near * (1 - flip(y, layer)) * (1 - jnp.minimum(jnp.abs(s - k), 1))
+        for i, (ref, into) in enumerate(((a_ref, a_in), (f_ref, f_in))):
+            src, dst = ref.at[layer, :, :, pl.ds(k * wide, wide)], into.at[role, s]
+            copy = remote(src, dst, send.at[i, n], recv.at[i, role, s], home)
+
+            @pl.when(is_me == 0)
+            def _():
+                copy.start()
+
+            @pl.when(is_me == 1)
+            def _():
+                pltpu.make_async_copy(src, dst, local.at[i]).start()
+
+    for other in (0, 1):
+        for j in range(4):
+            for i, into in enumerate((a_in, f_in)):
+                dst = into.at[other, j]
+                arrival = remote(dst, dst, send.at[i, 0], recv.at[i, other, j], at)
+                if other:
+                    arrival.wait_recv()
+                else:
+                    is_me = near * (1 - jnp.minimum(jnp.abs(s - j), 1))
+
+                    @pl.when(is_me == 0)
+                    def _():
+                        arrival.wait_recv()
+
+                    @pl.when(is_me == 1)
+                    def _():
+                        pltpu.make_async_copy(dst, dst, local.at[i]).wait()
+
+    for n, (layer, home) in enumerate(shard_homes(at)):
+        k = 2 * home[1] + home[2]
+        is_me = near * (1 - flip(y, layer)) * (1 - jnp.minimum(jnp.abs(s - k), 1))
+        for i, (ref, into) in enumerate(((a_ref, a_in), (f_ref, f_in))):
+
+            @pl.when(is_me == 0)
+            def _():
+                src, dst = ref.at[layer, :, :, pl.ds(k * wide, wide)], into.at[0, 0]
+                remote(src, dst, send.at[i, n], recv.at[i, 0, 0], at).wait_send()
+
+
+def attend_kernel(bounds, qkv_ref, start_ref, att_ref, flat_ref, lse_ref, key_n, val_t, *, bq, bk):
+    qi = pl.program_id(0)
+    length = qkv_ref.shape[1]
+
+    @pl.when(qi == 0)
+    def _():
+        for i in range(length // bk):
+            key_n[i * bk : (i + 1) * bk] = qkv_ref[HS : 2 * HS, i * bk : (i + 1) * bk].astype(F32).T.astype(LOW)
+        val_t[:HS] = qkv_ref[2 * HS :]
+        tail = lax.broadcasted_iota(jnp.int32, (16, length), 0)
+        val_t[HS:] = jnp.where(tail == 0, 1.0, 0.0).astype(LOW)
+
+    cols = span(qi, bq)
+    query = qkv_ref[:HS, cols]
+    start_row = start_ref[:, cols]
+    place = qi * bq + lax.broadcasted_iota(jnp.int32, (1, bq), 1)
+
+    def step(masked, kb, state):
+        largest, summed = state
+        scores = dot(key_n[span(kb, bk)], query)
+        if masked:
+            keys = kb * bk + lax.broadcasted_iota(jnp.int32, (bk, 1), 0)
+            allowed = (keys <= place) & (keys >= start_row)
+            scores = jnp.where(allowed, scores, NEGATIVE)
+        newest = jnp.maximum(largest, jnp.max(scores, axis=0, keepdims=True))
+        weights = jnp.exp(scores - newest)
+        if masked:
+            weights = jnp.where(allowed, weights, 0.0)
+        summed = summed * jnp.exp(largest - newest) + dot(val_t[:, span(kb, bk)], weights.astype(LOW))
+        return (newest, summed)
+
+    state = (jnp.full((1, bq), NEGATIVE, F32), jnp.zeros((HS + 16, bq), F32))
+    lo, mid, far, hi = (bounds[i, qi] for i in range(4))
+    state = lax.fori_loop(lo, mid, functools.partial(step, True), state)
+    state = lax.fori_loop(mid, far, functools.partial(step, False), state)
+    largest, summed = lax.fori_loop(far, hi, functools.partial(step, True), state)
+    totals = summed[HS : HS + 1]
+    attended = summed[:HS] / totals
+    att_ref[:, cols] = attended
+    flat_ref[span(qi, bq)] = attended.T.astype(LOW)
+    lse_ref[:, cols] = largest + jnp.log(totals)
+
+
+def attend(qkv, start_row, bq, bk):
+    length = qkv.shape[1]
+    blocks = length // bq
+    first = jnp.arange(blocks, dtype=jnp.int32) * bq
+    final = first + bq - 1
+    hi = final // bk + 1
+    lo = start_row[0][first] // bk
+    mid = jnp.clip(-(-start_row[0][final] // bk), lo, hi)
+    far = jnp.maximum((first + 1) // bk, mid)
+    whole = lambda shape: pl.BlockSpec(shape, lambda i, b: (0, 0))
+    return pl.pallas_call(
+        functools.partial(attend_kernel, bq=bq, bk=bk),
+        out_shape=[
+            jax.ShapeDtypeStruct((HS, length), F32),
+            jax.ShapeDtypeStruct((length, HS), LOW),
+            jax.ShapeDtypeStruct((1, length), F32),
+        ],
+        grid_spec=pltpu.PrefetchScalarGridSpec(
+            num_scalar_prefetch=1,
+            grid=(blocks,),
+            in_specs=[whole(qkv.shape), whole(start_row.shape)],
+            out_specs=[whole((HS, length)), whole((length, HS)), whole((1, length))],
+            scratch_shapes=[pltpu.VMEM((length, HS), LOW), pltpu.VMEM((HS + 16, length), LOW)],
+        ),
+        compiler_params=pltpu.CompilerParams(vmem_limit_bytes=VMEM_BYTES),
+        name="attend",
+    )(jnp.stack([lo, mid, far, hi]), qkv, start_row)
+
+
+def attend_back_kernel(
+    bounds, qkv_ref, start_ref, att_ref, lse_ref, dout_ref, cos_ref, sin_ref, *rest, bq, bk, first
+):
+    if first:
+        extra_ref, dqkv_ref, key_n, val_n, query_n, dout_n, delta, dq = rest
+    else:
+        dqkv_ref, send_ref, key_n, val_n, query_n, dout_n, delta, dq = rest
+    ki = pl.program_id(0)
+    length = qkv_ref.shape[1]
+    half = HS // 2
+
+    @pl.when(ki == 0)
+    def _():
+        for i in range(length // bk):
+            part = slice(i * bk, (i + 1) * bk)
+            query_n[part] = qkv_ref[:HS, part].astype(F32).T.astype(LOW)
+            key_n[part] = qkv_ref[HS : 2 * HS, part].astype(F32).T.astype(LOW)
+            val_n[part] = qkv_ref[2 * HS :, part].astype(F32).T.astype(LOW)
+            dout_n[part] = dout_ref[:, part].astype(F32).T.astype(LOW)
+        delta[...] = jnp.sum(dout_ref[...].astype(F32) * att_ref[...], axis=0, keepdims=True)
+        dq[...] = jnp.zeros_like(dq)
+
+    rows = span(ki, bk)
+    key, value, key_t = key_n[rows], val_n[rows], qkv_ref[HS : 2 * HS, rows]
+    keys = ki * bk + lax.broadcasted_iota(jnp.int32, (bk, 1), 0)
+
+    def step(masked, qb, state):
+        dk, dv = state
+        cols = span(qb, bq)
+        scores = dot(key, qkv_ref[:HS, cols])
+        weights = jnp.exp(scores - lse_ref[:, cols])
+        if masked:
+            place = qb * bq + lax.broadcasted_iota(jnp.int32, (1, bq), 1)
+            allowed = (keys <= place) & (keys >= start_ref[:, cols])
+            weights = jnp.where(allowed, weights, 0.0)
+        along = dot(value, dout_ref[:, cols])
+        ds = (weights * (along - delta[:, cols])).astype(LOW)
+        dv = dv + dot(weights.astype(LOW), dout_n[cols])
+        dk = dk + dot(ds, query_n[cols])
+        dq[:, cols] += dot(key_t, ds)
+        return (dk, dv)
+
+    state = (jnp.zeros((bk, HS), F32), jnp.zeros((bk, HS), F32))
+    lo, mid, far, hi = (bounds[i, ki] for i in range(4))
+    state = lax.fori_loop(lo, mid, functools.partial(step, True), state)
+    state = lax.fori_loop(mid, far, functools.partial(step, False), state)
+    dk, dv = lax.fori_loop(far, hi, functools.partial(step, True), state)
+    dk, dv = dk.T, dv.T
+    a, b = turned(dk[:half], dk[half:], cos_ref[:, rows], -sin_ref[:, rows])
+    dqkv_ref[HS : HS + half, rows] = a.astype(LOW)
+    dqkv_ref[HS + half : 2 * HS, rows] = b.astype(LOW)
+    if first:
+        dqkv_ref[2 * HS :, rows] = (dv + extra_ref[:, rows]).astype(LOW)
+    else:
+        dqkv_ref[2 * HS :, rows] = (0.5 * dv).astype(LOW)
+        send_ref[:, rows] = 0.5 * dv
+
+    @pl.when(ki == pl.num_programs(0) - 1)
+    def _():
+        scale = HS**-0.5
+        a, b = turned(dq[:half] * scale, dq[half:] * scale, cos_ref[...], -sin_ref[...])
+        dqkv_ref[:half] = a.astype(LOW)
+        dqkv_ref[half:HS] = b.astype(LOW)
+
+
+def attend_back(qkv, start_row, end_row, attended, lse, dout, tables, extra, bq, bk):
+    length = qkv.shape[1]
+    blocks = length // bk
+    first = jnp.arange(blocks, dtype=jnp.int32) * bk
+    final = first + bk - 1
+    lo = first // bq
+    hi = -(-end_row[0][final] // bq)
+    mid = jnp.minimum(-(-final // bq), hi)
+    far = jnp.maximum(jnp.minimum(end_row[0][first] // bq, hi), mid)
+    whole = lambda shape: pl.BlockSpec(shape, lambda i, b: (0, 0))
+    args = [qkv, start_row, attended, lse, dout, *tables]
+    outs = [jax.ShapeDtypeStruct(qkv.shape, LOW)]
+    if extra is None:
+        outs.append(jax.ShapeDtypeStruct((HS, length), F32))
+    else:
+        args.append(extra)
+    return pl.pallas_call(
+        functools.partial(attend_back_kernel, bq=bq, bk=bk, first=extra is not None),
+        out_shape=outs,
+        grid_spec=pltpu.PrefetchScalarGridSpec(
+            num_scalar_prefetch=1,
+            grid=(blocks,),
+            in_specs=[whole(arg.shape) for arg in args],
+            out_specs=[whole(out.shape) for out in outs],
+            scratch_shapes=[pltpu.VMEM((length, HS), LOW)] * 4
+            + [pltpu.VMEM((1, length), F32), pltpu.VMEM((HS, length), F32)],
+        ),
+        compiler_params=pltpu.CompilerParams(vmem_limit_bytes=VMEM_BYTES),
+        name="attend_back",
+    )(jnp.stack([lo, mid, far, hi]), *args)
+
+
+def number_of(y, s, z):
+    return (y * 4 + s) * 4 + z
+
+
+def far_pairs():
+    return [
+        (number_of(y, s, z), number_of(y, s, (z + 2) % 4))
+        for y in range(2)
+        for s in range(4)
+        for z in range(4)
+        if (y + s) % 2
+    ]
+
+
+def home_pairs(layer, micro):
+    pairs = []
+    for y in range(2):
+        for s in range(4):
+            for z in (2 * micro, 2 * micro + 1):
+                lane = (z + 2) % 4 if (y + s) % 2 else z
+                pairs.append((number_of(y, s, z), number_of(layer, s, lane)))
+    return pairs
+
+
+AXES = ("section", "seq", "tensor")
+
+
+def to_home(values, layer):
+    return [lax.ppermute(values, AXES, home_pairs(layer, micro)) for micro in range(2)]
+
+
+def on_grid(
+    inputs, cotangent, lengths, w_query, w_key, w_value, w_out, w_gate, w_up, w_down, attn_gain, mlp_gain
+):
+    at = spot()
+    y, x, c, half, p = at
+    far = far_role(at) == 1
+    rows, width = inputs.shape[1:]
+    length = 16 * rows
+    units = w_gate.shape[2] // 4
+    both = jnp.stack([lax.dynamic_index_in_dim(array, 1 - half, 0, keepdims=False) for array in (inputs, cotangent)])
+    swapped = lax.ppermute(both, AXES, far_pairs())
+    own_in = jnp.where(far, swapped[0], lax.dynamic_index_in_dim(inputs, half, 0, keepdims=False))
+    own_top = jnp.where(far, swapped[1], lax.dynamic_index_in_dim(cotangent, half, 0, keepdims=False))
+    length_row = lax.dynamic_index_in_dim(lengths, half, 0, keepdims=False)
+    places = jnp.arange(length, dtype=jnp.int32)
+    segment, within = doc_table(length_row, places)
+    start_row = (places - within)[None]
+    ends = jnp.cumsum(length_row)
+    member = segment[None, :] == jnp.arange(length_row.shape[0], dtype=jnp.int32)[:, None]
+    end_row = jnp.sum(jnp.where(member, ends[:, None], 0), axis=0)[None].astype(jnp.int32)
+    frequency = jnp.exp(jnp.arange(HS // 2, dtype=F32) * (-math.log(10000.0) / (HS // 2)))
+    angles = within.astype(F32)[None, :] * frequency[:, None]
+    tables = (jnp.cos(angles), jnp.sin(angles))
+    a_own = jnp.stack([w_query[0].T, w_key[0].T, w_value[0].T, w_out[0]])
+    f_own = jnp.stack([w_gate[0].T, w_up[0].T, w_down[0]])
+    a_all, f_all = pl.pallas_call(
+        weights_kernel,
+        out_shape=[
+            jax.ShapeDtypeStruct((2, 4, HS, width), LOW),
+            jax.ShapeDtypeStruct((2, 3, units, width), LOW),
+        ],
+        in_specs=[ANY_SPEC] * 2,
+        out_specs=[ANY_SPEC] * 2,
+        scratch_shapes=[
+            pltpu.SemaphoreType.DMA((2, 8)),
+            pltpu.SemaphoreType.DMA((2, 2, 4)),
+            pltpu.SemaphoreType.DMA((2,)),
+        ],
+        compiler_params=pltpu.CompilerParams(collective_id=0, has_side_effects=True),
+        name="weights",
+    )(a_own, f_own)
+    gains = lax.all_gather(jnp.concatenate([attn_gain, mlp_gain]), "section", axis=0, tiled=False)
+    gain_in, gain_mid = [gains[i, 0:1] for i in range(2)], [gains[i, 1:2] for i in range(2)]
+    w_in = [a_all[i, :3].reshape(3 * HS, width) for i in range(2)]
+    w_back = [a_all[i, 3] for i in range(2)]
+    f_w = [f_all[i] for i in range(2)]
+    buf = [pltpu.VMEM((16, rows, width), LOW)]
+    boxes = sum_boxes(rows, width)
+    sem = [pltpu.SemaphoreType.DMA]
+    every = ((16, rows, width), LOW, True)
+    turned_out = ((3 * HS, length), LOW, False)
+    hidden_out = ((length, units), LOW, False)
+    block_out = ((rows, width), F32, False)
+    low_out = ((rows, width), LOW, False)
+    gain_out = ((1, width), F32, False)
+    dout_out = ((HS, length), LOW, False)
+
+    qkv0, normed0 = reach(
+        first_kernel, 1, [own_in, gain_in[0], w_in[0], *tables], [turned_out, every], buf + [links()] + sem, "first"
+    )
+    att0, flat0, lse0 = attend(qkv0, start_row, 512, 512)
+    mid0, out0, hid0, one0, two0, qkv1, nmid0, normed1 = reach(
+        middle_kernel,
+        2,
+        [flat0, own_in, w_back[0], f_w[0], gain_mid[0], gain_in[1], w_in[1], *tables, qkv0[2 * HS :]],
+        [block_out, low_out, hidden_out, hidden_out, hidden_out, turned_out, every, every],
+        buf + boxes + [links(), links()] + sem,
+        "middle",
+    )
+    att1, flat1, lse1 = attend(qkv1, start_row, 512, 512)
+    out1, hid1, dgate1, dup1, dmid1, gmid1, dout1, nmid1, top1, dmid_all1 = reach(
+        turn_kernel,
+        3,
+        [flat1, out0, w_back[1], f_w[1], gain_mid[1], own_top],
+        [low_out, hidden_out, hidden_out, hidden_out, block_out, gain_out, dout_out, every, every, every],
+        buf
+        + boxes
+        + [pltpu.VMEM((rows, width), F32), pltpu.VMEM((length, units), LOW), pltpu.VMEM((length, units), LOW)]
+        + [links(), links()]
+        + sem,
+        "turn",
+    )
+    dqkv1, extra = attend_back(qkv1, start_row, end_row, att1, lse1, dout1, tables, None, 512, 512)
+    grad1, gin1, dgate0, dup0, dmid0, gmid0, dout0, top0, dmid_all0 = reach(
+        lower_kernel,
+        4,
+        [dqkv1, out0, w_in[1], gain_in[1], dmid1, f_w[0], one0, two0, w_back[0], gain_mid[0], mid0],
+        [block_out, gain_out, hidden_out, hidden_out, block_out, gain_out, dout_out, every, every],
+        buf + boxes + [links(), links()] + sem,
+        "lower",
+    )
+    (dqkv0,) = attend_back(qkv0, start_row, end_row, att0, lse0, dout0, tables, extra, 512, 512)
+    grad0, gin0 = reach(
+        last_kernel,
+        5,
+        [dqkv0, own_in, w_in[0], gain_in[0], dmid0],
+        [block_out, gain_out],
+        boxes + [links()],
+        "last",
+    )
+    a_grads, f_grads = [], []
+    for dqkv, normed, flat, dmid_all, dgate, dup, hid, nmid, top in (
+        (dqkv0, normed0, flat0, dmid_all0, dgate0, dup0, hid0, nmid0, top0),
+        (dqkv1, normed1, flat1, dmid_all1, dgate1, dup1, hid1, nmid1, top1),
+    ):
+        normed, dmid_all, nmid, top = (array.reshape(length, width) for array in (normed, dmid_all, nmid, top))
+        grad_in = product(dqkv, normed).reshape(3, HS, width)
+        a_grads.append(jnp.concatenate([grad_in, inner_rows(flat, dmid_all)[None]]).astype(LOW))
+        f_grads.append(
+            jnp.stack([inner_rows(dgate, nmid), inner_rows(dup, nmid), inner_rows(hid, top)]).astype(LOW)
+        )
+    a_in, f_in = pl.pallas_call(
+        grads_kernel,
+        out_shape=[
+            jax.ShapeDtypeStruct((2, 4, 4, HS, width // 4), LOW),
+            jax.ShapeDtypeStruct((2, 4, 3, units, width // 4), LOW),
+        ],
+        in_specs=[ANY_SPEC] * 2,
+        out_specs=[ANY_SPEC] * 2,
+        scratch_shapes=[
+            pltpu.SemaphoreType.DMA((2, 8)),
+            pltpu.SemaphoreType.DMA((2, 2, 4)),
+            pltpu.SemaphoreType.DMA((2,)),
+        ],
+        compiler_params=pltpu.CompilerParams(collective_id=6, has_side_effects=True),
+        name="grads",
+    )(jnp.stack(a_grads), jnp.stack(f_grads))
+    a_sum = jnp.sum(a_in.astype(F32), axis=0)
+    f_sum = jnp.sum(f_in.astype(F32), axis=0)
+    a_sum = jnp.transpose(a_sum, (1, 0, 2, 3)).reshape(4, 4 * HS, width // 4)
+    f_sum = jnp.transpose(f_sum, (1, 0, 2, 3)).reshape(3, 4 * units, width // 4)
+    on_first = y == 0
+    outs = [to_home(out0, 0), to_home(out1, 1)]
+    layer_out = jnp.stack([jnp.where(on_first, outs[0][m], outs[1][m]) for m in range(2)])
+    grads = [to_home(grad0.astype(LOW), 0), to_home(grad1.astype(LOW), 1)]
+    input_grad = jnp.stack([jnp.where(on_first, grads[0][m], grads[1][m]) for m in range(2)]).astype(F32)
+    gain_grads = lax.psum(jnp.concatenate([gin0, gin1, gmid0, gmid1]), AXES)
+    share = width // 16
+    first_col = (4 * (2 * x + c) + 2 * half + p) * share
+    gain_share = lax.dynamic_slice_in_dim(gain_grads, first_col, share, 1)
+    gain_in_share = jnp.where(on_first, gain_share[0:1], gain_share[1:2])
+    gain_mid_share = jnp.where(on_first, gain_share[2:3], gain_share[3:4])
+    return (
+        layer_out[None],
+        input_grad[None],
+        a_sum[0].T[None],
+        a_sum[1].T[None],
+        a_sum[2].T[None],
+        a_sum[3][None],
+        f_sum[0].T[None],
+        f_sum[1].T[None],
+        f_sum[2][None],
+        gain_in_share,
+        gain_mid_share,
+    )
+
+
 def solution(mesh):
     in_specs = (
         P(None, ("seq", "tensor"), None),
@@ -503,6 +1446,7 @@
         P("section", ("seq", "tensor")),
         P("section", ("seq", "tensor")),
     )
+    grid = (mesh.shape["section"], mesh.shape["seq"], mesh.shape["tensor"]) == (2, 4, 4)
     return jax.shard_map(
-        on_device, mesh=mesh, in_specs=in_specs, out_specs=out_specs, check_vma=False
-    )
+        on_grid if grid else on_device, mesh=mesh, in_specs=in_specs, out_specs=out_specs, check_vma=False
+    )

time: 3440 us -> 1050 us (0.31)
  waiting for transfers between devices: 1610 us -> 22.9 us
  matrix products: 1090 us -> 31 us
  Pallas kernels: 0 us -> 814 us
  other arithmetic: 357 us -> 19.7 us
  local copies, waits for them, and re-layouts: 258 us -> 23.5 us
    dot_general x123 -> x0, matrix products: 931 us -> none  [the longest x24 143 us: block_scores(): jnp.einsum('qhd,khd->hqk', query_heads, block_keys, preferred_element_typ...]
    pallas_call x0 -> x11, Pallas kernels: none -> 814 us  [the longest x5 589 us: reach(): pl.pallas_call(kernel, out_shape=[jax.ShapeDtypeStruct(shape, dtype) for...]
    all_gather x33 -> x0, waiting for transfers between devices: 768 us -> none  [the longest x18 623 us: spread(): return lax.all_gather(values, 'tensor', axis=0, tiled=True)]
    reduce_scatter x28 -> x0, waiting for transfers between devices: 739 us -> none  [the longest x15 485 us: fold_rows(): lax.psum_scatter(values.astype(jnp.bfloat16), 'tensor', scatter_dimension...]
    reduce_sum x29 -> x3, other arithmetic: 189 us -> 1.97 us  [the longest x1 1.51 us: on_grid(): a_sum = jnp.sum(a_in.astype(F32), axis=0)]
    dot_general x36 -> x2, matrix products: 115 us -> 3.67 us  [product(): return jnp.dot(left, right, preferred_element_type=jnp.float32)]
    ppermute x4 -> x9, waiting for transfers between devices: 93 us -> 22.9 us  [the longest x8 22.9 us: to_home(): lax.ppermute(values, AXES, home_pairs(layer, micro))]
    and x25 -> x0, other arithmetic: 59.6 us -> none  [allowed_mask(): (key_places[None, :] <= places[:, None]) & (key_segment[None, :] == segme...]
  transfers between devices with their start and end apart: 65 -> 9, of which waited for: 54 -> 1; matrix products, arithmetic and copies ran while one was open for 31% -> 6% of each run, Pallas kernels for 0% -> 56%
where the time goes in v1:
time: 1050 us; the launch traced here: 1040 us
  Pallas kernels  814 us (78%)
  blocking collectives  73.3 us (7%)
  starting transfers between devices  50.8 us (5%)
  matrix products  31 us (3%)
  local copies, waits for them, and re-layouts  23.5 us (2%)
  waiting for transfers between devices  22.9 us (2%)
  other arithmetic  19.7 us (2%)
    pallas_call x5, Pallas kernels, reach(): pl.pallas_call(kernel, out_shape=[jax.ShapeDtypeStruct(shape, dtype) for...  589 us
    pallas_call x2, Pallas kernels, attend_back(): pl.pallas_call(functools.partial(attend_back_kernel, bq=bq, bk=bk, first=...  80.8 us
    pallas_call x2, Pallas kernels, attend(): pl.pallas_call(functools.partial(attend_kernel, bq=bq, bk=bk), out_shape=...  59.3 us
    ppermute x8, starting transfers between devices, to_home(): lax.ppermute(values, AXES, home_pairs(layer, micro))  50.1 us
    pallas_call x1, Pallas kernels, on_grid(): pl.pallas_call(weights_kernel, out_shape=[jax.ShapeDtypeStruct((2, 4, HS,...  48.8 us
    psum x1, blocking collectives, on_grid(): gain_grads = lax.psum(jnp.concatenate([gin0, gin1, gmid0, gmid1]), AXES)  38.9 us
    pallas_call x1, Pallas kernels, on_grid(): pl.pallas_call(grads_kernel, out_shape=[jax.ShapeDtypeStruct((2, 4, 4, HS...  35.5 us
    all_gather x1, blocking collectives, on_grid(): lax.all_gather(jnp.concatenate([attn_gain, mlp_gain]), 'section', axis=0,...  34.4 us
  transfers between devices with their start and end apart: 9, of which 1 were waited for; matrix products, arithmetic and copies ran while one was open for 6% of the time, Pallas kernels for 56%

profile of v1, /device:TPU:0, one launch (start us, length us, event | category | flops | bytes accessed | tf_op | source)
XLA Modules:
  0.0 1036.3 jit_solution(10643680371787036199)
XLA Ops:
  0.7 1.3 constant_dynamic-slice_fusion.1
  2.0 1.1 pad_maximum_fusion.1
  3.1 0.7 collective-permute-start
  4.4 0.6 gather_fusion.3
  5.1 0.6 gather_fusion.2
  5.7 0.6 gather_fusion.1
  6.4 0.6 gather_fusion
  7.4 1.1 pad_maximum_fusion.f_ref
  8.5 0.9 pad_maximum_fusion.2.a_ref
  9.4 48.8 %weights.1 = (bf16[2,4,64,1024]{3,2,1,0:T(8,128)(2,1)}, bf16[2,3,176,1024]{3,2,1,0:T(8,128)(2,1)}) custom-call(bf16[4,256,256]{2,1,0:T(8,128)(2,1)} %pad_maximum_fusion.2.a_ref, bf16[3,704,256]{2,1,0:T(8,128)(2,1)} %pad_maximum_fusion.f_ref), custom_call_target="tpu_custom_call" | custom-call | tf_op jit(solution)/shard_map/weights/pallas_call | solution.py:1289
  58.2 1.8 slice_bitcast_fusion.2
  60.0 2.1 fusion.22
  62.2 34.4 %all-gather.1 = f32[2,2,1024]{2,1,0:T(2,128)S(1)} all-gather(f32[1,2,1024]{2,1,0:T(2,128)S(1)} %maximum_bitcast_fusion.1), channel_id=2, replica_groups=mesh['section'=2,'seq'=4,'tensor'=4] {'section'}, dimensions={0}, use_global_device_ids=true | all-gather | bytes 24576 | tf_op jit(solution)/shard_map/all_gather | solution.py:1305
  96.5 0.6 slice_bitcast_fusion.4
  97.1 1.5 slice_bitcast_fusion
  99.9 3.1 multiply_sine_fusion
  103.1 1.1 fusion.10
  104.1 58.4 %first.1 = (bf16[192,4096]{1,0:T(8,128)(2,1)}, bf16[16,256,1024]{2,1,0:T(8,128)(2,1)}) custom-call(bf16[256,1024]{1,0:T(8,128)(2,1)} %get-tuple-element.142.x_ref, f32[1,1024]{1,0:T(1,128)} %get-tuple-element.152.gain_ref, bf16[192,1024]{1,0:T(8,128)(2,1)} %bitcast.223, f32[32,4096]{1,0:T(8,128)} %get-tuple-element.148.cos_ref, ...), custom_call_target="tpu_custom_call" | custom-call | tf_op jit(solution)/shard_map/first/pallas_call | solution.py:905
  162.5 1.9 slice.91.mix_ref
  164.4 29.7 %attend.2 = (f32[64,4096]{1,0:T(8,128)}, bf16[4096,64]{1,0:T(8,128)(2,1)}, f32[1,4096]{1,0:T(1,128)}) custom-call(s32[4,8]{1,0:T(4,128)} %pad_add_fusion.bounds, bf16[192,4096]{1,0:T(8,128)(2,1)} %get-tuple-element.55.qkv_ref, s32[1,4096]{1,0:T(1,128)} %bitcast.206), custom_call_target="tpu_custom_call" | custom-call | tf_op jit(solution)/shard_map/attend/pallas_call | solution.py:1117
  194.1 148.5 %middle.1 = (f32[256,1024]{1,0:T(8,128)}, bf16[256,1024]{1,0:T(8,128)(2,1)}, bf16[4096,176]{1,0:T(8,128)(2,1)}, bf16[4096,176]{1,0:T(8,128)(2,1)}, bf16[4096,176...) custom-call(bf16[4096,64]{1,0:T(8,128)(2,1)} %get-tuple-element.56.at, ...), custom_call_target="tpu_custom_call" | custom-call | tf_op jit(solution)/shard_map/middle/pallas_call | solution.py:905
  342.6 1.3 collective-permute-start.3
  343.9 5.4 collective-permute-start.1
  349.3 29.6 %attend.3 = (f32[64,4096]{1,0:T(8,128)}, bf16[4096,64]{1,0:T(8,128)(2,1)}, f32[1,4096]{1,0:T(1,128)}) custom-call(s32[4,8]{1,0:T(4,128)} %pad_add_fusion.bounds, bf16[192,4096]{1,0:T(8,128)(2,1)} %get-tuple-element.59.qkv_ref, s32[1,4096]{1,0:T(1,128)} %bitcast.207), custom_call_target="tpu_custom_call" | custom-call | tf_op jit(solution)/shard_map/attend/pallas_call | solution.py:1117
  379.0 202.4 %turn.1 = (bf16[256,1024]{1,0:T(8,128)(2,1)}, bf16[4096,176]{1,0:T(8,128)(2,1)}, bf16[4096,176]{1,0:T(8,128)(2,1)}, bf16[4096,176]{1,0:T(8,128)(2,1)}, f32[256,1...) custom-call(bf16[4096,64]{1,0:T(8,128)(2,1)} %get-tuple-element.60.a, ...), custom_call_target="tpu_custom_call" | custom-call | tf_op jit(solution)/shard_map/turn/pallas_call | solution.py:905
  581.4 1.5 collective-permute-start.4
  582.9 3.6 collective-permute-start.2
  586.5 5.1 fusion.9
  591.7 0.6 copy-done
  592.9 1.7 fusion.5
  594.6 1.7 fusion.6
  596.3 40.5 %attend_back.2 = (bf16[192,4096]{1,0:T(8,128)(2,1)}, f32[64,4096]{1,0:T(8,128)}) custom-call(s32[4,8]{1,0:T(4,128)} %pad_add_fusion.1.bounds, bf16[192,4096]{1,0:T(8,128)(2,1)} %get-tuple-element.59.qkv_ref, s32[1,4096]{1,0:T(1,128)} %bitcast.208, f32[64,4096]{1,0:T(8,128)} %get-tuple-element.64.att_ref, f32[1,4096]{1,0:T(1,128)} %get-tuple-element.65.lse_ref, ...), custom_call_target="tpu_custom_call" | custom-call | tf_op jit(solution)/shard_map/attend_back/pallas_call | solution.py:1217
  636.8 142.6 %lower.1 = (f32[256,1024]{1,0:T(8,128)}, f32[1,1024]{1,0:T(1,128)}, bf16[4096,176]{1,0:T(8,128)(2,1)}, bf16[4096,176]{1,0:T(8,128)(2,1)}, f32[256,1024]{1,0:T(8,...) custom-call(bf16[192,4096]{1,0:T(8,128)(2,1)} %get-tuple-element.67., ...), custom_call_target="tpu_custom_call" | custom-call | tf_op jit(solution)/shard_map/lower/pallas_call | solution.py:905
  779.4 5.0 fusion.8
  784.4 40.3 %attend_back.3.dqkv_ref = bf16[192,4096]{1,0:T(8,128)(2,1)} custom-call(s32[4,8]{1,0:T(4,128)} %pad_add_fusion.1.bounds, bf16[192,4096]{1,0:T(8,128)(2,1)} %get-tuple-element.55.qkv_ref, s32[1,4096]{1,0:T(1,128)} %bitcast.209, f32[64,4096]{1,0:T(8,128)} %get-tuple-element.62.att_ref, f32[1,4096]{1,0:T(1,128)} %get-tuple-element.63.lse_ref, ...), custom_call_target="tpu_custom_call" | custom-call | tf_op jit(solution)/shard_map/attend_back/pallas_call | solution.py:1217
  824.7 37.2 %last.1 = (f32[256,1024]{1,0:T(8,128)}, f32[1,1024]{1,0:T(1,128)}) custom-call(bf16[192,4096]{1,0:T(8,128)(2,1)} %attend_back.3.dqkv_ref, bf16[256,1024]{1,0:T(8,128)(2,1)} %get-tuple-element.142.x_ref, bf16[192,1024]{1,0:T(8,128)(2,1)} %bitcast.224, f32[1,1024]{1,0:T(1,128)} %get-tuple-element.152.gain_ref, f32[256,1024]{1,0:T(8,128)} %get-tuple-element.74.dmid_ref), custom_call_target="tpu_custom_call" | custom-call | tf_op jit(solution)/shard_map/last/pallas_call | solution.py:905
  861.9 0.7 pad_maximum_fusion.3
  862.6 38.9 %psum.7 = f32[4,1024]{1,0:T(4,128)S(1)} all-reduce(f32[4,1024]{1,0:T(4,128)S(1)} %pad_maximum_fusion.3), channel_id=1, replica_groups=mesh['section'=2,'seq'=4,'tensor'=4] {'section','seq','tensor'}, use_global_device_ids=true, to_apply=%region_6.7 | all-reduce | flops 4096 | bytes 32768 | tf_op jit(solution)/shard_map/psum | solution.py:1400
  901.6 5.2 fusion.2
  906.8 5.3 fusion.3
  912.3 1.8 fusion.1
  914.2 1.7 fusion.7
  915.9 0.7 slice-done.3
  917.2 1.7 fusion.4
  918.9 1.2 slice-done.5
  920.1 1.8 fusion
  921.9 1.1 maximum_maximum_fusion.1.a_ref
  923.0 1.5 maximum_maximum_fusion.f_ref
  924.5 35.5 %grads.1 = (bf16[2,4,4,64,256]{4,3,2,1,0:T(8,128)(2,1)}, bf16[2,4,3,176,256]{4,3,2,1,0:T(8,128)(2,1)}) custom-call(bf16[2,4,64,1024]{3,2,1,0:T(8,128)(2,1)} %maximum_maximum_fusion.1.a_ref, bf16[2,3,176,1024]{3,2,1,0:T(8,128)(2,1)} %maximum_maximum_fusion.f_ref), custom_call_target="tpu_custom_call" | custom-call | tf_op jit(solution)/shard_map/grads/pallas_call | solution.py:1375
  960.0 1.5 convert_reduce_fusion.1
  961.5 0.9 fusion.21
  962.4 2.1 copy.46
  964.5 1.8 copy.45
  966.3 0.8 copy.44
  967.2 0.7 collective-permute-start.8
  968.3 1.4 fusion.20
  970.7 35.6 %collective-permute-start.6 = (bf16[256,1024]{1,0:T(8,128)(2,1)S(1)}, bf16[256,1024]{1,0:T(8,128)(2,1)S(1)}, u32[]{:S(2)}, u32[]{:S(2)}) collective-permute-start(bf16[256,1024]{1,0:T(8,128)(2,1)S(1)} %convert_element_type.67), channel_id=1, source_target_pairs={{0,16},{1,17},{4,22},{5,23},{8,24},{9,25},{12,30},{13,31},{16,18},... | collective-permute-start | bytes 1572872 | tf_op jit(solution)/shard_map/ppermute | solution.py:1261
  1006.4 1.3 collective-permute-start.7
  1007.7 1.1 select_bitcast_fusion.2
  1008.8 0.7 collective-permute-start.5
  1009.5 1.1 select_bitcast_fusion.3
  1010.6 1.1 maximum_bitcast_fusion
  1011.7 22.9 %collective-permute-done.7 = bf16[256,1024]{1,0:T(8,128)(2,1)S(1)} collective-permute-done((bf16[256,1024]{1,0:T(8,128)(2,1)S(1)}, bf16[256,1024]{1,0:T(8,128)(2,1)S(1)}, u32[]{:S(2)}, u32[]{:S(2)}) %collective-permute-start.7) | collective-permute-done | bytes 524320 | tf_op jit(solution)/shard_map/ppermute | solution.py:1261
  1034.7 1.5 maximum_convert_fusion
  (114 shorter events, 5.2 us)
Async XLA Ops:
  0.6 3.2 copy-start.30
  1.9 5.1 copy-start.21
  2.0 5.2 copy-start.22
  2.0 5.3 copy-start.23
  2.0 5.4 copy-start.18
  2.0 5.4 copy-start.19
  2.0 5.4 copy-start.20
  3.1 100.0 %collective-permute-start = (bf16[2,256,1024]{2,1,0:T(8,128)(2,1)}, bf16[2,256,1024]{2,1,0:T(8,128)(2,1)S(1)}, u32[]{:S(2)}, u32[]{:S(2)}) collective-permute-start(bf16[2,256,1024]{2,1,0:T(8,128)(2,1)} %pad_maximum_fusion.1), channel_id=1, source_target_pairs={{4,6},{5,7},{6,4},{7,5},{12,14},{13,15},{14,12},{15,13},{16,18},{1... | collective-permute-start | bytes 3145736 | tf_op jit(solution)/shard_map/ppermute | solution.py:1274
  4.4 4.1 copy-start.1
  5.1 3.4 copy-start.24
  8.5 53.6 %copy-start.25 = (f32[1,1024]{1,0:T(1,128)S(1)}, f32[1,1024]{1,0:T(1,128)}, u32[]{:S(2)}) copy-start(f32[1,1024]{1,0:T(1,128)} %param.23) | copy-start | bytes 12292
  8.5 53.6 %copy-start.26 = (f32[1,1024]{1,0:T(1,128)S(1)}, f32[1,1024]{1,0:T(1,128)}, u32[]{:S(2)}) copy-start(f32[1,1024]{1,0:T(1,128)} %param.22) | copy-start | bytes 12292
  58.2 38.9 %copy-start.12 = (bf16[2,3,176,1024]{3,2,1,0:T(8,128)(2,1)S(1)}, bf16[2,3,176,1024]{3,2,1,0:T(8,128)(2,1)}, u32[]{:S(2)}) copy-start(bf16[2,3,176,1024]{3,2,1,0:T(8,128)(2,1)} %get-tuple-element.57) | copy-start | bytes 6488068
  97.1 5.9 copy-start.16
  97.1 5.9 copy-start.17
  342.6 628.1 %collective-permute-start.3 = (bf16[256,1024]{1,0:T(8,128)(2,1)}, bf16[256,1024]{1,0:T(8,128)(2,1)}, u32[]{:S(2)}, u32[]{:S(2)}) collective-permute-start(bf16[256,1024]{1,0:T(8,128)(2,1)} %get-tuple-element.58.x_ref), channel_id=1, source_target_pairs={{2,2},{3,3},{6,4},{7,5},{10,10},{11,11},{14,12},{15,13},{18,0},{19... | collective-permute-start | bytes 1572872 | tf_op jit(solution)/shard_map/ppermute | solution.py:1261
  343.9 664.8 %collective-permute-start.1 = (bf16[256,1024]{1,0:T(8,128)(2,1)}, bf16[256,1024]{1,0:T(8,128)(2,1)}, u32[]{:S(2)}, u32[]{:S(2)}) collective-permute-start(bf16[256,1024]{1,0:T(8,128)(2,1)} %get-tuple-element.58.x_ref), channel_id=1, source_target_pairs={{0,0},{1,1},{4,6},{5,7},{8,8},{9,9},{12,14},{13,15},{16,2},{17,3},... | collective-permute-start | bytes 1572872 | tf_op jit(solution)/shard_map/ppermute | solution.py:1261
  379.0 207.6 %copy-start.2 = (bf16[4096,64]{1,0:T(8,128)(2,1)S(1)}, bf16[4096,64]{1,0:T(8,128)(2,1)}, u32[]{:S(2)}) copy-start(bf16[4096,64]{1,0:T(8,128)(2,1)} %get-tuple-element.60.att_ref) | copy-start | bytes 1572868
  581.4 424.9 %collective-permute-start.4 = (bf16[256,1024]{1,0:T(8,128)(2,1)}, bf16[256,1024]{1,0:T(8,128)(2,1)}, u32[]{:S(2)}, u32[]{:S(2)}) collective-permute-start(bf16[256,1024]{1,0:T(8,128)(2,1)} %get-tuple-element.61), channel_id=1, source_target_pairs={{2,18},{3,19},{6,20},{7,21},{10,26},{11,27},{14,28},{15,29},{18,16... | collective-permute-start | bytes 1572872 | tf_op jit(solution)/shard_map/ppermute | solution.py:1261
  582.9 426.6 %collective-permute-start.2 = (bf16[256,1024]{1,0:T(8,128)(2,1)}, bf16[256,1024]{1,0:T(8,128)(2,1)}, u32[]{:S(2)}, u32[]{:S(2)}) collective-permute-start(bf16[256,1024]{1,0:T(8,128)(2,1)} %get-tuple-element.61), channel_id=1, source_target_pairs={{0,16},{1,17},{4,22},{5,23},{8,24},{9,25},{12,30},{13,31},{16,18},... | collective-permute-start | bytes 1572872 | tf_op jit(solution)/shard_map/ppermute | solution.py:1261
  586.5 5.8 copy-start
  586.5 6.4 copy-start.10
  592.9 1.7 copy-start.9
  636.8 142.6 %copy-start.3 = (bf16[4096,64]{1,0:T(8,128)(2,1)S(1)}, bf16[4096,64]{1,0:T(8,128)(2,1)}, u32[]{:S(2)}) copy-start(bf16[4096,64]{1,0:T(8,128)(2,1)} %get-tuple-element.56.att_ref) | copy-start | bytes 1572868
  824.7 37.2 %copy-start.27 = (f32[1,1024]{1,0:T(1,128)S(1)}, f32[1,1024]{1,0:T(1,128)}, u32[]{:S(2)}) copy-start(f32[1,1024]{1,0:T(1,128)} %get-tuple-element.96) | copy-start | bytes 12292
  824.7 37.2 %copy-start.28 = (f32[1,1024]{1,0:T(1,128)S(1)}, f32[1,1024]{1,0:T(1,128)}, u32[]{:S(2)}) copy-start(f32[1,1024]{1,0:T(1,128)} %get-tuple-element.94) | copy-start | bytes 12292
  824.7 37.2 %copy-start.29 = (f32[1,1024]{1,0:T(1,128)S(1)}, f32[1,1024]{1,0:T(1,128)}, u32[]{:S(2)}) copy-start(f32[1,1024]{1,0:T(1,128)} %get-tuple-element.95) | copy-start | bytes 12292
  824.7 76.8 %copy-start.8 = (bf16[4096,176]{1,0:T(8,128)(2,1)S(1)}, bf16[4096,176]{1,0:T(8,128)(2,1)}, u32[]{:S(2)}) copy-start(bf16[4096,176]{1,0:T(8,128)(2,1)} %get-tuple-element.81) | copy-start | bytes 4325380
  901.5 5.2 copy-start.7
  901.5 10.6 %slice-start.6 = ((s8[8388608]{0:T(1024)(128)(4,1)}), s8[4194304]{0:T(1024)(128)(4,1)S(1)}, s32[]{:S(2)}) async-start(s8[8388608]{0:T(1024)(128)(4,1)} %bitcast.243), calls=%async_computation.6 | async-start | bytes 8388608
  901.5 12.6 %slice-start = ((s8[8388608]{0:T(1024)(128)(4,1)}), s8[4194304]{0:T(1024)(128)(4,1)S(1)}, s32[]{:S(2)}) async-start(s8[8388608]{0:T(1024)(128)(4,1)} %bitcast.212), calls=%async_computation | async-start | bytes 8388608
  906.8 5.3 copy-start.13
  906.8 5.5 slice-start.7
  906.8 7.3 slice-start.1
  912.3 1.9 copy-start.6
  912.3 3.6 slice-start.2
  914.1 2.4 slice-start.3
  914.2 3.0 copy-start.5
  914.2 4.7 slice-start.4
  917.2 1.7 copy-start.4
  917.2 2.9 slice-start.5
  961.5 5.7 copy-start.14
  961.5 6.4 copy-start.11
  967.2 44.4 %collective-permute-start.8 = (bf16[256,1024]{1,0:T(8,128)(2,1)S(1)}, bf16[256,1024]{1,0:T(8,128)(2,1)S(1)}, u32[]{:S(2)}, u32[]{:S(2)}) collective-permute-start(bf16[256,1024]{1,0:T(8,128)(2,1)S(1)} %convert_element_type.67), channel_id=1, source_target_pairs={{2,18},{3,19},{6,20},{7,21},{10,26},{11,27},{14,28},{15,29},{18,16... | collective-permute-start | bytes 1572872 | tf_op jit(solution)/shard_map/ppermute | solution.py:1261
  968.3 1.8 copy-start.15
  970.7 63.9 %collective-permute-start.6 = (bf16[256,1024]{1,0:T(8,128)(2,1)S(1)}, bf16[256,1024]{1,0:T(8,128)(2,1)S(1)}, u32[]{:S(2)}, u32[]{:S(2)}) collective-permute-start(bf16[256,1024]{1,0:T(8,128)(2,1)S(1)} %convert_element_type.67), channel_id=1, source_target_pairs={{0,16},{1,17},{4,22},{5,23},{8,24},{9,25},{12,30},{13,31},{16,18},... | collective-permute-start | bytes 1572872 | tf_op jit(solution)/shard_map/ppermute | solution.py:1261
  1006.4 28.2 %collective-permute-start.7 = (bf16[256,1024]{1,0:T(8,128)(2,1)S(1)}, bf16[256,1024]{1,0:T(8,128)(2,1)S(1)}, u32[]{:S(2)}, u32[]{:S(2)}) collective-permute-start(bf16[256,1024]{1,0:T(8,128)(2,1)S(1)} %convert_element_type.66), channel_id=1, source_target_pairs={{2,2},{3,3},{6,4},{7,5},{10,10},{11,11},{14,12},{15,13},{18,0},{19... | collective-permute-start | bytes 1572872 | tf_op jit(solution)/shard_map/ppermute | solution.py:1261
  1008.8 25.9 %collective-permute-start.5 = (bf16[256,1024]{1,0:T(8,128)(2,1)S(1)}, bf16[256,1024]{1,0:T(8,128)(2,1)S(1)}, u32[]{:S(2)}, u32[]{:S(2)}) collective-permute-start(bf16[256,1024]{1,0:T(8,128)(2,1)S(1)} %convert_element_type.66), channel_id=1, source_target_pairs={{0,0},{1,1},{4,6},{5,7},{8,8},{9,9},{12,14},{13,15},{16,2},{17,3},... | collective-permute-start | bytes 1572872 | tf_op jit(solution)/shard_map/ppermute | solution.py:1261

commit v2 on v0

--- a/solution.py
+++ b/solution.py
@@ -1,8 +1,11 @@
+import functools
 import math
 
 import jax
 import jax.numpy as jnp
 from jax import lax
+from jax.experimental import pallas as pl
+from jax.experimental.pallas import tpu as pltpu
 from jax.sharding import PartitionSpec as P
 
 HS = 64
@@ -475,6 +478,1264 @@
     )
 
 
+MESH_ID = pl.DeviceIdType.MESH
+LOW = jnp.bfloat16
+F32 = jnp.float32
+ORDERS = ((1, 2, 4), (2, 4, 1), (4, 1, 2))
+LEVELS = ((0,), (1, 2, 4), (3, 5, 6), (7,))
+NT = (((1,), (1,)), ((), ()))
+NN = (((1,), (0,)), ((), ()))
+TN = (((0,), (0,)), ((), ()))
+VMEM_BYTES = 52 * 2**20
+
+
+def dot(left, right, dims=NN):
+    return lax.dot_general(left, right, dims, preferred_element_type=F32)
+
+
+def flip(value, bit):
+    if isinstance(bit, int):
+        return 1 - value if bit else value
+    return value + bit - 2 * value * bit
+
+
+def spot():
+    y, s, z = lax.axis_index("section"), lax.axis_index("seq"), lax.axis_index("tensor")
+    return (y, lax.div(s, 2), lax.rem(s, 2), lax.div(z, 2), lax.rem(z, 2))
+
+
+def device(at):
+    y, x, c, h, p = at
+    return (y, 2 * x + c, 2 * h + p)
+
+
+def moved(at, mask, core=0):
+    y, x, c, h, p = at
+    if isinstance(mask, int):
+        bits = (mask & 1, (mask >> 1) & 1, mask >> 2)
+    else:
+        bits = (lax.rem(mask, 2), lax.rem(lax.div(mask, 2), 2), lax.div(mask, 4))
+    return (flip(y, bits[1]), flip(x, bits[0]), flip(c, core), h, flip(p, bits[2]))
+
+
+def far_role(at):
+    return flip(at[0], at[2])
+
+
+def lane_of(at):
+    return 2 * flip(at[3], far_role(at)) + at[4]
+
+
+def block_of(at):
+    return (2 * at[1] + at[2]) * 4 + lane_of(at)
+
+
+def level_mask(level, i):
+    if level == 0:
+        return 0 * i
+    if level == 1:
+        return 1 + i + lax.div(i, 2)
+    if level == 2:
+        return 3 + i + lax.div(i + 1, 2)
+    return 0 * i + 7
+
+
+def last_bit(k, mask):
+    return [bit for bit in ORDERS[k] if bit & mask][-1]
+
+
+def parts_of(rows):
+    units = rows // 16
+    small = units // 3
+    sizes = (16 * (units - 2 * small), 16 * small, 16 * small)
+    return ((0, sizes[0]), (sizes[0], sizes[1]), (sizes[0] + sizes[1], sizes[2]))
+
+
+def remote(src, dst, send, recv, at):
+    return pltpu.make_async_remote_copy(
+        src_ref=src, dst_ref=dst, send_sem=send, recv_sem=recv, device_id=device(at), device_id_type=MESH_ID
+    )
+
+
+def greet(at, *pushes, peers=()):
+    count = 4 + len(peers)
+    for mask, core in ((1, 0), (2, 0), (4, 0), (0, 1)):
+        signal(moved(at, mask, core))
+    for peer in peers:
+        signal(peer)
+    for push in pushes:
+        count = count + push.greet()
+    pl.semaphore_wait(pltpu.get_barrier_semaphore(), count)
+
+
+def gather(at, buf, sems, on_block, keep=None, ready=None):
+    send, recv, csend, crecv = sems
+    parts = parts_of(buf.shape[1])
+
+    def rows(mask, k, core=0):
+        return buf.at[block_of(moved(at, mask, core)), pl.ds(*parts[k])]
+
+    def hop(k, target):
+        bit = last_bit(k, target)
+        ref = rows(target ^ bit, k)
+        return remote(ref, ref, send.at[k, target], recv.at[k, target], moved(at, bit))
+
+    def arrival(k, target):
+        ref = rows(target, k)
+        return remote(ref, ref, send.at[k, target], recv.at[k, target], moved(at, last_bit(k, target)))
+
+    def across(mask, core=0):
+        ref = buf.at[block_of(moved(at, mask, core))]
+        return remote(ref, ref, csend.at[mask], crecv.at[mask], moved(at, 0, 1))
+
+    def visit(level, core):
+        def one(i, none):
+            b = block_of(moved(at, level_mask(level, i), core))
+            if keep is not None:
+                pltpu.make_async_copy(buf.at[b], keep[0].at[b], keep[1].at[b]).start()
+            on_block(b)
+            return none
+
+        lax.fori_loop(0, len(LEVELS[level]), one, 0)
+
+    for i in range(2):
+        for k in range(3):
+            hop(k, ORDERS[k][i]).start()
+        if i == 0:
+            across(0).start()
+    if ready is not None:
+        ready()
+    visit(0, 0)
+    across(0, 1).wait_recv()
+    visit(0, 1)
+    for k in range(3):
+        first, second, third = ORDERS[k]
+        arrival(k, first).wait_recv()
+        hop(k, first | second).start()
+    for k in range(3):
+        first, second, third = ORDERS[k]
+        hop(k, third).start()
+        hop(k, first | third).start()
+    for k in range(3):
+        first, second, third = ORDERS[k]
+        arrival(k, second).wait_recv()
+        hop(k, second | third).start()
+    for k in range(3):
+        first, second, third = ORDERS[k]
+        arrival(k, first | second).wait_recv()
+        hop(k, 7).start()
+    for level in (1, 2, 3):
+        for mask in LEVELS[level]:
+            for k in range(3):
+                first, second, third = ORDERS[k]
+                if mask not in (first, second, first | second):
+                    arrival(k, mask).wait_recv()
+            across(mask).start()
+        visit(level, 0)
+        for mask in LEVELS[level]:
+            across(mask, 1).wait_recv()
+        visit(level, 1)
+    for k in range(3):
+        for target in range(1, 8):
+            hop(k, target).wait_send()
+    for mask in range(8):
+        across(mask).wait_send()
+
+
+def kept(buf, keep):
+    for b in range(16):
+        pltpu.make_async_copy(buf.at[b], keep[0].at[b], keep[1].at[b]).wait()
+
+
+def scatter(at, total, boxes, sems, partial, before_last=None):
+    out_c, in_c, rin = boxes
+    send, recv, csend, crecv = sems
+    parts = parts_of(total.shape[0])
+
+    def hop(k, target):
+        rows = pl.ds(*parts[k])
+        return remote(
+            in_c.at[target, rows],
+            rin.at[target - 1, rows],
+            send.at[k, target],
+            recv.at[k, target],
+            moved(at, last_bit(k, target)),
+        )
+
+    def across(mask):
+        return remote(out_c.at[mask], in_c.at[mask], csend.at[mask], crecv.at[mask], moved(at, 0, 1))
+
+    def emit(level):
+        def one(i, none):
+            mask = level_mask(level, i)
+            out_c[mask] = partial(block_of(moved(at, mask, 1))).astype(LOW)
+            return none
+
+        lax.fori_loop(0, len(LEVELS[level]), one, 0)
+        for mask in LEVELS[level]:
+            across(mask).start()
+
+    def settle(level):
+        for mask in LEVELS[level]:
+            across(mask).wait_recv()
+
+        def one(i, none):
+            mask = level_mask(level, i)
+            mine = partial(block_of(moved(at, mask))) + in_c[mask].astype(F32)
+            if level == 0:
+                total[...] = mine
+            else:
+                in_c[mask] = mine.astype(LOW)
+            return none
+
+        lax.fori_loop(0, len(LEVELS[level]), one, 0)
+        for mask in LEVELS[level]:
+            for k in range(3):
+                if mask & ORDERS[k][2]:
+                    hop(k, mask).start()
+
+    def arrived(k, target):
+        hop(k, target).wait_recv()
+        return rin[target - 1, pl.ds(*parts[k])].astype(F32)
+
+    emit(3)
+    emit(2)
+    settle(3)
+    settle(2)
+    emit(1)
+    settle(1)
+    if before_last is not None:
+        before_last()
+    emit(0)
+    settle(0)
+    for mask_of in (lambda a, b: a | b, lambda a, b: b):
+        for k in range(3):
+            first, second, third = ORDERS[k]
+            mask, rows = mask_of(first, second), pl.ds(*parts[k])
+            in_c[mask, rows] = (in_c[mask, rows].astype(F32) + arrived(k, mask | third)).astype(LOW)
+            hop(k, mask).start()
+    for k in range(3):
+        first, second, third = ORDERS[k]
+        rows = pl.ds(*parts[k])
+        in_c[first, rows] = (
+            in_c[first, rows].astype(F32) + arrived(k, first | third) + arrived(k, first | second)
+        ).astype(LOW)
+        hop(k, first).start()
+    for k in range(3):
+        first, second, third = ORDERS[k]
+        rows = pl.ds(*parts[k])
+        total[rows] = total[rows] + arrived(k, third) + arrived(k, second) + arrived(k, first)
+    for k in range(3):
+        for target in range(1, 8):
+            hop(k, target).wait_send()
+    for mask in range(8):
+        across(mask).wait_send()
+
+
+def same(a, b):
+    return 1 - jnp.minimum(jnp.abs(a - b), 1)
+
+
+def signal(at):
+    pl.semaphore_signal(pltpu.get_barrier_semaphore(), inc=1, device_id=device(at), device_id_type=MESH_ID)
+
+
+class ToHeads:
+    def __init__(self, at, layer, piece, place, sems):
+        self.at, self.layer, self.piece, self.place = at, layer, piece, place
+        self.send, self.recv, self.local = sems
+        y, x, c, h, p = at
+        self.s = 2 * x + c
+        self.sends = same(y, layer)
+        self.near = 1 - far_role(at)
+
+    def is_me(self, j):
+        return self.sends * self.near * same(self.s, j)
+
+    def greet(self):
+        half = flip(self.at[3], far_role(self.at))
+        for k in range(4):
+
+            @pl.when(self.is_me(k) == 0)
+            def _(k=k):
+                signal((self.layer, k // 2, k % 2, half, self.at[4]))
+
+        return self.sends * (8 - self.near)
+
+    def home(self, j, other):
+        h, p = self.at[3], self.at[4]
+        return (1 - j % 2, j // 2, j % 2, 1 - h, p) if other else (j % 2, j // 2, j % 2, h, p)
+
+    def copy(self, j, other):
+        return remote(
+            self.piece(j), self.place(self.s), self.send.at[4 * other + j], self.recv.at[self.s], self.home(j, other)
+        )
+
+    def start(self):
+        for j in range(4):
+
+            @pl.when(self.sends == 1)
+            def _(j=j):
+                self.copy(j, 1).start()
+
+        for j in range(4):
+
+            @pl.when(self.sends - self.is_me(j) == 1)
+            def _(j=j):
+                self.copy(j, 0).start()
+
+            @pl.when(self.is_me(j) == 1)
+            def _(j=j):
+                pltpu.make_async_copy(self.piece(j), self.place(j), self.local).start()
+
+    def finish(self):
+        for k in range(4):
+            dst = self.place(k)
+
+            @pl.when(self.is_me(k) == 0)
+            def _(k=k, dst=dst):
+                remote(dst, dst, self.send.at[0], self.recv.at[k], self.at).wait_recv()
+
+            @pl.when(self.is_me(k) == 1)
+            def _(k=k, dst=dst):
+                pltpu.make_async_copy(self.piece(k), dst, self.local).wait()
+
+        for j in range(4):
+
+            @pl.when(self.sends == 1)
+            def _(j=j):
+                self.copy(j, 1).wait_send()
+
+            @pl.when(self.sends - self.is_me(j) == 1)
+            def _(j=j):
+                self.copy(j, 0).wait_send()
+
+
+class ToShards:
+    def __init__(self, at, layer, piece, place, sems):
+        self.at, self.layer, self.piece, self.place = at, layer, piece, place
+        self.send, self.recv, self.local = sems
+        y, x, c, h, p = at
+        self.s = 2 * x + c
+        self.gets = same(y, layer)
+        self.role = far_role(at)
+
+    def is_me(self, k):
+        return self.gets * (1 - self.role) * same(self.s, k)
+
+    def greet(self):
+        h, p = self.at[3], self.at[4]
+        for j in range(4):
+
+            @pl.when(self.gets == 1)
+            def _(j=j):
+                signal((1 - j % 2, j // 2, j % 2, 1 - h, p))
+
+            @pl.when(self.gets - self.is_me(j) == 1)
+            def _(j=j):
+                signal((j % 2, j // 2, j % 2, h, p))
+
+        return 4 - self.gets * (1 - self.role)
+
+    def copy(self, k):
+        home = (self.layer, k // 2, k % 2, flip(self.at[3], self.role), self.at[4])
+        return remote(
+            self.piece(k), self.place(self.role, self.s), self.send.at[k], self.recv.at[self.role, self.s], home
+        )
+
+    def start(self):
+        for k in range(4):
+
+            @pl.when(self.is_me(k) == 0)
+            def _(k=k):
+                self.copy(k).start()
+
+            @pl.when(self.is_me(k) == 1)
+            def _(k=k):
+                pltpu.make_async_copy(self.piece(k), self.place(0, k), self.local).start()
+
+    def finish(self):
+        for role in range(2):
+            for j in range(4):
+                dst = self.place(role, j)
+                comes = self.gets if role else self.gets - self.is_me(j)
+
+                @pl.when(comes == 1)
+                def _(role=role, j=j, dst=dst):
+                    remote(dst, dst, self.send.at[0], self.recv.at[role, j], self.at).wait_recv()
+
+        for k in range(4):
+
+            @pl.when(self.is_me(k) == 0)
+            def _(k=k):
+                self.copy(k).wait_send()
+
+            @pl.when(self.is_me(k) == 1)
+            def _(k=k):
+                pltpu.make_async_copy(self.piece(k), self.place(0, k), self.local).wait()
+
+
+class ToHome:
+    def __init__(self, at, layer, block, place, sems):
+        self.at, self.layer, self.block, self.place = at, layer, block, place
+        self.send, self.recv, self.local = sems
+        y, x, c, h, p = at
+        self.gets = same(y, layer)
+        self.role = far_role(at)
+        self.is_me = self.gets * (1 - self.role)
+
+    def holder(self, micro):
+        y, x, c, h, p = self.at
+        role = flip(h, micro)
+        return (flip(role, c), x, c, micro, p), (1 - role) * self.is_me
+
+    def greet(self):
+        for micro in range(2):
+            holder, is_me = self.holder(micro)
+
+            @pl.when(self.gets - is_me == 1)
+            def _(holder=holder):
+                signal(holder)
+
+        return 1 - self.is_me
+
+    def copy(self):
+        y, x, c, h, p = self.at
+        home = (self.layer, x, c, flip(h, self.role), p)
+        return remote(self.block, self.place(h), self.send, self.recv.at[h], home)
+
+    def keep(self):
+        return pltpu.make_async_copy(self.block, self.place(self.at[3]), self.local)
+
+    def start(self):
+        @pl.when(self.is_me == 0)
+        def _():
+            self.copy().start()
+
+        @pl.when(self.is_me == 1)
+        def _():
+            self.keep().start()
+
+    def finish(self):
+        for micro in range(2):
+            dst = self.place(micro)
+
+            @pl.when(self.gets - self.holder(micro)[1] == 1)
+            def _(micro=micro, dst=dst):
+                remote(dst, dst, self.send, self.recv.at[micro], self.at).wait_recv()
+
+        @pl.when(self.is_me == 0)
+        def _():
+            self.copy().wait_send()
+
+        @pl.when(self.is_me == 1)
+        def _():
+            self.keep().wait()
+
+
+def home_sems():
+    dma = pltpu.SemaphoreType.DMA
+    return (dma, dma((2,)), dma)
+
+
+def head_sems():
+    dma = pltpu.SemaphoreType.DMA
+    return (dma((8,)), dma((4,)), dma)
+
+
+def shard_sems():
+    dma = pltpu.SemaphoreType.DMA
+    return (dma((4,)), dma((2, 4)), dma)
+
+
+def slices(ref, size):
+    return lambda j: ref.at[:, pl.ds(j * size, size)]
+
+
+def columns(ref):
+    wide = ref.shape[-1] // 4
+
+    def place(s):
+        start = s * wide
+        return ref.at[:, :, pl.ds(start if isinstance(s, int) else pl.multiple_of(start, wide), wide)]
+
+    return place
+
+
+def unit_of(values):
+    inverse = lax.rsqrt(jnp.mean(values * values, axis=-1, keepdims=True) + EPSILON)
+    return (values * inverse, inverse)
+
+
+def back_of(grad_normed, values, gain_row):
+    unit, inverse = unit_of(values)
+    shaped = grad_normed * gain_row
+    inner = jnp.mean(shaped * unit, axis=-1, keepdims=True)
+    return (inverse * (shaped - unit * inner), jnp.sum(grad_normed * unit, axis=0, keepdims=True))
+
+
+def span(b, rows):
+    return pl.ds(pl.multiple_of(b * rows, rows), rows)
+
+
+def turned(top, bottom, cosine, sine):
+    return (top * cosine - bottom * sine, bottom * cosine + top * sine)
+
+
+def project_block(b, buf, w_ref, cos_ref, sin_ref, mix_ref, qkv_ref):
+    rows, half = buf.shape[1], HS // 2
+    cols = span(b, rows)
+    raw = dot(w_ref[...], buf[b], NT)
+    cosine, sine = cos_ref[:, cols], sin_ref[:, cols]
+    for first, scale in ((0, HS**-0.5), (HS, 1.0)):
+        a, bb = turned(raw[first : first + half], raw[first + half : first + HS], cosine, sine)
+        qkv_ref[first : first + half, cols] = (a.astype(LOW) * scale).astype(LOW)
+        qkv_ref[first + half : first + HS, cols] = (bb.astype(LOW) * scale).astype(LOW)
+    value = raw[2 * HS :]
+    if mix_ref is not None:
+        value = 0.5 * value + 0.5 * mix_ref[:, cols].astype(F32)
+    qkv_ref[2 * HS :, cols] = value.astype(LOW)
+
+
+def first_kernel(
+    cos_ref, sin_ref, seg_ref, in_ref, a_ref, f_ref, gain_ref,
+    qkv_ref, att_ref, flat_ref, lse_ref, x_ref, normed_ref, a0, a1, f0, f1, gains,
+    buf, x_here, w_ref, gain_here, key_x, query_x, val_x, scores,
+    ag_sems, block_sems, a0_sems, a1_sems, f0_sems, f1_sems, swap, gain_sems, loads,
+):
+    at = spot()
+    y, x, c, h, p = at
+    far = far_role(at)
+    partner, above = (y, x, c, 1 - h, p), (1 - y, x, c, h, p)
+    size = f_ref.shape[1] // 4
+    a_pushes = [
+        ToHeads(at, layer, slices(a_ref, HS), columns(into), sems)
+        for layer, into, sems in ((0, a0, a0_sems), (1, a1, a1_sems))
+    ]
+    f_pushes = [
+        ToHeads(at, layer, slices(f_ref, size), columns(into), sems)
+        for layer, into, sems in ((0, f0, f0_sems), (1, f1, f1_sems))
+    ]
+    greet(at, *a_pushes, *f_pushes, peers=(above, partner))
+    swapped = remote(in_ref.at[1 - h], x_here, swap.at[0], swap.at[1], partner)
+    stays = pltpu.make_async_copy(in_ref.at[h], x_here, swap.at[2])
+
+    @pl.when(far == 1)
+    def _():
+        swapped.start()
+
+    @pl.when(far == 0)
+    def _():
+        stays.start()
+
+    across = remote(gain_ref, gains.at[y], gain_sems.at[0], gain_sems.at[1], above)
+    across.start()
+    keeps = pltpu.make_async_copy(gain_ref, gains.at[y], gain_sems.at[2])
+    keeps.start()
+    for push in a_pushes:
+        push.start()
+    keeps.wait()
+    across.wait_send()
+    remote(gain_ref, gains.at[1 - y], gain_sems.at[0], gain_sems.at[1], above).wait_recv()
+    gain_copy = pltpu.make_async_copy(gains.at[0], gain_here, loads.at[0])
+    gain_copy.start()
+
+    @pl.when(far == 1)
+    def _():
+        swapped.wait()
+
+    @pl.when(far == 0)
+    def _():
+        stays.wait()
+
+    gain_copy.wait()
+    save = pltpu.make_async_copy(x_here, x_ref, loads.at[1])
+    save.start()
+    buf[block_of(at)] = (unit_of(x_here[...].astype(F32))[0] * gain_here[0:1]).astype(LOW)
+
+    def ready():
+        a_pushes[0].finish()
+        copies = [pltpu.make_async_copy(a0.at[i], w_ref.at[pl.ds(i * HS, HS)], loads.at[2 + i]) for i in range(3)]
+        for copy in copies:
+            copy.start()
+        for push in f_pushes:
+            push.start()
+        for copy in copies:
+            copy.wait()
+
+    keep = (normed_ref, block_sems)
+    gather(at, buf, ag_sems, lambda b: project_block(b, buf, w_ref, cos_ref, sin_ref, None, qkv_ref), keep, ready)
+    attend_body(qkv_ref, seg_ref, att_ref, flat_ref, lse_ref, key_x, query_x, val_x, scores)
+    kept(buf, keep)
+    save.wait()
+    a_pushes[1].finish()
+    for push in f_pushes:
+        push.finish()
+
+
+def up_block(b, buf, f_ref, hidden_ref, one_ref, two_ref):
+    rows = span(b, buf.shape[1])
+    x = buf[b]
+    gate, up = dot(x, f_ref[0], NT), dot(x, f_ref[1], NT)
+    sigmoid = 1.0 / (1.0 + jnp.exp(-gate))
+    activated = gate * sigmoid
+    hidden_ref[rows] = (activated * up).astype(LOW)
+    one_ref[rows] = (up * sigmoid * (1.0 + gate * (1.0 - sigmoid))).astype(LOW)
+    two_ref[rows] = activated.astype(LOW)
+
+
+def middle_kernel(
+    att_ref, x_ref, wo_ref, f_ref, gain_mid_ref, gain_in_ref, w_ref, cos_ref, sin_ref, mix_ref,
+    middle_ref, out_ref, hidden_ref, one_ref, two_ref, qkv_ref, nmid_ref, normed_ref, home_ref,
+    buf, total, out_c, in_c, rin, ag_sems, rs_sems, block_sems, homing,
+):
+    at = spot()
+    rows = x_ref.shape[0]
+    push = ToHome(at, 0, out_ref, lambda m: home_ref.at[m], homing)
+    greet(at, push)
+    boxes = (out_c, in_c, rin)
+    scatter(at, total, boxes, rs_sems, lambda b: dot(att_ref[span(b, rows)], wo_ref[...]))
+    middle = x_ref[...].astype(F32) + total[...]
+    middle_ref[...] = middle
+    buf[block_of(at)] = (unit_of(middle)[0] * gain_mid_ref[...]).astype(LOW)
+    keep = (nmid_ref, block_sems)
+    gather(at, buf, ag_sems, lambda b: up_block(b, buf, f_ref, hidden_ref, one_ref, two_ref), keep)
+    scatter(
+        at, total, boxes, rs_sems, lambda b: dot(hidden_ref[span(b, rows)], f_ref[2]), lambda: kept(buf, keep)
+    )
+    out = (middle_ref[...] + total[...]).astype(LOW)
+    out_ref[...] = out
+    push.start()
+    buf[block_of(at)] = (unit_of(out.astype(F32))[0] * gain_in_ref[...]).astype(LOW)
+    keep = (normed_ref, block_sems)
+    gather(at, buf, ag_sems, lambda b: project_block(b, buf, w_ref, cos_ref, sin_ref, mix_ref, qkv_ref), keep)
+    kept(buf, keep)
+    push.finish()
+
+
+def down_back(
+    at, top, buf, nmid, total, boxes, ag_sems, rs_sems, f_ref, hidden_ref, one_ref, two_ref, wo_ref, att_ref,
+    gain_ref, middle_ref, sums_ref, out_sum_ref,
+    dmid_ref, gain_grad_ref, dout_ref, f_grad_ref, out_grad_ref,
+):
+    rows = buf.shape[1]
+    buf[block_of(at)] = top.astype(LOW)
+    sums_ref[...] = jnp.zeros_like(sums_ref)
+    out_sum_ref[...] = jnp.zeros_like(out_sum_ref)
+
+    def hidden_back(b):
+        here = span(b, rows)
+        grad = dot(buf[b], f_ref[2], NT)
+        one_ref[here] = (grad * one_ref[here].astype(F32)).astype(LOW)
+        two_ref[here] = (grad * two_ref[here].astype(F32)).astype(LOW)
+        sums_ref[2] += dot(hidden_ref[here], buf[b], TN)
+
+    gather(at, buf, ag_sems, hidden_back)
+
+    def partial(b):
+        here = span(b, rows)
+        return dot(one_ref[here], f_ref[0]) + dot(two_ref[here], f_ref[1])
+
+    scatter(at, total, boxes, rs_sems, partial)
+    grad, gain_grad = back_of(total[...], middle_ref[...], gain_ref[...])
+    gain_grad_ref[...] = gain_grad
+    grad = grad + top
+    dmid_ref[...] = grad
+    buf[block_of(at)] = grad.astype(LOW)
+
+    def out_back(b):
+        here = span(b, rows)
+        dout_ref[:, here] = dot(wo_ref[...], buf[b], NT).astype(LOW)
+        out_sum_ref[...] += dot(att_ref[here], buf[b], TN)
+        sums_ref[0] += dot(one_ref[here], nmid[b], TN)
+        sums_ref[1] += dot(two_ref[here], nmid[b], TN)
+
+    gather(at, buf, ag_sems, out_back)
+    f_grad_ref[...] = sums_ref[...].astype(LOW)
+    out_grad_ref[...] = out_sum_ref[...].astype(LOW)
+
+
+def turn_kernel(
+    att_ref, x_ref, wo_ref, f_ref, gain_ref, top_ref,
+    dmid_ref, gain_grad_ref, dout_ref, f_grad_ref, out_grad_ref, home_ref,
+    buf, nmid, out_ref, total, out_c, in_c, rin, middle_ref, hidden_ref, one_ref, two_ref, sums_ref,
+    out_sum_ref, ag_sems, rs_sems, homing,
+):
+    at = spot()
+    rows = x_ref.shape[0]
+    push = ToHome(at, 1, out_ref, lambda m: home_ref.at[m], homing)
+    greet(at, push)
+    boxes = (out_c, in_c, rin)
+    scatter(at, total, boxes, rs_sems, lambda b: dot(att_ref[span(b, rows)], wo_ref[...]))
+    middle = x_ref[...].astype(F32) + total[...]
+    middle_ref[...] = middle
+    nmid[block_of(at)] = (unit_of(middle)[0] * gain_ref[...]).astype(LOW)
+    gather(at, nmid, ag_sems, lambda b: up_block(b, nmid, f_ref, hidden_ref, one_ref, two_ref))
+    scatter(at, total, boxes, rs_sems, lambda b: dot(hidden_ref[span(b, rows)], f_ref[2]))
+    out_ref[...] = (middle_ref[...] + total[...]).astype(LOW)
+    push.start()
+    down_back(
+        at, top_ref[...].astype(F32), buf, nmid, total, boxes, ag_sems, rs_sems, f_ref, hidden_ref, one_ref, two_ref,
+        wo_ref, att_ref, gain_ref, middle_ref, sums_ref, out_sum_ref,
+        dmid_ref, gain_grad_ref, dout_ref, f_grad_ref, out_grad_ref,
+    )
+    push.finish()
+
+
+def input_back(
+    at, dqkv_ref, w_ref, x_ref, gain_ref, dmid_ref, gain_grad_ref, total, boxes, rs_sems, normed, load, sum_ref, after=None
+):
+    rows = total.shape[0]
+
+    def weight_sum():
+        load.wait()
+        sum_ref[...] = jnp.zeros_like(sum_ref)
+
+        def one(b, none):
+            sum_ref[...] += dot(dqkv_ref[:, span(b, rows)], normed[b])
+            return none
+
+        lax.fori_loop(0, 16, one, 0)
+        if after is not None:
+            after()
+
+    scatter(
+        at, total, boxes, rs_sems, lambda b: dot(dqkv_ref[:, span(b, rows)], w_ref[...], TN), weight_sum
+    )
+    grad, gain_grad = back_of(total[...], x_ref[...].astype(F32), gain_ref[...])
+    gain_grad_ref[...] = gain_grad
+    return grad + dmid_ref[...]
+
+
+def lower_kernel(
+    dqkv_ref, x_ref, w_ref, gain_in_ref, dmid_above_ref, f_ref, wo_ref, att_ref, gain_mid_ref, middle_ref,
+    hidden_far, one_far, two_far, normed_far, nmid_far,
+    gain_in_grad_ref, a_grad_ref, dmid_ref, gain_mid_grad_ref, dout_ref, f_grad_ref, out_grad_ref, home_ref,
+    buf, nmid, grad_ref, low_ref, total, out_c, in_c, rin, hidden_ref, one_ref, two_ref, sums_ref, out_sum_ref,
+    in_sum_ref, ag_sems, rs_sems, loads, homing,
+):
+    at = spot()
+    push = ToHome(at, 1, low_ref, lambda m: home_ref.at[m], homing)
+    copies = [
+        pltpu.make_async_copy(far, near, loads.at[i])
+        for i, (far, near) in enumerate(
+            (
+                (normed_far, buf),
+                (hidden_far, hidden_ref),
+                (one_far, one_ref),
+                (two_far, two_ref),
+                (nmid_far, nmid),
+            )
+        )
+    ]
+    for copy in copies:
+        copy.start()
+    greet(at, push)
+    boxes = (out_c, in_c, rin)
+    grad = input_back(
+        at, dqkv_ref, w_ref, x_ref, gain_in_ref, dmid_above_ref, gain_in_grad_ref, total, boxes, rs_sems, buf,
+        copies[0], in_sum_ref,
+    )
+    grad_ref[...] = grad
+    low_ref[...] = grad.astype(LOW)
+    push.start()
+    a_grad_ref[...] = in_sum_ref[...].astype(LOW)
+    for copy in copies[1:]:
+        copy.wait()
+    down_back(
+        at, grad_ref[...], buf, nmid, total, boxes, ag_sems, rs_sems, f_ref, hidden_ref, one_ref, two_ref, wo_ref,
+        att_ref, gain_mid_ref, middle_ref, sums_ref, out_sum_ref,
+        dmid_ref, gain_mid_grad_ref, dout_ref, f_grad_ref, out_grad_ref,
+    )
+    push.finish()
+
+
+def last_kernel(
+    dqkv_ref, x_ref, w_ref, gain_ref, dmid_ref, out_grad_ref, gains_ref, normed_far,
+    home_ref, a_in, gain_sum,
+    buf, total, out_c, in_c, rin, in_sum_ref, a_grad_ref, low_ref, gain_grad_ref, heard, rs_sems, loads, homing,
+    a_sems, gain_sems,
+):
+    at = spot()
+    y, x, c, h, p = at
+    copy = pltpu.make_async_copy(normed_far, buf, loads.at[0])
+    copy.start()
+    wide = a_grad_ref.shape[-1] // 4
+    shards = ToShards(
+        at, 0, lambda k: a_grad_ref.at[:, :, pl.ds(k * wide, wide)], lambda role, j: a_in.at[role, j], a_sems
+    )
+    push = ToHome(at, 0, low_ref, lambda m: home_ref.at[m], homing)
+    peers = [moved(at, 0, 1), moved(at, 1), moved(at, 2), moved(at, 4), (y, x, c, 1 - h, p)]
+    greet(at, push, shards, peers=peers[4:])
+    boxes = (out_c, in_c, rin)
+
+    def after():
+        for i in range(3):
+            a_grad_ref[i] = in_sum_ref[i * HS : (i + 1) * HS].astype(LOW)
+        a_grad_ref[3] = out_grad_ref[...]
+        shards.start()
+
+    grad = input_back(
+        at, dqkv_ref, w_ref, x_ref, gain_ref, dmid_ref, gain_grad_ref, total, boxes, rs_sems, buf, copy, in_sum_ref,
+        after,
+    )
+    low_ref[...] = grad.astype(LOW)
+    push.start()
+    gain_sum[0, 0:1] = gain_grad_ref[...]
+    gain_sum[0, 1:4] = gains_ref[...]
+    for i, peer in enumerate(peers):
+        copy = remote(gain_sum.at[i], heard.at[i], gain_sems.at[0, i], gain_sems.at[1, i], peer)
+        copy.start()
+        copy.wait()
+        gain_sum[i + 1] = gain_sum[i] + heard[i]
+    shards.finish()
+    push.finish()
+
+
+VMEM_SPEC = pl.BlockSpec(memory_space=pltpu.VMEM)
+ANY_SPEC = pl.BlockSpec(memory_space=pl.ANY)
+
+
+def links():
+    dma = pltpu.SemaphoreType.DMA
+    return (dma((3, 8)), dma((3, 8)), dma((8,)), dma((8,)))
+
+
+def sum_boxes(rows, width):
+    return [
+        pltpu.VMEM((rows, width), F32),
+        pltpu.VMEM((8, rows, width), LOW),
+        pltpu.VMEM((8, rows, width), LOW),
+        pltpu.VMEM((7, rows, width), LOW),
+    ]
+
+
+def reach(kernel, number, args, outs, scratch, name, far=()):
+    return pl.pallas_call(
+        kernel,
+        out_shape=[jax.ShapeDtypeStruct(shape, dtype) for shape, dtype, _ in outs],
+        in_specs=[VMEM_SPEC] * len(args) + [ANY_SPEC] * len(far),
+        out_specs=[ANY_SPEC if stays else VMEM_SPEC for _, _, stays in outs],
+        scratch_shapes=scratch,
+        compiler_params=pltpu.CompilerParams(
+            collective_id=number, has_side_effects=number is not None, vmem_limit_bytes=VMEM_BYTES
+        ),
+        name=name,
+    )(*args, *far)
+
+
+TILE = 512
+MORE = 16
+DOC_ROOM = 13
+FLOOR = -1e20
+
+
+def one_hot(seg_ref, part):
+    rows = lax.broadcasted_iota(jnp.int32, (MORE, TILE), 0)
+    return (rows, rows == seg_ref[:, part])
+
+
+def tiles(length):
+    return [slice(i * TILE, (i + 1) * TILE) for i in range(length // TILE)]
+
+
+def causal():
+    return lax.broadcasted_iota(jnp.int32, (TILE, 1), 0) <= lax.broadcasted_iota(jnp.int32, (1, TILE), 1)
+
+
+def attend_body(qkv_ref, seg_ref, att_ref, flat_ref, lse_ref, key_x, query_x, val_x, scores):
+    length = qkv_ref.shape[1]
+    for part in tiles(length):
+        rows, hot = one_hot(seg_ref, part)
+        key = jnp.concatenate([qkv_ref[HS : 2 * HS, part].astype(F32), jnp.where(hot, 1.0, 0.0)])
+        key_x[part] = key.T.astype(LOW)
+        query_x[:HS, part] = qkv_ref[:HS, part]
+        query_x[HS:, part] = jnp.where(hot | (rows >= DOC_ROOM), 0.0, NEGATIVE).astype(LOW)
+        val_x[:HS, part] = qkv_ref[2 * HS :, part]
+        val_x[HS:, part] = jnp.where(rows == 0, 1.0, 0.0).astype(LOW)
+
+    def query_tile(qi):
+        cols = slice(qi * TILE, (qi + 1) * TILE)
+        query = query_x[:, cols]
+
+        def ahead(slot, kb):
+            scores[slot] = dot(key_x[span(kb, TILE)], query)
+
+        def update(slot, kb, state, diagonal=False):
+            largest, summed = state
+            found = scores[slot]
+            if diagonal:
+                found = jnp.where(causal(), found, NEGATIVE)
+            newest = jnp.maximum(largest, jnp.max(found, axis=0, keepdims=True))
+            weights = jnp.exp(found - newest).astype(LOW)
+            summed = summed * jnp.exp(largest - newest) + dot(val_x[:, span(kb, TILE)], weights)
+            return (newest, summed)
+
+        def pair(i, state):
+            ahead(1, 2 * i + 1)
+            state = update(0, 2 * i, state)
+            ahead(0, 2 * i + 2)
+            return update(1, 2 * i + 1, state)
+
+        state = (jnp.full((1, TILE), FLOOR, F32), jnp.zeros((HS + MORE, TILE), F32))
+        ahead(0, 0)
+        state = lax.fori_loop(0, qi // 2, pair, state)
+        if qi % 2:
+            ahead(1, qi)
+            state = update(0, qi - 1, state)
+        largest, summed = update(qi % 2, qi, state, True)
+        totals = summed[HS : HS + 1]
+        attended = summed[:HS] / totals
+        att_ref[:, cols] = attended
+        flat_ref[cols] = attended.T.astype(LOW)
+        lse_ref[:, cols] = largest + jnp.log(totals)
+
+    for qi in range(length // TILE):
+        query_tile(qi)
+
+
+def attend_scratch(length):
+    return [
+        pltpu.VMEM((length, HS + MORE), LOW),
+        pltpu.VMEM((HS + MORE, length), LOW),
+        pltpu.VMEM((HS + MORE, length), LOW),
+        pltpu.VMEM((2, TILE, TILE), F32),
+    ]
+
+
+def three(values):
+    high = values.astype(LOW).astype(F32)
+    mid = (values - high).astype(LOW).astype(F32)
+    return (high, mid, values - high - mid)
+
+
+def attend_back_body(
+    qkv_ref, seg_ref, att_ref, lse_ref, dout_ref, cos_ref, sin_ref, extra_ref, dqkv_ref, send_ref,
+    key_x, val_x, query_x, dout_x, dq, scores, along,
+):
+    length = qkv_ref.shape[1]
+    half, count = HS // 2, length // TILE
+    for part in tiles(length):
+        rows, hot = one_hot(seg_ref, part)
+        ones = jnp.where(rows >= DOC_ROOM, 1.0, 0.0)
+        key = jnp.concatenate([qkv_ref[HS : 2 * HS, part].astype(F32), jnp.where(hot, 1.0, ones)])
+        key_x[part] = key.T.astype(LOW)
+        val_x[part] = jnp.concatenate([qkv_ref[2 * HS :, part].astype(F32), ones]).T.astype(LOW)
+
+        def tail(values, rest, rows=rows):
+            for i, piece in enumerate(three(values)):
+                rest = jnp.where(rows == DOC_ROOM + i, piece, rest)
+            return rest.astype(LOW)
+
+        dout = dout_ref[:, part]
+        delta = jnp.sum(dout.astype(F32) * att_ref[:, part], axis=0, keepdims=True)
+        query_x[:HS, part] = qkv_ref[:HS, part]
+        query_x[HS:, part] = tail(-lse_ref[:, part], jnp.where(hot, 0.0, NEGATIVE))
+        dout_x[:HS, part] = dout
+        dout_x[HS:, part] = tail(-delta, jnp.zeros((MORE, TILE), F32))
+    dq[...] = jnp.zeros_like(dq)
+
+    def key_tile(ki):
+        here = slice(ki * TILE, (ki + 1) * TILE)
+        rest = count - 1 - ki
+
+        def ahead(slot, qb):
+            cols = span(qb, TILE)
+            scores[slot] = dot(key_x[here], query_x[:, cols])
+            along[slot] = dot(val_x[here], dout_x[:, cols])
+
+        def update(slot, qb, state, diagonal=False):
+            dk, dv = state
+            cols = span(qb, TILE)
+            weights = jnp.exp(scores[slot])
+            if diagonal:
+                weights = jnp.where(causal(), weights, 0.0)
+            ds = (weights * along[slot]).astype(LOW)
+            dv = dv + dot(dout_x[:HS, cols], weights.astype(LOW), NT)
+            dk = dk + dot(query_x[:HS, cols], ds, NT)
+            dq[:, cols] += dot(qkv_ref[HS : 2 * HS, here], ds)
+            return (dk, dv)
+
+        def pair(i, state):
+            qb = ki + 1 + 2 * i
+            ahead(0, qb + 1)
+            state = update(1, qb, state)
+            ahead(1, qb + 2)
+            return update(0, qb + 1, state)
+
+        zero = jnp.zeros((HS, TILE), F32)
+        ahead(0, ki)
+        if rest:
+            ahead(1, ki + 1)
+        state = update(0, ki, (zero, zero), True)
+        state = lax.fori_loop(0, max(0, (rest - 1) // 2), pair, state)
+        if rest % 2:
+            state = update(1, count - 1, state)
+        elif rest:
+            ahead(0, count - 1)
+            state = update(1, count - 2, state)
+            state = update(0, count - 1, state)
+        dk, dv = state
+        a, b = turned(dk[:half], dk[half:], cos_ref[:, here], -sin_ref[:, here])
+        dqkv_ref[HS : HS + half, here] = a.astype(LOW)
+        dqkv_ref[HS + half : 2 * HS, here] = b.astype(LOW)
+        if send_ref is None:
+            dqkv_ref[2 * HS :, here] = (dv + extra_ref[:, here]).astype(LOW)
+        else:
+            dqkv_ref[2 * HS :, here] = (0.5 * dv).astype(LOW)
+            send_ref[:, here] = 0.5 * dv
+
+    for ki in range(count):
+        key_tile(ki)
+    scale = HS**-0.5
+    a, b = turned(dq[:half] * scale, dq[half:] * scale, cos_ref[...], -sin_ref[...])
+    dqkv_ref[:half] = a.astype(LOW)
+    dqkv_ref[half:HS] = b.astype(LOW)
+
+
+def attend_back_scratch(length):
+    wide = HS + MORE
+    return [
+        pltpu.VMEM((length, wide), LOW),
+        pltpu.VMEM((length, wide), LOW),
+        pltpu.VMEM((wide, length), LOW),
+        pltpu.VMEM((wide, length), LOW),
+        pltpu.VMEM((HS, length), F32),
+        pltpu.VMEM((2, TILE, TILE), F32),
+        pltpu.VMEM((2, TILE, TILE), F32),
+    ]
+
+
+def attend_back_upper(
+    qkv_ref, seg_ref, att_ref, lse_ref, dout_ref, cos_ref, sin_ref, f_grad, dqkv_ref, send_ref, f_in, *rest
+):
+    *scratch, sems = rest
+    at = spot()
+    wide = f_grad.shape[-1] // 4
+    push = ToShards(
+        at, 1, lambda k: f_grad.at[:, :, pl.ds(k * wide, wide)], lambda role, j: f_in.at[role, j], sems
+    )
+    count = push.greet()
+    pl.semaphore_wait(pltpu.get_barrier_semaphore(), count)
+    push.start()
+    attend_back_body(
+        qkv_ref, seg_ref, att_ref, lse_ref, dout_ref, cos_ref, sin_ref, None, dqkv_ref, send_ref, *scratch
+    )
+    push.finish()
+
+
+def attend_back_lower(
+    qkv_ref, seg_ref, att_ref, lse_ref, dout_ref, cos_ref, sin_ref, extra_ref, f_grad, a_grad,
+    dqkv_ref, f_in, a_in, *rest,
+):
+    *scratch, f_sems, a_sems = rest
+    at = spot()
+    wide = f_grad.shape[-1] // 4
+    pushes = [
+        ToShards(
+            at,
+            layer,
+            lambda k, ref=ref: ref.at[:, :, pl.ds(k * wide, wide)],
+            lambda role, j, into=into: into.at[role, j],
+            sems,
+        )
+        for layer, ref, into, sems in ((0, f_grad, f_in, f_sems), (1, a_grad, a_in, a_sems))
+    ]
+    count = pushes[0].greet() + pushes[1].greet()
+    pl.semaphore_wait(pltpu.get_barrier_semaphore(), count)
+    for push in pushes:
+        push.start()
+    attend_back_body(
+        qkv_ref, seg_ref, att_ref, lse_ref, dout_ref, cos_ref, sin_ref, extra_ref, dqkv_ref, None, *scratch
+    )
+    for push in pushes:
+        push.finish()
+
+
+def number_of(y, s, z):
+    return (y * 4 + s) * 4 + z
+
+
+def far_pairs():
+    return [
+        (number_of(y, s, z), number_of(y, s, (z + 2) % 4))
+        for y in range(2)
+        for s in range(4)
+        for z in range(4)
+        if (y + s) % 2
+    ]
+
+
+AXES = ("section", "seq", "tensor")
+
+
+def on_grid(
+    inputs, cotangent, lengths, w_query, w_key, w_value, w_out, w_gate, w_up, w_down, attn_gain, mlp_gain
+):
+    at = spot()
+    y, x, c, half, p = at
+    far = far_role(at) == 1
+    rows, width = inputs.shape[1:]
+    length = 16 * rows
+    units = w_gate.shape[2] // 4
+    length_row = lax.dynamic_index_in_dim(lengths, half, 0, keepdims=False)
+    places = jnp.arange(length, dtype=jnp.int32)
+    segment, within = doc_table(length_row, places)
+    segment = segment[None]
+    frequency = jnp.exp(jnp.arange(HS // 2, dtype=F32) * (-math.log(10000.0) / (HS // 2)))
+    angles = within.astype(F32)[None, :] * frequency[:, None]
+    tables = [jnp.cos(angles), jnp.sin(angles)]
+    a_own = jnp.stack([w_query[0].T, w_key[0].T, w_value[0].T, w_out[0]])
+    f_own = jnp.stack([w_gate[0].T, w_up[0].T, w_down[0]])
+    buf = [pltpu.VMEM((16, rows, width), LOW)]
+    boxes = sum_boxes(rows, width)
+    dma = pltpu.SemaphoreType.DMA
+    every = ((16, rows, width), LOW, True)
+    turned_out = ((3 * HS, length), LOW, False)
+    hidden_out = ((length, units), LOW, False)
+    block_out = ((rows, width), F32, False)
+    low_out = ((rows, width), LOW, False)
+    gain_out = ((1, width), F32, False)
+    dout_out = ((HS, length), LOW, False)
+    head_out = ((HS, length), F32, False)
+    flat_out = ((length, HS), LOW, False)
+    lse_out = ((1, length), F32, False)
+    f_out = ((3, units, width), LOW, False)
+    wo_out = ((HS, width), LOW, False)
+    f_far = ((3, units, width), LOW, True)
+    a_far = ((4, HS, width), LOW, True)
+    a_shards = ((2, 4, 4, HS, width // 4), LOW, True)
+    f_shards = ((2, 4, 3, units, width // 4), LOW, True)
+    hidden_scratch = pltpu.VMEM((length, units), LOW)
+    f_sum = [pltpu.VMEM((3, units, width), F32), pltpu.VMEM((HS, width), F32)]
+    in_sum = [pltpu.VMEM((3 * HS, width), F32)]
+
+    home_out = ((2, rows, width), LOW, True)
+    qkv0, att0, flat0, lse0, own_in, normed0, a0, a1, f0, f1, gains = reach(
+        first_kernel,
+        0,
+        [*tables, segment],
+        [turned_out, head_out, flat_out, lse_out, ((rows, width), LOW, True), every, a_far, a_far, f_far, f_far]
+        + [((2, 2, width), F32, True)],
+        buf
+        + [pltpu.VMEM((rows, width), LOW), pltpu.VMEM((3 * HS, width), LOW), pltpu.VMEM((2, width), F32)]
+        + attend_scratch(length)
+        + [links(), dma((16,)), head_sems(), head_sems(), head_sems(), head_sems(), dma((3,)), dma((3,)), dma((5,))],
+        "first",
+        [inputs, a_own, f_own, jnp.concatenate([attn_gain, mlp_gain])],
+    )
+    both = lax.dynamic_index_in_dim(cotangent, 1 - half, 0, keepdims=False)
+    own_top = jnp.where(
+        far,
+        lax.ppermute(both, AXES, far_pairs()),
+        lax.dynamic_index_in_dim(cotangent, half, 0, keepdims=False),
+    )
+    gain_in, gain_mid = [gains[i, 0:1] for i in range(2)], [gains[i, 1:2] for i in range(2)]
+    w_in = [a[:3].reshape(3 * HS, width) for a in (a0, a1)]
+    w_back = [a[3] for a in (a0, a1)]
+
+    mid0, out0, hid0, one0, two0, qkv1, nmid0, normed1, home_out0 = reach(
+        middle_kernel,
+        2,
+        [flat0, own_in, w_back[0], f0, gain_mid[0], gain_in[1], w_in[1], *tables, qkv0[2 * HS :]],
+        [block_out, low_out, hidden_out, hidden_out, hidden_out, turned_out, every, every, home_out],
+        buf + boxes + [links(), links(), dma((16,)), home_sems()],
+        "middle",
+    )
+    att1, flat1, lse1 = reach(
+        attend_body, None, [qkv1, segment], [head_out, flat_out, lse_out], attend_scratch(length), "attend"
+    )
+    dmid1, gmid1, dout1, f_grad1, wo_grad1, home_out1 = reach(
+        turn_kernel,
+        3,
+        [flat1, out0, w_back[1], f1, gain_mid[1], own_top],
+        [block_out, gain_out, dout_out, f_out, wo_out, home_out],
+        buf
+        + buf
+        + [pltpu.VMEM((rows, width), LOW)]
+        + boxes
+        + [pltpu.VMEM((rows, width), F32)]
+        + [hidden_scratch] * 3
+        + f_sum
+        + [links(), links(), home_sems()],
+        "turn",
+    )
+    dqkv1, extra, f_in1 = reach(
+        attend_back_upper,
+        9,
+        [qkv1, segment, att1, lse1, dout1, *tables],
+        [turned_out, head_out, f_shards],
+        attend_back_scratch(length) + [shard_sems()],
+        "attend_back",
+        [f_grad1],
+    )
+    gin1, in_grad1, dmid0, gmid0, dout0, f_grad0, wo_grad0, home_grad1 = reach(
+        lower_kernel,
+        4,
+        [dqkv1, out0, w_in[1], gain_in[1], dmid1, f0, w_back[0], flat0, gain_mid[0], mid0],
+        [gain_out, ((3 * HS, width), LOW, False), block_out, gain_out, dout_out, f_out, wo_out, home_out],
+        buf
+        + buf
+        + [pltpu.VMEM((rows, width), F32), pltpu.VMEM((rows, width), LOW)]
+        + boxes
+        + [hidden_scratch] * 3
+        + f_sum
+        + in_sum
+        + [links(), links(), dma((5,)), home_sems()],
+        "lower",
+        [hid0, one0, two0, normed1, nmid0],
+    )
+    a_grad1 = jnp.concatenate([in_grad1, wo_grad1]).reshape(4, HS, width)
+    dqkv0, f_in0, a_in1 = reach(
+        attend_back_lower,
+        10,
+        [qkv0, segment, att0, lse0, dout0, *tables, extra],
+        [turned_out, f_shards, a_shards],
+        attend_back_scratch(length) + [shard_sems(), shard_sems()],
+        "attend_back",
+        [f_grad0, a_grad1],
+    )
+    home_grad0, a_in0, gain_sums = reach(
+        last_kernel,
+        5,
+        [dqkv0, own_in, w_in[0], gain_in[0], dmid0, wo_grad0, jnp.concatenate([gin1, gmid0, gmid1])],
+        [home_out, a_shards, ((6, 4, width), F32, False)],
+        buf
+        + boxes
+        + in_sum
+        + [pltpu.VMEM((4, HS, width), LOW), pltpu.VMEM((rows, width), LOW), pltpu.VMEM((1, width), F32)]
+        + [pltpu.VMEM((5, 4, width), F32)]
+        + [links(), dma((1,)), home_sems(), shard_sems(), dma((2, 5))],
+        "last",
+        [normed0],
+    )
+    on_first = y == 0
+    a_sum = jnp.sum(jnp.where(on_first, a_in0, a_in1).astype(F32), axis=0)
+    f_total = jnp.sum(jnp.where(on_first, f_in0, f_in1).astype(F32), axis=0)
+    a_sum = jnp.transpose(a_sum, (1, 0, 2, 3)).reshape(4, 4 * HS, width // 4)
+    f_total = jnp.transpose(f_total, (1, 0, 2, 3)).reshape(3, 4 * units, width // 4)
+    layer_out = jnp.where(on_first, home_out0, home_out1)
+    input_grad = jnp.where(on_first, home_grad0, home_grad1).astype(F32)
+    share = width // 16
+    first_col = (4 * (2 * x + c) + 2 * half + p) * share
+    gain_share = lax.dynamic_slice_in_dim(gain_sums[5], first_col, share, 1)
+    gain_in_share = jnp.where(on_first, gain_share[0:1], gain_share[1:2])
+    gain_mid_share = jnp.where(on_first, gain_share[2:3], gain_share[3:4])
+    return (
+        layer_out[None],
+        input_grad[None],
+        a_sum[0].T[None],
+        a_sum[1].T[None],
+        a_sum[2].T[None],
+        a_sum[3][None],
+        f_total[0].T[None],
+        f_total[1].T[None],
+        f_total[2][None],
+        gain_in_share,
+        gain_mid_share,
+    )
+
+
 def solution(mesh):
     in_specs = (
         P(None, ("seq", "tensor"), None),
@@ -503,6 +1764,7 @@
         P("section", ("seq", "tensor")),
         P("section", ("seq", "tensor")),
     )
+    grid = (mesh.shape["section"], mesh.shape["seq"], mesh.shape["tensor"]) == (2, 4, 4)
     return jax.shard_map(
-        on_device, mesh=mesh, in_specs=in_specs, out_specs=out_specs, check_vma=False
-    )
+        on_grid if grid else on_device, mesh=mesh, in_specs=in_specs, out_specs=out_specs, check_vma=False
+    )

time: 3440 us -> 825 us (0.24)
  waiting for transfers between devices: 1610 us -> 0.01 us
  matrix products: 1090 us -> 0 us
  Pallas kernels: 0 us -> 782 us
  other arithmetic: 357 us -> 16.5 us
  local copies, waits for them, and re-layouts: 258 us -> 13.5 us
  blocking collectives: 63.1 us -> 0 us
    dot_general x180 -> x0, matrix products: 1090 us -> none  [the longest x24 143 us: block_scores(): jnp.einsum('qhd,khd->hqk', query_heads, block_keys, preferred_element_typ...]
    pallas_call x0 -> x8, Pallas kernels: none -> 782 us  [reach(): pl.pallas_call(kernel, out_shape=[jax.ShapeDtypeStruct(shape, dtype) for...]
    all_gather x33 -> x0, waiting for transfers between devices: 768 us -> none  [the longest x18 623 us: spread(): return lax.all_gather(values, 'tensor', axis=0, tiled=True)]
    reduce_scatter x28 -> x0, waiting for transfers between devices: 739 us -> none  [the longest x15 485 us: fold_rows(): lax.psum_scatter(values.astype(jnp.bfloat16), 'tensor', scatter_dimension...]
    reduce_sum x29 -> x2, other arithmetic: 189 us -> 4.26 us  [the longest x1 2.52 us: on_grid(): f_total = jnp.sum(jnp.where(on_first, f_in0, f_in1).astype(F32), axis=0)]
    ppermute x4 -> x1, waiting for transfers between devices: 93 us -> 0.01 us  [on_grid(): lax.ppermute(both, AXES, far_pairs())]
    and x25 -> x0, other arithmetic: 59.6 us -> none  [allowed_mask(): (key_places[None, :] <= places[:, None]) & (key_segment[None, :] == segme...]
    unnamed x520 -> x30, local copies, waits for them, and re-layouts: 65.3 us -> 6.62 us
  transfers between devices with their start and end apart: 65 -> 1, of which waited for: 54 -> 0; matrix products, arithmetic and copies ran while one was open for 31% -> 2% of each run, Pallas kernels for 0% -> 35%
where the time goes in v2:
time: 825 us; the launch traced here: 814 us
  Pallas kernels  782 us (95%)
  other arithmetic  16.5 us (2%)
  local copies, waits for them, and re-layouts  13.5 us (2%)
    pallas_call x8, Pallas kernels, reach(): pl.pallas_call(kernel, out_shape=[jax.ShapeDtypeStruct(shape, dtype) for...  782 us
  transfers between devices with their start and end apart: 1, of which 0 were waited for; matrix products, arithmetic and copies ran while one was open for 2% of the time, Pallas kernels for 35%

profile of v2, /device:TPU:0, one launch (start us, length us, event | category | flops | bytes accessed | tf_op | source)
XLA Modules:
  0.0 814.4 jit_solution(7438731291999779986)
XLA Ops:
  0.6 0.0 copy-start.8
  0.7 0.0 copy-start.9
  0.7 0.0 copy-start.10
  0.7 2.0 dynamic-slice_bitcast_fusion
  2.7 0.0 copy-start.11
  2.7 1.6 collective-permute-start
  4.3 0.7 fusion.3
  5.0 0.2 reduce-window.4
  5.1 0.7 fusion.2
  5.8 0.1 convert_reduce_fusion.2
  5.9 0.1 select_reduce_fusion
  6.1 1.0 copy.41
  7.1 1.0 copy.42
  8.1 1.0 copy.43
  9.1 0.7 pad_maximum_fusion.4.gain_ref
  9.8 2.8 multiply_sine_fusion
  12.6 0.0 copy-done.8
  12.6 0.0 copy-done.9
  12.6 0.0 copy-done.10
  12.6 1.1 pad_maximum_fusion.f_ref
  13.7 0.0 copy-done.11
  13.7 0.9 pad_maximum_fusion.1.a_ref
  14.6 121.1 %first.1 = (bf16[192,4096]{1,0:T(8,128)(2,1)}, f32[64,4096]{1,0:T(8,128)}, bf16[4096,64]{1,0:T(8,128)(2,1)}, f32[1,4096]{1,0:T(1,128)S(1)}, bf16[256,1024]{1,0:T...) custom-call(f32[32,4096]{1,0:T(8,128)} %get-tuple-element.144.cos_re, ...), custom_call_target="tpu_custom_call" | custom-call | tf_op jit(solution)/shard_map/first/pallas_call | solution.py:1314
  135.8 1.9 slice.82.mix_ref
  137.7 147.6 %middle.1 = (f32[256,1024]{1,0:T(8,128)}, bf16[256,1024]{1,0:T(8,128)(2,1)S(1)}, bf16[4096,176]{1,0:T(8,128)(2,1)}, bf16[4096,176]{1,0:T(8,128)(2,1)}, bf16[4096...) custom-call(bf16[4096,64]{1,0:T(8,128)(2,1)} %get-tuple-element.57.a, ...), custom_call_target="tpu_custom_call" | custom-call | tf_op jit(solution)/shard_map/middle/pallas_call | solution.py:1314
  285.3 0.0 copy-start.2
  285.3 14.7 %attend.1 = (f32[64,4096]{1,0:T(8,128)S(1)}, bf16[4096,64]{1,0:T(8,128)(2,1)}, f32[1,4096]{1,0:T(1,128)S(1)}) custom-call(bf16[192,4096]{1,0:T(8,128)(2,1)} %get-tuple-element.65.qkv_ref, s32[1,4096]{1,0:T(1,128)S(1)} %bitcast.96), custom_call_target="tpu_custom_call" | custom-call | tf_op jit(solution)/shard_map/attend/pallas_call | solution.py:1314
  300.1 0.0 copy-start.3
  300.1 1.0 copy-done.3
  301.0 0.0 copy-start
  301.1 0.0 copy-start.1
  301.1 0.0 collective-permute-done
  301.1 1.2 bitcast_select_fusion.top_ref
  302.3 210.0 %turn.1 = (f32[256,1024]{1,0:T(8,128)}, f32[1,1024]{1,0:T(1,128)S(1)}, bf16[64,4096]{1,0:T(8,128)(2,1)S(1)}, bf16[3,176,1024]{2,1,0:T(8,128)(2,1)}, bf16[64,1024...) custom-call(bf16[4096,64]{1,0:T(8,128)(2,1)} %get-tuple-element.66.att_ref, ...), custom_call_target="tpu_custom_call" | custom-call | tf_op jit(solution)/shard_map/turn/pallas_call | solution.py:1314
  512.2 0.0 copy-done.2
  512.2 0.0 copy-done
  512.3 0.0 copy-done.1
  512.3 29.9 %attend_back.2 = (bf16[192,4096]{1,0:T(8,128)(2,1)}, f32[64,4096]{1,0:T(8,128)}, bf16[2,4,3,176,256]{4,3,2,1,0:T(8,128)(2,1)}) custom-call(bf16[192,4096]{1,0:T(8,128)(2,1)} %get-tuple-element.65.qkv_ref, s32[1,4096]{1,0:T(1,128)S(1)} %bitcast.97, f32[64,4096]{1,0:T(8,128)} %copy-done.3, f32[1,4096]{1,0:T(1,128)S(1)} %get-tuple-element.73.lse_ref, ...), custom_call_target="tpu_custom_call" | custom-call | tf_op jit(solution)/shard_map/attend_back/pallas_call | solution.py:1314
  542.2 150.9 %lower.1 = (f32[1,1024]{1,0:T(1,128)S(1)}, bf16[192,1024]{1,0:T(8,128)(2,1)S(1)}, f32[256,1024]{1,0:T(8,128)}, f32[1,1024]{1,0:T(1,128)S(1)}, bf16[64,4096]{1,0:...) custom-call(bf16[192,4096]{1,0:T(8,128)(2,1)} %get-tuple-element.76.dq, ...), custom_call_target="tpu_custom_call" | custom-call | tf_op jit(solution)/shard_map/lower/pallas_call | solution.py:1314
  693.1 0.8 pad_maximum_fusion.2
  694.0 31.3 %attend_back.3 = (bf16[192,4096]{1,0:T(8,128)(2,1)}, bf16[2,4,3,176,256]{4,3,2,1,0:T(8,128)(2,1)}, bf16[2,4,4,64,256]{4,3,2,1,0:T(8,128)(2,1)}) custom-call(bf16[192,4096]{1,0:T(8,128)(2,1)} %get-tuple-element.63.qkv_ref, s32[1,4096]{1,0:T(1,128)S(1)} %bitcast.98, f32[64,4096]{1,0:T(8,128)} %get-tuple-element.70.att_ref, ...), custom_call_target="tpu_custom_call" | custom-call | tf_op jit(solution)/shard_map/attend_back/pallas_call | solution.py:1314
  725.3 0.0 copy-start.5
  725.3 76.1 %last.1 = (bf16[2,256,1024]{2,1,0:T(8,128)(2,1)}, bf16[2,4,4,64,256]{4,3,2,1,0:T(8,128)(2,1)}, f32[6,4,1024]{2,1,0:T(4,128)S(1)}) custom-call(bf16[192,4096]{1,0:T(8,128)(2,1)} %get-tuple-element.89.dqkv_ref, bf16[256,1024]{1,0:T(8,128)(2,1)S(1)} %get-tuple-element.58.x_ref, bf16[192,1024]{1,0:T(8,128)(2,1)S(1)} %bitcast.94, ...), custom_call_target="tpu_custom_call" | custom-call | tf_op jit(solution)/shard_map/last/pallas_call | solution.py:1314
  801.4 0.0 copy-done.5
  801.4 1.7 convert_reduce_fusion.1
  803.2 0.0 copy-start.4
  803.2 0.8 fusion.5
  803.9 0.8 copy.46
  804.8 0.1 copy-done.4
  804.9 2.5 convert_reduce_fusion
  807.4 0.0 copy-start.6
  807.4 0.0 copy-start.7
  807.4 1.4 fusion.4
  808.8 0.1 constant_dynamic-slice_fusion
  808.9 0.5 fusion.1
  809.4 0.8 copy.45
  810.2 0.8 copy.44
  811.1 0.0 copy-done.6
  811.1 0.0 copy-done.7
  811.1 3.1 bitcast_convert_fusion
  (9 shorter events, 0.1 us)
Async XLA Ops:
  0.6 12.0 %copy-start.8 = (bf16[1,704,256]{2,1,0:T(8,128)(2,1)S(1)}, bf16[1,704,256]{2,1,0:T(8,128)(2,1)}, u32[]{:S(2)}) copy-start(bf16[1,704,256]{2,1,0:T(8,128)(2,1)} %param.21) | copy-start | bytes 1081348
  0.7 12.0 %copy-start.9 = (bf16[1,256,704]{1,2,0:T(8,128)(2,1)S(1)}, bf16[1,256,704]{1,2,0:T(8,128)(2,1)}, u32[]{:S(2)}) copy-start(bf16[1,256,704]{1,2,0:T(8,128)(2,1)} %param.20) | copy-start | bytes 1081348
  0.7 12.0 %copy-start.10 = (bf16[1,256,704]{1,2,0:T(8,128)(2,1)S(1)}, bf16[1,256,704]{1,2,0:T(8,128)(2,1)}, u32[]{:S(2)}) copy-start(bf16[1,256,704]{1,2,0:T(8,128)(2,1)} %param.19) | copy-start | bytes 1081348
  2.7 11.1 %copy-start.11 = (bf16[1,256,256]{2,1,0:T(8,128)(2,1)S(1)}, bf16[1,256,256]{2,1,0:T(8,128)(2,1)}, u32[]{:S(2)}) copy-start(bf16[1,256,256]{2,1,0:T(8,128)(2,1)} %param.18) | copy-start | bytes 393220
  2.7 298.4 %collective-permute-start = (bf16[256,1024]{1,0:T(8,128)(2,1)}, bf16[256,1024]{1,0:T(8,128)(2,1)}, u32[]{:S(2)}, u32[]{:S(2)}) collective-permute-start(bf16[256,1024]{1,0:T(8,128)(2,1)} %dynamic-slice_bitcast_fusion), channel_id=1, source_target_pairs={{4,6},{5,7},{6,4},{7,5},{12,14},{13,15},{14,12},{15,13},{16,18},{1... | collective-permute-start | bytes 1572872 | tf_op jit(solution)/shard_map/ppermute | solution.py:1630
  285.3 226.9 %copy-start.2 = (bf16[256,1024]{1,0:T(8,128)(2,1)}, bf16[256,1024]{1,0:T(8,128)(2,1)S(1)}, u32[]{:S(2)}) copy-start(bf16[256,1024]{1,0:T(8,128)(2,1)S(1)} %get-tuple-element.67.x_ref) | copy-start | bytes 1572868
  300.1 1.0 copy-start.3
  301.0 211.2 %copy-start = (f32[32,4096]{1,0:T(8,128)S(1)}, f32[32,4096]{1,0:T(8,128)}, u32[]{:S(2)}) copy-start(f32[32,4096]{1,0:T(8,128)} %get-tuple-element.143.sin_ref) | copy-start | bytes 1572868
  301.1 211.2 %copy-start.1 = (f32[32,4096]{1,0:T(8,128)S(1)}, f32[32,4096]{1,0:T(8,128)}, u32[]{:S(2)}) copy-start(f32[32,4096]{1,0:T(8,128)} %get-tuple-element.144.cos_ref) | copy-start | bytes 1572868
  725.3 76.1 %copy-start.5 = (bf16[2,4,4,64,256]{4,3,2,1,0:T(8,128)(2,1)S(1)}, bf16[2,4,4,64,256]{4,3,2,1,0:T(8,128)(2,1)}, u32[]{:S(2)}) copy-start(bf16[2,4,4,64,256]{4,3,2,1,0:T(8,128)(2,1)} %get-tuple-element.99) | copy-start | bytes 3145732
  803.2 1.7 copy-start.4
  807.4 3.7 copy-start.6
  807.4 3.7 copy-start.7

commit v3 on v2

--- a/solution.py
+++ b/solution.py
@@ -486,7 +486,7 @@
 NT = (((1,), (1,)), ((), ()))
 NN = (((1,), (0,)), ((), ()))
 TN = (((0,), (0,)), ((), ()))
-VMEM_BYTES = 52 * 2**20
+VMEM_BYTES = 53 * 2**20
 
 
 def dot(left, right, dims=NN):
@@ -557,18 +557,30 @@
     )
 
 
+def others(at):
+    return [moved(at, mask, core) for mask in range(8) for core in range(2) if mask + core]
+
+
 def greet(at, *pushes, peers=()):
-    count = 4 + len(peers)
-    for mask, core in ((1, 0), (2, 0), (4, 0), (0, 1)):
-        signal(moved(at, mask, core))
-    for peer in peers:
+    met = others(at) + list(peers)
+    count = len(met)
+    for peer in met:
         signal(peer)
     for push in pushes:
         count = count + push.greet()
     pl.semaphore_wait(pltpu.get_barrier_semaphore(), count)
 
 
-def gather(at, buf, sems, on_block, keep=None, ready=None):
+def run(steps):
+    for _ in steps:
+        pass
+
+
+def gather(*args, **kwargs):
+    run(gathering(*args, **kwargs))
+
+
+def gathering(at, buf, sems, on_block=None, keep=None, ready=None):
     send, recv, csend, crecv = sems
     parts = parts_of(buf.shape[1])
 
@@ -589,11 +601,15 @@
         return remote(ref, ref, csend.at[mask], crecv.at[mask], moved(at, 0, 1))
 
     def visit(level, core):
+        if on_block is None and keep is None:
+            return
+
         def one(i, none):
             b = block_of(moved(at, level_mask(level, i), core))
             if keep is not None:
                 pltpu.make_async_copy(buf.at[b], keep[0].at[b], keep[1].at[b]).start()
-            on_block(b)
+            if on_block is not None:
+                on_block(b)
             return none
 
         lax.fori_loop(0, len(LEVELS[level]), one, 0)
@@ -608,6 +624,7 @@
     visit(0, 0)
     across(0, 1).wait_recv()
     visit(0, 1)
+    yield
     for k in range(3):
         first, second, third = ORDERS[k]
         arrival(k, first).wait_recv()
@@ -616,14 +633,17 @@
         first, second, third = ORDERS[k]
         hop(k, third).start()
         hop(k, first | third).start()
+    yield
     for k in range(3):
         first, second, third = ORDERS[k]
         arrival(k, second).wait_recv()
         hop(k, second | third).start()
+    yield
     for k in range(3):
         first, second, third = ORDERS[k]
         arrival(k, first | second).wait_recv()
         hop(k, 7).start()
+    yield
     for level in (1, 2, 3):
         for mask in LEVELS[level]:
             for k in range(3):
@@ -635,6 +655,7 @@
         for mask in LEVELS[level]:
             across(mask, 1).wait_recv()
         visit(level, 1)
+        yield
     for k in range(3):
         for target in range(1, 8):
             hop(k, target).wait_send()
@@ -647,7 +668,11 @@
         pltpu.make_async_copy(buf.at[b], keep[0].at[b], keep[1].at[b]).wait()
 
 
-def scatter(at, total, boxes, sems, partial, before_last=None):
+def scatter(*args, **kwargs):
+    run(scattering(*args, **kwargs))
+
+
+def scattering(at, total, boxes, sems, partial, before_last=None):
     out_c, in_c, rin = boxes
     send, recv, csend, crecv = sems
     parts = parts_of(total.shape[0])
@@ -663,12 +688,17 @@
         )
 
     def across(mask):
-        return remote(out_c.at[mask], in_c.at[mask], csend.at[mask], crecv.at[mask], moved(at, 0, 1))
+        slot = 0 if mask in (0, 7) else 1 + (LEVELS[1] + LEVELS[2]).index(mask) % 3
+        return remote(out_c.at[slot], in_c.at[mask], csend.at[mask], crecv.at[mask], moved(at, 0, 1))
 
     def emit(level):
+        if level < 2:
+            for mask in LEVELS[3 - level]:
+                across(mask).wait_send()
+
         def one(i, none):
-            mask = level_mask(level, i)
-            out_c[mask] = partial(block_of(moved(at, mask, 1))).astype(LOW)
+            slot = 1 + i if level in (1, 2) else 0
+            out_c[slot] = partial(block_of(moved(at, level_mask(level, i), 1))).astype(LOW)
             return none
 
         lax.fori_loop(0, len(LEVELS[level]), one, 0)
@@ -700,20 +730,24 @@
 
     emit(3)
     emit(2)
+    yield
     settle(3)
     settle(2)
     emit(1)
+    yield
     settle(1)
     if before_last is not None:
         before_last()
     emit(0)
     settle(0)
+    yield
     for mask_of in (lambda a, b: a | b, lambda a, b: b):
         for k in range(3):
             first, second, third = ORDERS[k]
             mask, rows = mask_of(first, second), pl.ds(*parts[k])
             in_c[mask, rows] = (in_c[mask, rows].astype(F32) + arrived(k, mask | third)).astype(LOW)
             hop(k, mask).start()
+        yield
     for k in range(3):
         first, second, third = ORDERS[k]
         rows = pl.ds(*parts[k])
@@ -721,6 +755,7 @@
             in_c[first, rows].astype(F32) + arrived(k, first | third) + arrived(k, first | second)
         ).astype(LOW)
         hop(k, first).start()
+    yield
     for k in range(3):
         first, second, third = ORDERS[k]
         rows = pl.ds(*parts[k])
@@ -728,8 +763,48 @@
     for k in range(3):
         for target in range(1, 8):
             hop(k, target).wait_send()
-    for mask in range(8):
+    for mask in LEVELS[0] + LEVELS[1]:
         across(mask).wait_send()
+
+
+class ToRows:
+    def __init__(self, at, block, place, sems):
+        self.at, self.block, self.place = at, block, place
+        self.send, self.recv, self.local = sems
+        self.mine = block_of(at)
+
+    def copy(self, b):
+        lane, (y, x, c, h, p) = b % 4, self.at
+        x, c = b // 8, (b // 4) % 2
+        home = (flip(flip(h, lane // 2), c), x, c, h, lane % 2)
+        return remote(self.block(b), self.place(self.mine), self.send.at[b], self.recv.at[self.mine], home)
+
+    def start(self, b):
+        @pl.when(same(b, self.mine) == 0)
+        def _():
+            self.copy(b).start()
+
+        @pl.when(same(b, self.mine) == 1)
+        def _():
+            pltpu.make_async_copy(self.block(b), self.place(b), self.local).start()
+
+    def finish(self):
+        for b in range(16):
+
+            @pl.when(same(b, self.mine) == 0)
+            def _(b=b):
+                dst = self.place(b)
+                remote(dst, dst, self.send.at[b], self.recv.at[b], self.at).wait_recv()
+                self.copy(b).wait_send()
+
+            @pl.when(same(b, self.mine) == 1)
+            def _(b=b):
+                pltpu.make_async_copy(self.block(b), self.place(b), self.local).wait()
+
+
+def row_sems():
+    dma = pltpu.SemaphoreType.DMA
+    return (dma((16,)), dma((16,)), dma)
 
 
 def same(a, b):
@@ -741,9 +816,9 @@
 
 
 class ToHeads:
-    def __init__(self, at, layer, piece, place, sems):
-        self.at, self.layer, self.piece, self.place = at, layer, piece, place
-        self.send, self.recv, self.local = sems
+    def __init__(self, at, layer, piece, place, relay, sems):
+        self.at, self.layer, self.piece, self.place, self.relay = at, layer, piece, place, relay
+        self.send, self.recv, self.local, self.relay_send, self.relay_recv = sems
         y, x, c, h, p = at
         self.s = 2 * x + c
         self.sends = same(y, layer)
@@ -753,41 +828,72 @@
         return self.sends * self.near * same(self.s, j)
 
     def greet(self):
-        half = flip(self.at[3], far_role(self.at))
+        y, x, c, h, p = self.at
+        source = self.near * self.layer + (1 - self.near) * y
         for k in range(4):
 
             @pl.when(self.is_me(k) == 0)
             def _(k=k):
-                signal((self.layer, k // 2, k % 2, half, self.at[4]))
-
-        return self.sends * (8 - self.near)
-
-    def home(self, j, other):
+                signal((source, k // 2, k % 2, flip(h, 1 - self.near), p))
+
+        return 2 + self.sends * (4 - self.near)
+
+    def near_copy(self, j):
         h, p = self.at[3], self.at[4]
-        return (1 - j % 2, j // 2, j % 2, 1 - h, p) if other else (j % 2, j // 2, j % 2, h, p)
-
-    def copy(self, j, other):
+        home = (j % 2, j // 2, j % 2, h, p)
+        return remote(self.piece(j), self.place(self.s), self.send.at[j], self.recv.at[self.s], home)
+
+    def far_copy(self, src, i, j):
+        h, p = self.at[3], self.at[4]
+        home = (1 - j % 2, j // 2, j % 2, 1 - h, p)
+        return remote(src, self.place(self.s), self.send.at[4 + i], self.recv.at[self.s], home)
+
+    def direct(self, i):
+        j = 2 * i + 1 - self.layer
+        return self.far_copy(self.piece(j), i, j)
+
+    def relayed(self, i):
+        return self.far_copy(self.relay.at[i], i, 2 * i + self.layer)
+
+    def to_twin(self, i):
+        y, x, c, h, p = self.at
         return remote(
-            self.piece(j), self.place(self.s), self.send.at[4 * other + j], self.recv.at[self.s], self.home(j, other)
+            self.piece(2 * i + self.layer),
+            self.relay.at[i],
+            self.relay_send.at[i],
+            self.relay_recv.at[i],
+            (1 - self.layer, x, c, h, p),
         )
 
+    def start_relay(self):
+        @pl.when(self.sends == 1)
+        def _():
+            for i in range(2):
+                self.to_twin(i).start()
+
     def start(self):
-        for j in range(4):
-
-            @pl.when(self.sends == 1)
-            def _(j=j):
-                self.copy(j, 1).start()
+        @pl.when(self.sends == 1)
+        def _():
+            for i in range(2):
+                self.direct(i).start()
 
         for j in range(4):
 
             @pl.when(self.sends - self.is_me(j) == 1)
             def _(j=j):
-                self.copy(j, 0).start()
+                self.near_copy(j).start()
 
             @pl.when(self.is_me(j) == 1)
             def _(j=j):
                 pltpu.make_async_copy(self.piece(j), self.place(j), self.local).start()
 
+    def forward(self):
+        @pl.when(self.sends == 0)
+        def _():
+            for i in range(2):
+                self.to_twin(i).wait_recv()
+                self.relayed(i).start()
+
     def finish(self):
         for k in range(4):
             dst = self.place(k)
@@ -800,42 +906,53 @@
             def _(k=k, dst=dst):
                 pltpu.make_async_copy(self.piece(k), dst, self.local).wait()
 
+        @pl.when(self.sends == 0)
+        def _():
+            for i in range(2):
+                self.relayed(i).wait_send()
+
+        @pl.when(self.sends == 1)
+        def _():
+            for i in range(2):
+                self.direct(i).wait_send()
+                self.to_twin(i).wait_send()
+
         for j in range(4):
-
-            @pl.when(self.sends == 1)
-            def _(j=j):
-                self.copy(j, 1).wait_send()
 
             @pl.when(self.sends - self.is_me(j) == 1)
             def _(j=j):
-                self.copy(j, 0).wait_send()
+                self.near_copy(j).wait_send()
 
 
 class ToShards:
-    def __init__(self, at, layer, piece, place, sems):
-        self.at, self.layer, self.piece, self.place = at, layer, piece, place
+    def __init__(self, at, layer, piece, place, sems, roles=(0, 1)):
+        self.at, self.layer, self.piece, self.place, self.roles = at, layer, piece, place, roles
         self.send, self.recv, self.local = sems
         y, x, c, h, p = at
         self.s = 2 * x + c
         self.gets = same(y, layer)
         self.role = far_role(at)
+        self.active = {(0, 1): 1, (0,): 1 - self.role, (1,): self.role}[roles]
 
     def is_me(self, k):
-        return self.gets * (1 - self.role) * same(self.s, k)
+        return self.gets * (1 - self.role) * same(self.s, k) if 0 in self.roles else 0 * self.gets
 
     def greet(self):
         h, p = self.at[3], self.at[4]
         for j in range(4):
-
-            @pl.when(self.gets == 1)
-            def _(j=j):
-                signal((1 - j % 2, j // 2, j % 2, 1 - h, p))
-
-            @pl.when(self.gets - self.is_me(j) == 1)
-            def _(j=j):
-                signal((j % 2, j // 2, j % 2, h, p))
-
-        return 4 - self.gets * (1 - self.role)
+            if 1 in self.roles:
+
+                @pl.when(self.gets == 1)
+                def _(j=j):
+                    signal((1 - j % 2, j // 2, j % 2, 1 - h, p))
+
+            if 0 in self.roles:
+
+                @pl.when(self.gets - self.is_me(j) == 1)
+                def _(j=j):
+                    signal((j % 2, j // 2, j % 2, h, p))
+
+        return self.active * (4 - self.gets * (1 - self.role))
 
     def copy(self, k):
         home = (self.layer, k // 2, k % 2, flip(self.at[3], self.role), self.at[4])
@@ -846,7 +963,7 @@
     def start(self):
         for k in range(4):
 
-            @pl.when(self.is_me(k) == 0)
+            @pl.when(self.active - self.is_me(k) == 1)
             def _(k=k):
                 self.copy(k).start()
 
@@ -855,7 +972,7 @@
                 pltpu.make_async_copy(self.piece(k), self.place(0, k), self.local).start()
 
     def finish(self):
-        for role in range(2):
+        for role in self.roles:
             for j in range(4):
                 dst = self.place(role, j)
                 comes = self.gets if role else self.gets - self.is_me(j)
@@ -866,7 +983,7 @@
 
         for k in range(4):
 
-            @pl.when(self.is_me(k) == 0)
+            @pl.when(self.active - self.is_me(k) == 1)
             def _(k=k):
                 self.copy(k).wait_send()
 
@@ -940,7 +1057,7 @@
 
 def head_sems():
     dma = pltpu.SemaphoreType.DMA
-    return (dma((8,)), dma((4,)), dma)
+    return (dma((6,)), dma((4,)), dma, dma((2,)), dma((2,)))
 
 
 def shard_sems():
@@ -985,7 +1102,7 @@
 def project_block(b, buf, w_ref, cos_ref, sin_ref, mix_ref, qkv_ref):
     rows, half = buf.shape[1], HS // 2
     cols = span(b, rows)
-    raw = dot(w_ref[...], buf[b], NT)
+    raw = dot(w_ref[:3].reshape(3 * HS, buf.shape[2]), buf[b], NT)
     cosine, sine = cos_ref[:, cols], sin_ref[:, cols]
     for first, scale in ((0, HS**-0.5), (HS, 1.0)):
         a, bb = turned(raw[first : first + half], raw[first + half : first + HS], cosine, sine)
@@ -997,82 +1114,6 @@
     qkv_ref[2 * HS :, cols] = value.astype(LOW)
 
 
-def first_kernel(
-    cos_ref, sin_ref, seg_ref, in_ref, a_ref, f_ref, gain_ref,
-    qkv_ref, att_ref, flat_ref, lse_ref, x_ref, normed_ref, a0, a1, f0, f1, gains,
-    buf, x_here, w_ref, gain_here, key_x, query_x, val_x, scores,
-    ag_sems, block_sems, a0_sems, a1_sems, f0_sems, f1_sems, swap, gain_sems, loads,
-):
-    at = spot()
-    y, x, c, h, p = at
-    far = far_role(at)
-    partner, above = (y, x, c, 1 - h, p), (1 - y, x, c, h, p)
-    size = f_ref.shape[1] // 4
-    a_pushes = [
-        ToHeads(at, layer, slices(a_ref, HS), columns(into), sems)
-        for layer, into, sems in ((0, a0, a0_sems), (1, a1, a1_sems))
-    ]
-    f_pushes = [
-        ToHeads(at, layer, slices(f_ref, size), columns(into), sems)
-        for layer, into, sems in ((0, f0, f0_sems), (1, f1, f1_sems))
-    ]
-    greet(at, *a_pushes, *f_pushes, peers=(above, partner))
-    swapped = remote(in_ref.at[1 - h], x_here, swap.at[0], swap.at[1], partner)
-    stays = pltpu.make_async_copy(in_ref.at[h], x_here, swap.at[2])
-
-    @pl.when(far == 1)
-    def _():
-        swapped.start()
-
-    @pl.when(far == 0)
-    def _():
-        stays.start()
-
-    across = remote(gain_ref, gains.at[y], gain_sems.at[0], gain_sems.at[1], above)
-    across.start()
-    keeps = pltpu.make_async_copy(gain_ref, gains.at[y], gain_sems.at[2])
-    keeps.start()
-    for push in a_pushes:
-        push.start()
-    keeps.wait()
-    across.wait_send()
-    remote(gain_ref, gains.at[1 - y], gain_sems.at[0], gain_sems.at[1], above).wait_recv()
-    gain_copy = pltpu.make_async_copy(gains.at[0], gain_here, loads.at[0])
-    gain_copy.start()
-
-    @pl.when(far == 1)
-    def _():
-        swapped.wait()
-
-    @pl.when(far == 0)
-    def _():
-        stays.wait()
-
-    gain_copy.wait()
-    save = pltpu.make_async_copy(x_here, x_ref, loads.at[1])
-    save.start()
-    buf[block_of(at)] = (unit_of(x_here[...].astype(F32))[0] * gain_here[0:1]).astype(LOW)
-
-    def ready():
-        a_pushes[0].finish()
-        copies = [pltpu.make_async_copy(a0.at[i], w_ref.at[pl.ds(i * HS, HS)], loads.at[2 + i]) for i in range(3)]
-        for copy in copies:
-            copy.start()
-        for push in f_pushes:
-            push.start()
-        for copy in copies:
-            copy.wait()
-
-    keep = (normed_ref, block_sems)
-    gather(at, buf, ag_sems, lambda b: project_block(b, buf, w_ref, cos_ref, sin_ref, None, qkv_ref), keep, ready)
-    attend_body(qkv_ref, seg_ref, att_ref, flat_ref, lse_ref, key_x, query_x, val_x, scores)
-    kept(buf, keep)
-    save.wait()
-    a_pushes[1].finish()
-    for push in f_pushes:
-        push.finish()
-
-
 def up_block(b, buf, f_ref, hidden_ref, one_ref, two_ref):
     rows = span(b, buf.shape[1])
     x = buf[b]
@@ -1084,108 +1125,299 @@
     two_ref[rows] = activated.astype(LOW)
 
 
-def middle_kernel(
-    att_ref, x_ref, wo_ref, f_ref, gain_mid_ref, gain_in_ref, w_ref, cos_ref, sin_ref, mix_ref,
-    middle_ref, out_ref, hidden_ref, one_ref, two_ref, qkv_ref, nmid_ref, normed_ref, home_ref,
-    buf, total, out_c, in_c, rin, ag_sems, rs_sems, block_sems, homing,
+def held(buf):
+    def blocks(use):
+        def one(b, none):
+            use(b, buf[b])
+            return none
+
+        lax.fori_loop(0, buf.shape[0], one, 0)
+
+    return blocks
+
+
+def streamed(far, ring, sems):
+    half = ring.shape[0]
+
+    def copy(b, slot):
+        return pltpu.make_async_copy(far.at[b], ring.at[slot], sems.at[slot])
+
+    for slot in range(half):
+        copy(slot, slot).start()
+
+    def blocks(use):
+        def first(b, none):
+            copy(b, b).wait()
+            use(b, ring[b])
+            copy(b + half, b).start()
+            return none
+
+        def second(b, none):
+            copy(b + half, b).wait()
+            use(b + half, ring[b])
+            return none
+
+        lax.fori_loop(0, half, first, 0)
+        lax.fori_loop(0, half, second, 0)
+
+    return blocks
+
+
+class Stage:
+    def __init__(self, sems):
+        self.sems, self.count = sems, 0
+
+    def copy(self, src, dst):
+        copy = pltpu.make_async_copy(src, dst, self.sems.at[self.count])
+        self.count += 1
+        copy.start()
+        return copy
+
+
+def taking_turns(*steps):
+    steps = list(steps)
+    while steps:
+        for one in list(steps):
+            if next(one, True):
+                steps.remove(one)
+        yield
+
+
+def feed_scratch(length, f_ref):
+    return [pltpu.VMEM((length, f_ref.shape[1]), LOW)] * 3 + [pltpu.VMEM(f_ref.shape, F32)]
+
+
+def out_project(at, push, att_in, wo_all, x_ref):
+    push.finish()
+    heads = att_in.shape[0] * HS
+    summed = dot(att_in[...].reshape(heads, -1), wo_all[...].reshape(heads, -1), TN)
+    return x_ref[...].astype(F32) + summed
+
+
+def attend_and_share(at, steps, push, before, *refs):
+    def after(qi):
+        if qi == 0 and before is not None:
+            before()
+        each = TILE * 16 // refs[0].shape[1]
+        for b in range(qi * each, (qi + 1) * each):
+            push.start(b)
+        next(steps, None)
+
+    attend_body(*refs, after)
+    run(steps)
+
+
+def hidden_back(b, buf, f_ref, hidden_ref, one_ref, two_ref, sums_ref):
+    here = span(b, buf.shape[1])
+    grad = dot(buf[b], f_ref[2], NT)
+    one_ref[here] = (grad * one_ref[here].astype(F32)).astype(LOW)
+    two_ref[here] = (grad * two_ref[here].astype(F32)).astype(LOW)
+    sums_ref[2] += dot(hidden_ref[here], buf[b], TN)
+
+
+def down_back(
+    at, top, ready, buf, blocks, total, boxes, ag_sems, rs_sems, f_ref, hidden_ref, one_ref, two_ref,
+    gain_ref, middle_ref, sums_ref, wo_all, dout_block, push, dmid_ref, gain_grad_ref,
+):
+    rows = buf.shape[1]
+    if not ready:
+        sums_ref[...] = jnp.zeros_like(sums_ref)
+        buf[block_of(at)] = top().astype(LOW)
+        gather(at, buf, ag_sems, lambda b: hidden_back(b, buf, f_ref, hidden_ref, one_ref, two_ref, sums_ref))
+
+    def partial(b):
+        here = span(b, rows)
+        return dot(one_ref[here], f_ref[0]) + dot(two_ref[here], f_ref[1])
+
+    scatter(at, total, boxes, rs_sems, partial)
+    grad, gain_grad = back_of(total[...], middle_ref[...], gain_ref[...])
+    gain_grad_ref[...] = gain_grad
+    grad = grad + top()
+    dmid_ref[...] = grad
+    heads = wo_all.shape[0] * HS
+    found = dot(wo_all[...].reshape(heads, -1), grad.astype(LOW), NT).astype(LOW)
+    dout_block[...] = found.reshape(dout_block.shape)
+    for b in range(16):
+        push.start(b)
+
+    def gate_up(b, normed):
+        here = span(b, rows)
+        sums_ref[0] += dot(one_ref[here], normed, TN)
+        sums_ref[1] += dot(two_ref[here], normed, TN)
+
+    blocks(gate_up)
+    push.finish()
+
+
+def first_kernel(
+    cos_ref, sin_ref, seg_ref, in_ref, a_ref, f_ref, gain_ref,
+    qkv0_ref, att_ref, lse_ref, att_in, wo_all, x_here, middle_ref, out_ref, qkv1_ref,
+    normed0_far, nmid_far, normed1_far, hidden_far, one_far, two_far, home_ref, a0, a1, f0, f1, gains, a0_relay, a1_relay, f0_relay, f1_relay,
+    buf, low_ref, a_here, f_here, gain_here, hidden_ref, one_ref, two_ref,
+    key_x, query_x, val_x, scores, total, out_c, in_c, rin,
+    ag_sems, wo_sems, rs_sems, share_sems, block_sems, a0_sems, a1_sems, f0_sems, f1_sems, swap, gain_sems, loads,
+    homing,
+):
+    at = spot()
+    y, x, c, h, p = at
+    rows = x_here.shape[0]
+    far = far_role(at)
+    stage = Stage(loads)
+    partner, above = (y, x, c, 1 - h, p), (1 - y, x, c, h, p)
+    size = f_ref.shape[1] // 4
+    a_pushes = [
+        ToHeads(at, layer, slices(a_ref, HS), columns(into), relay, sems)
+        for layer, into, relay, sems in ((0, a0, a0_relay, a0_sems), (1, a1, a1_relay, a1_sems))
+    ]
+    f_pushes = [
+        ToHeads(at, layer, slices(f_ref, size), columns(into), relay, sems)
+        for layer, into, relay, sems in ((0, f0, f0_relay, f0_sems), (1, f1, f1_relay, f1_sems))
+    ]
+    home = ToHome(at, 0, out_ref, lambda m: home_ref.at[m], homing)
+    share = ToRows(at, lambda b: low_ref.at[:, pl.ds(b * rows, rows)], lambda b: att_in.at[b], share_sems)
+    greet(at, *a_pushes, *f_pushes, home, peers=(partner,))
+    swapped = remote(in_ref.at[1 - h], x_here, swap.at[0], swap.at[1], partner)
+    stays = pltpu.make_async_copy(in_ref.at[h], x_here, swap.at[2])
+
+    @pl.when(far == 1)
+    def _():
+        swapped.start()
+
+    @pl.when(far == 0)
+    def _():
+        stays.start()
+
+    across = remote(gain_ref, gains.at[y], gain_sems.at[0], gain_sems.at[1], above)
+    across.start()
+    keeps = pltpu.make_async_copy(gain_ref, gains.at[y], gain_sems.at[2])
+    keeps.start()
+    for push in a_pushes:
+        push.start_relay()
+    a_pushes[0].start()
+    for push in f_pushes:
+        push.start_relay()
+    a_pushes[0].forward()
+    keeps.wait()
+    across.wait_send()
+    remote(gain_ref, gains.at[1 - y], gain_sems.at[0], gain_sems.at[1], above).wait_recv()
+    gain_copy = stage.copy(gains, gain_here)
+
+    @pl.when(far == 1)
+    def _():
+        swapped.wait()
+
+    @pl.when(far == 0)
+    def _():
+        stays.wait()
+
+    gain_copy.wait()
+    buf[block_of(at)] = (unit_of(x_here[...].astype(F32))[0] * gain_here[0, 0:1]).astype(LOW)
+
+    def ready():
+        a_pushes[0].finish()
+        copy = stage.copy(a0, a_here)
+        for push in (a_pushes[1], f_pushes[0]):
+            push.start()
+            push.forward()
+        copy.wait()
+
+    keep = (normed0_far, block_sems)
+    gather(at, buf, ag_sems, lambda b: project_block(b, buf, a_here, cos_ref, sin_ref, None, qkv0_ref), keep, ready)
+    wo_all[block_of(at)] = a_here[3]
+    attend_and_share(
+        at, gathering(at, wo_all, wo_sems), share, lambda: kept(buf, keep),
+        qkv0_ref, seg_ref, att_ref, low_ref, lse_ref, key_x, query_x, val_x, scores,
+    )
+    middle = out_project(at, share, att_in, wo_all, x_here)
+    middle_ref[...] = middle
+    buf[block_of(at)] = (unit_of(middle)[0] * gain_here[0, 1:2]).astype(LOW)
+    keep = (nmid_far, block_sems)
+
+    def more():
+        f_pushes[0].finish()
+        copy = stage.copy(f0, f_here)
+        f_pushes[1].start()
+        f_pushes[1].forward()
+        copy.wait()
+
+    gather(at, buf, ag_sems, lambda b: up_block(b, buf, f_here, hidden_ref, one_ref, two_ref), keep, more)
+    saves = [stage.copy(*pair) for pair in ((hidden_ref, hidden_far), (one_ref, one_far), (two_ref, two_far))]
+    boxes = (out_c, in_c, rin)
+    scatter(
+        at, total, boxes, rs_sems, lambda b: dot(hidden_ref[span(b, rows)], f_here[2]), lambda: kept(buf, keep)
+    )
+    out = (middle_ref[...] + total[...]).astype(LOW)
+    out_ref[...] = out
+    home.start()
+    buf[block_of(at)] = (unit_of(out.astype(F32))[0] * gain_here[1, 0:1]).astype(LOW)
+    keep = (normed1_far, block_sems)
+
+    def last():
+        a_pushes[1].finish()
+        stage.copy(a1, a_here).wait()
+
+    mix_ref = qkv0_ref.at[pl.ds(2 * HS, HS)]
+    gather(
+        at, buf, ag_sems, lambda b: project_block(b, buf, a_here, cos_ref, sin_ref, mix_ref, qkv1_ref), keep, last
+    )
+    kept(buf, keep)
+    for save in saves:
+        save.wait()
+    home.finish()
+    f_pushes[1].finish()
+
+
+def turn_kernel(
+    qkv_ref, seg_ref, a_ref, f_ref, gain_ref, x_ref, top_ref,
+    att_ref, lse_ref, att_in, dmid_ref, gain_grad_ref, dout_ref, f_grad_ref, middle_ref, hidden_far,
+    buf, nmid, wo_all, low_ref, dout_block, total, out_c, in_c, rin,
+    ag_sems, wo_sems, rs_sems, share_sems, back_sems, loads,
 ):
     at = spot()
     rows = x_ref.shape[0]
-    push = ToHome(at, 0, out_ref, lambda m: home_ref.at[m], homing)
-    greet(at, push)
-    boxes = (out_c, in_c, rin)
-    scatter(at, total, boxes, rs_sems, lambda b: dot(att_ref[span(b, rows)], wo_ref[...]))
-    middle = x_ref[...].astype(F32) + total[...]
-    middle_ref[...] = middle
-    buf[block_of(at)] = (unit_of(middle)[0] * gain_mid_ref[...]).astype(LOW)
-    keep = (nmid_ref, block_sems)
-    gather(at, buf, ag_sems, lambda b: up_block(b, buf, f_ref, hidden_ref, one_ref, two_ref), keep)
-    scatter(
-        at, total, boxes, rs_sems, lambda b: dot(hidden_ref[span(b, rows)], f_ref[2]), lambda: kept(buf, keep)
-    )
-    out = (middle_ref[...] + total[...]).astype(LOW)
-    out_ref[...] = out
-    push.start()
-    buf[block_of(at)] = (unit_of(out.astype(F32))[0] * gain_in_ref[...]).astype(LOW)
-    keep = (normed_ref, block_sems)
-    gather(at, buf, ag_sems, lambda b: project_block(b, buf, w_ref, cos_ref, sin_ref, mix_ref, qkv_ref), keep)
-    kept(buf, keep)
-    push.finish()
-
-
-def down_back(
-    at, top, buf, nmid, total, boxes, ag_sems, rs_sems, f_ref, hidden_ref, one_ref, two_ref, wo_ref, att_ref,
-    gain_ref, middle_ref, sums_ref, out_sum_ref,
-    dmid_ref, gain_grad_ref, dout_ref, f_grad_ref, out_grad_ref,
-):
-    rows = buf.shape[1]
-    buf[block_of(at)] = top.astype(LOW)
-    sums_ref[...] = jnp.zeros_like(sums_ref)
-    out_sum_ref[...] = jnp.zeros_like(out_sum_ref)
-
-    def hidden_back(b):
-        here = span(b, rows)
-        grad = dot(buf[b], f_ref[2], NT)
-        one_ref[here] = (grad * one_ref[here].astype(F32)).astype(LOW)
-        two_ref[here] = (grad * two_ref[here].astype(F32)).astype(LOW)
-        sums_ref[2] += dot(hidden_ref[here], buf[b], TN)
-
-    gather(at, buf, ag_sems, hidden_back)
-
-    def partial(b):
-        here = span(b, rows)
-        return dot(one_ref[here], f_ref[0]) + dot(two_ref[here], f_ref[1])
-
-    scatter(at, total, boxes, rs_sems, partial)
-    grad, gain_grad = back_of(total[...], middle_ref[...], gain_ref[...])
-    gain_grad_ref[...] = gain_grad
-    grad = grad + top
-    dmid_ref[...] = grad
-    buf[block_of(at)] = grad.astype(LOW)
-
-    def out_back(b):
-        here = span(b, rows)
-        dout_ref[:, here] = dot(wo_ref[...], buf[b], NT).astype(LOW)
-        out_sum_ref[...] += dot(att_ref[here], buf[b], TN)
-        sums_ref[0] += dot(one_ref[here], nmid[b], TN)
-        sums_ref[1] += dot(two_ref[here], nmid[b], TN)
-
-    gather(at, buf, ag_sems, out_back)
-    f_grad_ref[...] = sums_ref[...].astype(LOW)
-    out_grad_ref[...] = out_sum_ref[...].astype(LOW)
-
-
-def turn_kernel(
-    att_ref, x_ref, wo_ref, f_ref, gain_ref, top_ref,
-    dmid_ref, gain_grad_ref, dout_ref, f_grad_ref, out_grad_ref, home_ref,
-    buf, nmid, out_ref, total, out_c, in_c, rin, middle_ref, hidden_ref, one_ref, two_ref, sums_ref,
-    out_sum_ref, ag_sems, rs_sems, homing,
-):
-    at = spot()
-    rows = x_ref.shape[0]
-    push = ToHome(at, 1, out_ref, lambda m: home_ref.at[m], homing)
-    greet(at, push)
-    boxes = (out_c, in_c, rin)
-    scatter(at, total, boxes, rs_sems, lambda b: dot(att_ref[span(b, rows)], wo_ref[...]))
-    middle = x_ref[...].astype(F32) + total[...]
+    share = ToRows(at, lambda b: low_ref.at[:, pl.ds(b * rows, rows)], lambda b: att_in.at[b], share_sems)
+
+    def column(b):
+        start = b * rows
+        return dout_ref.at[:, pl.ds(start if isinstance(b, int) else pl.multiple_of(start, rows), rows)]
+
+    back = ToRows(at, lambda b: dout_block.at[b], column, back_sems)
+    greet(at)
+    wo_all[block_of(at)] = a_ref[3]
+    buf[block_of(at)] = top_ref[...]
+    steps = taking_turns(gathering(at, wo_all, wo_sems), gathering(at, buf, ag_sems))
+    pl.run_scoped(
+        functools.partial(attend_and_share, at, steps, share, None, qkv_ref, seg_ref, att_ref, low_ref, lse_ref),
+        *attend_scratch(qkv_ref.shape[1]),
+    )
+    middle = out_project(at, share, att_in, wo_all, x_ref)
     middle_ref[...] = middle
     nmid[block_of(at)] = (unit_of(middle)[0] * gain_ref[...]).astype(LOW)
-    gather(at, nmid, ag_sems, lambda b: up_block(b, nmid, f_ref, hidden_ref, one_ref, two_ref))
-    scatter(at, total, boxes, rs_sems, lambda b: dot(hidden_ref[span(b, rows)], f_ref[2]))
-    out_ref[...] = (middle_ref[...] + total[...]).astype(LOW)
-    push.start()
-    down_back(
-        at, top_ref[...].astype(F32), buf, nmid, total, boxes, ag_sems, rs_sems, f_ref, hidden_ref, one_ref, two_ref,
-        wo_ref, att_ref, gain_ref, middle_ref, sums_ref, out_sum_ref,
-        dmid_ref, gain_grad_ref, dout_ref, f_grad_ref, out_grad_ref,
-    )
-    push.finish()
+
+    def rest(hidden_ref, one_ref, two_ref, sums_ref):
+        sums_ref[...] = jnp.zeros_like(sums_ref)
+
+        def both_ways(b):
+            up_block(b, nmid, f_ref, hidden_ref, one_ref, two_ref)
+            hidden_back(b, buf, f_ref, hidden_ref, one_ref, two_ref, sums_ref)
+
+        gather(at, nmid, ag_sems, both_ways)
+        save = Stage(loads).copy(hidden_ref, hidden_far)
+        boxes = (out_c, in_c, rin)
+        down_back(
+            at, lambda: top_ref[...].astype(F32), True, buf, held(nmid), total, boxes, ag_sems, rs_sems, f_ref, hidden_ref, one_ref,
+            two_ref, gain_ref, middle_ref, sums_ref, wo_all, dout_block, back, dmid_ref, gain_grad_ref,
+        )
+        f_grad_ref[...] = sums_ref[...].astype(LOW)
+        save.wait()
+
+    pl.run_scoped(rest, *feed_scratch(qkv_ref.shape[1], f_ref))
 
 
 def input_back(
-    at, dqkv_ref, w_ref, x_ref, gain_ref, dmid_ref, gain_grad_ref, total, boxes, rs_sems, normed, load, sum_ref, after=None
+    at, dqkv_ref, a_ref, x_ref, gain_ref, dmid_ref, gain_grad_ref, total, boxes, rs_sems, normed, load, sum_ref, after
 ):
-    rows = total.shape[0]
+    rows, width = total.shape
 
     def weight_sum():
         load.wait()
@@ -1196,91 +1428,189 @@
             return none
 
         lax.fori_loop(0, 16, one, 0)
-        if after is not None:
-            after()
-
-    scatter(
-        at, total, boxes, rs_sems, lambda b: dot(dqkv_ref[:, span(b, rows)], w_ref[...], TN), weight_sum
-    )
+        after()
+
+    def partial(b):
+        return dot(dqkv_ref[:, span(b, rows)], a_ref[:3].reshape(3 * HS, width), TN)
+
+    scatter(at, total, boxes, rs_sems, partial, weight_sum)
     grad, gain_grad = back_of(total[...], x_ref[...].astype(F32), gain_ref[...])
     gain_grad_ref[...] = gain_grad
     return grad + dmid_ref[...]
 
 
+def staged_scratch(refs):
+    return [pltpu.VMEM(ref.shape, ref.dtype) for ref in refs]
+
+
+def attend_back_staged(stage, far, outs, steps, early, *refs):
+    near, scratch = refs[: len(far)], refs[len(far) :]
+    copies = [stage.copy(*pair) for pair in zip(far, near)]
+    for _ in range(early):
+        next(steps, None)
+    for copy in copies:
+        copy.wait()
+    attend_back_body(*near, *outs, *scratch, lambda ki: next(steps, None))
+    run(steps)
+
+
+def out_weight_steps(at, total, boxes, sems, att_in, dmid_ref, low_ref):
+    low_ref[...] = dmid_ref[...].astype(LOW)
+    return scattering(at, total, boxes, sems, lambda b: dot(att_in[b], low_ref[...]))
+
+
+def put_grads(a_grad_ref, in_sum_ref, out_total):
+    for i in range(3):
+        a_grad_ref[i] = in_sum_ref[i * HS : (i + 1) * HS].astype(LOW)
+    a_grad_ref[3] = out_total[...].astype(LOW)
+
+
+def by_columns(ref):
+    wide = ref.shape[-1] // 4
+    return lambda k: ref.at[:, :, pl.ds(k * wide, wide)]
+
+
 def lower_kernel(
-    dqkv_ref, x_ref, w_ref, gain_in_ref, dmid_above_ref, f_ref, wo_ref, att_ref, gain_mid_ref, middle_ref,
-    hidden_far, one_far, two_far, normed_far, nmid_far,
-    gain_in_grad_ref, a_grad_ref, dmid_ref, gain_mid_grad_ref, dout_ref, f_grad_ref, out_grad_ref, home_ref,
-    buf, nmid, grad_ref, low_ref, total, out_c, in_c, rin, hidden_ref, one_ref, two_ref, sums_ref, out_sum_ref,
-    in_sum_ref, ag_sems, rs_sems, loads, homing,
+    a_ref, gain_in_ref, dmid_above, att_in, gain_mid_ref,
+    x_far, f_far, middle_far, qkv_far, seg_far, att_far, lse_far, dout_far, cos_far, sin_far,
+    hidden_far, one_far, two_far, normed_far, nmid_far, wo_far, hidden_above, middle_above, f_above, f_grad_above,
+    send_ref, gain_in_grad_ref, dmid_ref, gain_mid_grad_ref, dout_ref, f_grad_ref, a_grad_ref, home_ref, out_home, f_in_far,
+    buf, wo_all, dqkv_ref, low_ref, out_ref, in_sum_ref, dout_block,
+    total, out_c, in_c, rin, out_total, out_c2, in_c2, rin2,
+    ag_sems, rs_sems, rs2_sems, back_sems, f_sems, homing, out_homing, loads, ring_sems,
 ):
     at = spot()
-    push = ToHome(at, 1, low_ref, lambda m: home_ref.at[m], homing)
-    copies = [
-        pltpu.make_async_copy(far, near, loads.at[i])
-        for i, (far, near) in enumerate(
-            (
-                (normed_far, buf),
-                (hidden_far, hidden_ref),
-                (one_far, one_ref),
-                (two_far, two_ref),
-                (nmid_far, nmid),
-            )
+    rows = low_ref.shape[0]
+    stage = Stage(loads)
+    normed_copy = stage.copy(normed_far, buf)
+    wo_copy = stage.copy(wo_far, wo_all)
+    length = dqkv_ref.shape[1]
+    home = ToHome(at, 1, low_ref, lambda m: home_ref.at[m], homing)
+    out = ToHome(at, 1, out_ref, lambda m: out_home.at[m], out_homing)
+
+    def column(b):
+        start = b * rows
+        return dout_ref.at[:, pl.ds(start if isinstance(b, int) else pl.multiple_of(start, rows), rows)]
+
+    back = ToRows(at, lambda b: dout_block.at[b], column, back_sems)
+    push = ToShards(at, 1, by_columns(f_grad_above), lambda role, j: f_in_far.at[j], f_sems, (1,))
+    greet(at, home, out, push)
+    push.start()
+    boxes = (out_c, in_c, rin)
+
+    def out_steps(hidden_ref, down_ref):
+        yield from scattering(
+            at, total, boxes, rs_sems, lambda b: dot(hidden_ref[span(b, rows)], down_ref[...])
         )
-    ]
-    for copy in copies:
-        copy.start()
-    greet(at, push)
-    boxes = (out_c, in_c, rin)
-    grad = input_back(
-        at, dqkv_ref, w_ref, x_ref, gain_in_ref, dmid_above_ref, gain_in_grad_ref, total, boxes, rs_sems, buf,
-        copies[0], in_sum_ref,
-    )
-    grad_ref[...] = grad
-    low_ref[...] = grad.astype(LOW)
-    push.start()
-    a_grad_ref[...] = in_sum_ref[...].astype(LOW)
-    for copy in copies[1:]:
-        copy.wait()
-    down_back(
-        at, grad_ref[...], buf, nmid, total, boxes, ag_sems, rs_sems, f_ref, hidden_ref, one_ref, two_ref, wo_ref,
-        att_ref, gain_mid_ref, middle_ref, sums_ref, out_sum_ref,
-        dmid_ref, gain_mid_grad_ref, dout_ref, f_grad_ref, out_grad_ref,
-    )
+        out_ref[...] = (dmid_ref[...] + total[...]).astype(LOW)
+        out.start()
+
+    def weight_steps():
+        for _ in range(5):
+            yield
+        yield from out_weight_steps(at, out_total, (out_c2, in_c2, rin2), rs2_sems, att_in, dmid_above, low_ref)
+
+    def attention(hidden_ref, down_ref, *refs):
+        copies = [
+            stage.copy(*pair)
+            for pair in ((hidden_above, hidden_ref), (f_above.at[2], down_ref), (middle_above, dmid_ref))
+        ]
+        for copy in copies:
+            copy.wait()
+        steps = taking_turns(out_steps(hidden_ref, down_ref), weight_steps())
+        attend_back_staged(
+            stage, (qkv_far, seg_far, att_far, lse_far, dout_far, cos_far, sin_far), (None, dqkv_ref, send_ref),
+            steps, 3, *refs,
+        )
+
+    pl.run_scoped(
+        attention,
+        pltpu.VMEM(hidden_above.shape, LOW),
+        pltpu.VMEM(f_above.shape[1:], LOW),
+        *staged_scratch((qkv_far, seg_far, att_far, lse_far, dout_far, cos_far, sin_far)),
+        *attend_back_scratch(length),
+    )
+
+    def after():
+        put_grads(a_grad_ref, in_sum_ref, out_total)
+
+    def rest(hidden_ref, one_ref, two_ref, sums_ref, x_ref, f_ref, middle_ref, ring):
+        blocks = streamed(nmid_far, ring, ring_sems)
+        pairs = (
+            (x_far, x_ref),
+            (f_far, f_ref),
+            (middle_far, middle_ref),
+            (hidden_far, hidden_ref),
+            (one_far, one_ref),
+            (two_far, two_ref),
+        )
+        copies = [stage.copy(*pair) for pair in pairs]
+        copies.pop(0).wait()
+        grad = input_back(
+            at, dqkv_ref, a_ref, x_ref, gain_in_ref, dmid_above, gain_in_grad_ref, total, boxes, rs_sems, buf,
+            normed_copy, in_sum_ref, after,
+        )
+        dmid_ref[...] = grad
+        low_ref[...] = grad.astype(LOW)
+        home.start()
+        for copy in copies + [wo_copy]:
+            copy.wait()
+        down_back(
+            at, lambda: dmid_ref[...], False, buf, blocks, total, boxes, ag_sems, rs_sems, f_ref, hidden_ref, one_ref, two_ref,
+            gain_mid_ref, middle_ref, sums_ref, wo_all, dout_block, back, dmid_ref, gain_mid_grad_ref,
+        )
+        f_grad_ref[...] = sums_ref[...].astype(LOW)
+
+    ring_type = pltpu.VMEM((8, *nmid_far.shape[1:]), LOW)
+    pl.run_scoped(rest, *feed_scratch(length, f_far), *staged_scratch((x_far, f_far, middle_far)), ring_type)
+    home.finish()
+    out.finish()
     push.finish()
 
 
 def last_kernel(
-    dqkv_ref, x_ref, w_ref, gain_ref, dmid_ref, out_grad_ref, gains_ref, normed_far,
-    home_ref, a_in, gain_sum,
-    buf, total, out_c, in_c, rin, in_sum_ref, a_grad_ref, low_ref, gain_grad_ref, heard, rs_sems, loads, homing,
-    a_sems, gain_sems,
+    qkv_ref, seg_ref, att_ref, lse_ref, dout_in, cos_ref, sin_ref, extra_ref, x_ref, a_ref, gain_ref, dmid_ref,
+    att_in, gains_ref, f_grad, f_above, a_above, normed_far,
+    home_ref, f_in, f_in_above, a_in, a_in_above, gain_sum,
+    buf, dqkv_ref, low_ref, in_sum_ref, a_grad_ref, gain_grad_ref, heard,
+    key_x, val_x, query_x, dout_x, dq, scores, along,
+    total, out_c, in_c, rin, out_total, out_c2, in_c2, rin2,
+    rs_sems, rs2_sems, f_sems, f1_sems, a_sems, a1_sems, homing, gain_sems, loads,
 ):
     at = spot()
     y, x, c, h, p = at
-    copy = pltpu.make_async_copy(normed_far, buf, loads.at[0])
-    copy.start()
-    wide = a_grad_ref.shape[-1] // 4
-    shards = ToShards(
-        at, 0, lambda k: a_grad_ref.at[:, :, pl.ds(k * wide, wide)], lambda role, j: a_in.at[role, j], a_sems
-    )
-    push = ToHome(at, 0, low_ref, lambda m: home_ref.at[m], homing)
+    copy = Stage(loads).copy(normed_far, buf)
+    home = ToHome(at, 0, low_ref, lambda m: home_ref.at[m], homing)
+    early = [
+        ToShards(at, layer, by_columns(ref), place, sems, roles)
+        for layer, ref, place, sems, roles in (
+            (1, f_above, lambda role, j: f_in_above.at[j], f1_sems, (0,)),
+            (0, f_grad, lambda role, j: f_in.at[role, j], f_sems, (0, 1)),
+            (1, a_above, lambda role, j: a_in_above.at[role, j], a1_sems, (0, 1)),
+        )
+    ]
+    a_push = ToShards(at, 0, by_columns(a_grad_ref), lambda role, j: a_in.at[role, j], a_sems)
     peers = [moved(at, 0, 1), moved(at, 1), moved(at, 2), moved(at, 4), (y, x, c, 1 - h, p)]
-    greet(at, push, shards, peers=peers[4:])
-    boxes = (out_c, in_c, rin)
+    greet(at, home, a_push, *early, peers=peers[4:])
+    for push in early:
+        push.start()
+    steps = out_weight_steps(at, out_total, (out_c2, in_c2, rin2), rs2_sems, att_in, dmid_ref, low_ref)
+    attend_back_body(
+        qkv_ref, seg_ref, att_ref, lse_ref, dout_in, cos_ref, sin_ref, extra_ref, dqkv_ref, None,
+        key_x, val_x, query_x, dout_x, dq, scores, along, lambda ki: next(steps, None),
+    )
+    run(steps)
 
     def after():
-        for i in range(3):
-            a_grad_ref[i] = in_sum_ref[i * HS : (i + 1) * HS].astype(LOW)
-        a_grad_ref[3] = out_grad_ref[...]
-        shards.start()
+        put_grads(a_grad_ref, in_sum_ref, out_total)
+        a_push.start()
 
     grad = input_back(
-        at, dqkv_ref, w_ref, x_ref, gain_ref, dmid_ref, gain_grad_ref, total, boxes, rs_sems, buf, copy, in_sum_ref,
-        after,
+        at, dqkv_ref, a_ref, x_ref, gain_ref, dmid_ref, gain_grad_ref, total, (out_c, in_c, rin), rs_sems, buf, copy,
+        in_sum_ref, after,
     )
     low_ref[...] = grad.astype(LOW)
-    push.start()
+    home.start()
     gain_sum[0, 0:1] = gain_grad_ref[...]
     gain_sum[0, 1:4] = gains_ref[...]
     for i, peer in enumerate(peers):
@@ -1288,8 +1618,10 @@
         copy.start()
         copy.wait()
         gain_sum[i + 1] = gain_sum[i] + heard[i]
-    shards.finish()
-    push.finish()
+    for push in early:
+        push.finish()
+    a_push.finish()
+    home.finish()
 
 
 VMEM_SPEC = pl.BlockSpec(memory_space=pltpu.VMEM)
@@ -1304,7 +1636,7 @@
 def sum_boxes(rows, width):
     return [
         pltpu.VMEM((rows, width), F32),
-        pltpu.VMEM((8, rows, width), LOW),
+        pltpu.VMEM((4, rows, width), LOW),
         pltpu.VMEM((8, rows, width), LOW),
         pltpu.VMEM((7, rows, width), LOW),
     ]
@@ -1343,7 +1675,7 @@
     return lax.broadcasted_iota(jnp.int32, (TILE, 1), 0) <= lax.broadcasted_iota(jnp.int32, (1, TILE), 1)
 
 
-def attend_body(qkv_ref, seg_ref, att_ref, flat_ref, lse_ref, key_x, query_x, val_x, scores):
+def attend_body(qkv_ref, seg_ref, att_ref, low_ref, lse_ref, key_x, query_x, val_x, scores, after):
     length = qkv_ref.shape[1]
     for part in tiles(length):
         rows, hot = one_hot(seg_ref, part)
@@ -1387,11 +1719,12 @@
         totals = summed[HS : HS + 1]
         attended = summed[:HS] / totals
         att_ref[:, cols] = attended
-        flat_ref[cols] = attended.T.astype(LOW)
+        low_ref[:, cols] = attended.astype(LOW)
         lse_ref[:, cols] = largest + jnp.log(totals)
 
     for qi in range(length // TILE):
         query_tile(qi)
+        after(qi)
 
 
 def attend_scratch(length):
@@ -1411,7 +1744,7 @@
 
 def attend_back_body(
     qkv_ref, seg_ref, att_ref, lse_ref, dout_ref, cos_ref, sin_ref, extra_ref, dqkv_ref, send_ref,
-    key_x, val_x, query_x, dout_x, dq, scores, along,
+    key_x, val_x, query_x, dout_x, dq, scores, along, after,
 ):
     length = qkv_ref.shape[1]
     half, count = HS // 2, length // TILE
@@ -1487,6 +1820,7 @@
 
     for ki in range(count):
         key_tile(ki)
+        after(ki)
     scale = HS**-0.5
     a, b = turned(dq[:half] * scale, dq[half:] * scale, cos_ref[...], -sin_ref[...])
     dqkv_ref[:half] = a.astype(LOW)
@@ -1504,52 +1838,6 @@
         pltpu.VMEM((2, TILE, TILE), F32),
         pltpu.VMEM((2, TILE, TILE), F32),
     ]
-
-
-def attend_back_upper(
-    qkv_ref, seg_ref, att_ref, lse_ref, dout_ref, cos_ref, sin_ref, f_grad, dqkv_ref, send_ref, f_in, *rest
-):
-    *scratch, sems = rest
-    at = spot()
-    wide = f_grad.shape[-1] // 4
-    push = ToShards(
-        at, 1, lambda k: f_grad.at[:, :, pl.ds(k * wide, wide)], lambda role, j: f_in.at[role, j], sems
-    )
-    count = push.greet()
-    pl.semaphore_wait(pltpu.get_barrier_semaphore(), count)
-    push.start()
-    attend_back_body(
-        qkv_ref, seg_ref, att_ref, lse_ref, dout_ref, cos_ref, sin_ref, None, dqkv_ref, send_ref, *scratch
-    )
-    push.finish()
-
-
-def attend_back_lower(
-    qkv_ref, seg_ref, att_ref, lse_ref, dout_ref, cos_ref, sin_ref, extra_ref, f_grad, a_grad,
-    dqkv_ref, f_in, a_in, *rest,
-):
-    *scratch, f_sems, a_sems = rest
-    at = spot()
-    wide = f_grad.shape[-1] // 4
-    pushes = [
-        ToShards(
-            at,
-            layer,
-            lambda k, ref=ref: ref.at[:, :, pl.ds(k * wide, wide)],
-            lambda role, j, into=into: into.at[role, j],
-            sems,
-        )
-        for layer, ref, into, sems in ((0, f_grad, f_in, f_sems), (1, a_grad, a_in, a_sems))
-    ]
-    count = pushes[0].greet() + pushes[1].greet()
-    pl.semaphore_wait(pltpu.get_barrier_semaphore(), count)
-    for push in pushes:
-        push.start()
-    attend_back_body(
-        qkv_ref, seg_ref, att_ref, lse_ref, dout_ref, cos_ref, sin_ref, extra_ref, dqkv_ref, None, *scratch
-    )
-    for push in pushes:
-        push.finish()
 
 
 def number_of(y, s, z):
@@ -1587,131 +1875,124 @@
     tables = [jnp.cos(angles), jnp.sin(angles)]
     a_own = jnp.stack([w_query[0].T, w_key[0].T, w_value[0].T, w_out[0]])
     f_own = jnp.stack([w_gate[0].T, w_up[0].T, w_down[0]])
-    buf = [pltpu.VMEM((16, rows, width), LOW)]
+    dma = pltpu.SemaphoreType.DMA
+
+    def vmem(*shape, dtype=LOW):
+        return pltpu.VMEM(shape, dtype)
+
+    def near(*shape, dtype=LOW):
+        return (shape, dtype, False)
+
+    def stays(*shape, dtype=LOW):
+        return (shape, dtype, True)
+
+    buf = [vmem(16, rows, width)]
     boxes = sum_boxes(rows, width)
-    dma = pltpu.SemaphoreType.DMA
-    every = ((16, rows, width), LOW, True)
-    turned_out = ((3 * HS, length), LOW, False)
-    hidden_out = ((length, units), LOW, False)
-    block_out = ((rows, width), F32, False)
-    low_out = ((rows, width), LOW, False)
-    gain_out = ((1, width), F32, False)
-    dout_out = ((HS, length), LOW, False)
-    head_out = ((HS, length), F32, False)
-    flat_out = ((length, HS), LOW, False)
-    lse_out = ((1, length), F32, False)
-    f_out = ((3, units, width), LOW, False)
-    wo_out = ((HS, width), LOW, False)
-    f_far = ((3, units, width), LOW, True)
-    a_far = ((4, HS, width), LOW, True)
-    a_shards = ((2, 4, 4, HS, width // 4), LOW, True)
-    f_shards = ((2, 4, 3, units, width // 4), LOW, True)
-    hidden_scratch = pltpu.VMEM((length, units), LOW)
-    f_sum = [pltpu.VMEM((3, units, width), F32), pltpu.VMEM((HS, width), F32)]
-    in_sum = [pltpu.VMEM((3 * HS, width), F32)]
-
-    home_out = ((2, rows, width), LOW, True)
-    qkv0, att0, flat0, lse0, own_in, normed0, a0, a1, f0, f1, gains = reach(
-        first_kernel,
-        0,
-        [*tables, segment],
-        [turned_out, head_out, flat_out, lse_out, ((rows, width), LOW, True), every, a_far, a_far, f_far, f_far]
-        + [((2, 2, width), F32, True)],
-        buf
-        + [pltpu.VMEM((rows, width), LOW), pltpu.VMEM((3 * HS, width), LOW), pltpu.VMEM((2, width), F32)]
-        + attend_scratch(length)
-        + [links(), dma((16,)), head_sems(), head_sems(), head_sems(), head_sems(), dma((3,)), dma((3,)), dma((5,))],
-        "first",
-        [inputs, a_own, f_own, jnp.concatenate([attn_gain, mlp_gain])],
-    )
+    small_boxes = sum_boxes(HS, width)
+    wo_buf = [vmem(16, HS, width)]
+    low_head = [vmem(HS, length)]
+    block, low_block = [vmem(rows, width, dtype=F32)], [vmem(rows, width)]
+    hidden = [vmem(length, units)] * 3
+    dout_block = [vmem(16, HS, rows)]
+    in_sum = [vmem(3 * HS, width, dtype=F32), vmem(4, HS, width)]
+    turned_out, head_out, lse_out = near(3 * HS, length), near(HS, length, dtype=F32), near(1, length, dtype=F32)
+    att_in_out, every = near(16, HS, rows), stays(16, rows, width)
+    block_out, low_out, gain_out = near(rows, width, dtype=F32), near(rows, width), near(1, width, dtype=F32)
+    dout_out, f_out = near(HS, length), near(3, units, width)
+    hidden_far, home_out = stays(length, units), stays(2, rows, width)
+    a_far, f_far = stays(4, HS, width), stays(3, units, width)
+    f_half = stays(4, 3, units, width // 4)
+    a_shards, f_shards = stays(2, 4, 4, HS, width // 4), stays(2, 4, 3, units, width // 4)
+
     both = lax.dynamic_index_in_dim(cotangent, 1 - half, 0, keepdims=False)
     own_top = jnp.where(
         far,
         lax.ppermute(both, AXES, far_pairs()),
         lax.dynamic_index_in_dim(cotangent, half, 0, keepdims=False),
     )
+    (
+        qkv0, att0, lse0, att_in0, wo_all0, own_in, mid0, out0, qkv1,
+        normed0, nmid0, normed1, hid0, one0, two0, home_out0, a0, a1, f0, f1, gains, *_,
+    ) = reach(
+        first_kernel,
+        0,
+        [*tables, segment],
+        [turned_out, head_out, lse_out, att_in_out, near(16, HS, width), low_out, block_out, low_out, turned_out]
+        + [every] * 3
+        + [hidden_far] * 3
+        + [home_out, a_far, a_far, f_far, f_far, stays(2, 2, width, dtype=F32)]
+        + [stays(2, 4, HS, width // 4)] * 2
+        + [stays(2, 3, units, width // 4)] * 2,
+        buf
+        + low_head
+        + [vmem(4, HS, width), vmem(3, units, width), vmem(2, 2, width, dtype=F32)]
+        + hidden
+        + attend_scratch(length)
+        + boxes
+        + [links(), links(), links(), row_sems(), dma((16,))]
+        + [head_sems()] * 4
+        + [dma((3,)), dma((3,)), dma((7,)), home_sems()],
+        "first",
+        [inputs, a_own, f_own, jnp.concatenate([attn_gain, mlp_gain])],
+    )
     gain_in, gain_mid = [gains[i, 0:1] for i in range(2)], [gains[i, 1:2] for i in range(2)]
-    w_in = [a[:3].reshape(3 * HS, width) for a in (a0, a1)]
-    w_back = [a[3] for a in (a0, a1)]
-
-    mid0, out0, hid0, one0, two0, qkv1, nmid0, normed1, home_out0 = reach(
-        middle_kernel,
-        2,
-        [flat0, own_in, w_back[0], f0, gain_mid[0], gain_in[1], w_in[1], *tables, qkv0[2 * HS :]],
-        [block_out, low_out, hidden_out, hidden_out, hidden_out, turned_out, every, every, home_out],
-        buf + boxes + [links(), links(), dma((16,)), home_sems()],
-        "middle",
-    )
-    att1, flat1, lse1 = reach(
-        attend_body, None, [qkv1, segment], [head_out, flat_out, lse_out], attend_scratch(length), "attend"
-    )
-    dmid1, gmid1, dout1, f_grad1, wo_grad1, home_out1 = reach(
+    att1, lse1, att_in1, dmid1, gmid1, dout1, f_grad1, mid1, hid1 = reach(
         turn_kernel,
-        3,
-        [flat1, out0, w_back[1], f1, gain_mid[1], own_top],
-        [block_out, gain_out, dout_out, f_out, wo_out, home_out],
+        1,
+        [qkv1, segment, a1, f1, gain_mid[1], out0, own_top],
+        [head_out, lse_out, att_in_out, block_out, gain_out, dout_out, f_out, block_out, hidden_far],
         buf
         + buf
-        + [pltpu.VMEM((rows, width), LOW)]
+        + wo_buf
+        + low_head
+        + dout_block
         + boxes
-        + [pltpu.VMEM((rows, width), F32)]
-        + [hidden_scratch] * 3
-        + f_sum
-        + [links(), links(), home_sems()],
+        + [links(), links(), links(), row_sems(), row_sems(), dma((1,))],
         "turn",
     )
-    dqkv1, extra, f_in1 = reach(
-        attend_back_upper,
-        9,
-        [qkv1, segment, att1, lse1, dout1, *tables],
-        [turned_out, head_out, f_shards],
-        attend_back_scratch(length) + [shard_sems()],
-        "attend_back",
-        [f_grad1],
-    )
-    gin1, in_grad1, dmid0, gmid0, dout0, f_grad0, wo_grad0, home_grad1 = reach(
+    extra, gin1, dmid0, gmid0, dout0, f_grad0, a_grad1, home_grad1, home_out1, f_far1 = reach(
         lower_kernel,
-        4,
-        [dqkv1, out0, w_in[1], gain_in[1], dmid1, f0, w_back[0], flat0, gain_mid[0], mid0],
-        [gain_out, ((3 * HS, width), LOW, False), block_out, gain_out, dout_out, f_out, wo_out, home_out],
+        2,
+        [a1, gain_in[1], dmid1, att_in1, gain_mid[0]],
+        [head_out, gain_out, block_out, gain_out, dout_out, f_out, near(4, HS, width), home_out, home_out, f_half],
         buf
-        + buf
-        + [pltpu.VMEM((rows, width), F32), pltpu.VMEM((rows, width), LOW)]
+        + wo_buf
+        + [vmem(3 * HS, length)]
+        + low_block
+        + low_block
+        + in_sum[:1]
+        + dout_block
         + boxes
-        + [hidden_scratch] * 3
-        + f_sum
+        + small_boxes
+        + [links(), links(), links(), row_sems(), shard_sems(), home_sems(), home_sems()]
+        + [dma((18,)), dma((8,))],
+        "lower",
+        [out0, f0, mid0, qkv1, segment, att1, lse1, dout1, *tables, hid0, one0, two0, normed1, nmid0, wo_all0]
+        + [hid1, mid1, f1, f_grad1],
+    )
+    home_grad0, f_in0, f_near1, a_in0, a_in1, gain_sums = reach(
+        last_kernel,
+        3,
+        [qkv0, segment, att0, lse0, dout0, *tables, extra, own_in, a0, gain_in[0], dmid0, att_in0]
+        + [jnp.concatenate([gin1, gmid0, gmid1])],
+        [home_out, f_shards, f_half, a_shards, a_shards, near(6, 4, width, dtype=F32)],
+        buf
+        + [vmem(3 * HS, length)]
+        + low_block
         + in_sum
-        + [links(), links(), dma((5,)), home_sems()],
-        "lower",
-        [hid0, one0, two0, normed1, nmid0],
-    )
-    a_grad1 = jnp.concatenate([in_grad1, wo_grad1]).reshape(4, HS, width)
-    dqkv0, f_in0, a_in1 = reach(
-        attend_back_lower,
-        10,
-        [qkv0, segment, att0, lse0, dout0, *tables, extra],
-        [turned_out, f_shards, a_shards],
-        attend_back_scratch(length) + [shard_sems(), shard_sems()],
-        "attend_back",
-        [f_grad0, a_grad1],
-    )
-    home_grad0, a_in0, gain_sums = reach(
-        last_kernel,
-        5,
-        [dqkv0, own_in, w_in[0], gain_in[0], dmid0, wo_grad0, jnp.concatenate([gin1, gmid0, gmid1])],
-        [home_out, a_shards, ((6, 4, width), F32, False)],
-        buf
+        + [vmem(1, width, dtype=F32), vmem(5, 4, width, dtype=F32)]
+        + attend_back_scratch(length)
         + boxes
-        + in_sum
-        + [pltpu.VMEM((4, HS, width), LOW), pltpu.VMEM((rows, width), LOW), pltpu.VMEM((1, width), F32)]
-        + [pltpu.VMEM((5, 4, width), F32)]
-        + [links(), dma((1,)), home_sems(), shard_sems(), dma((2, 5))],
+        + small_boxes
+        + [links(), links()]
+        + [shard_sems()] * 4
+        + [home_sems(), dma((2, 5)), dma((1,))],
         "last",
-        [normed0],
+        [f_grad0, f_grad1, a_grad1, normed0],
     )
     on_first = y == 0
     a_sum = jnp.sum(jnp.where(on_first, a_in0, a_in1).astype(F32), axis=0)
-    f_total = jnp.sum(jnp.where(on_first, f_in0, f_in1).astype(F32), axis=0)
+    f_total = jnp.where(on_first, f_in0[0], f_near1).astype(F32) + jnp.where(on_first, f_in0[1], f_far1).astype(F32)
     a_sum = jnp.transpose(a_sum, (1, 0, 2, 3)).reshape(4, 4 * HS, width // 4)
     f_total = jnp.transpose(f_total, (1, 0, 2, 3)).reshape(3, 4 * units, width // 4)
     layer_out = jnp.where(on_first, home_out0, home_out1)

time: 825 us -> 710 us (0.86)
  Pallas kernels: 782 us -> 677 us
    pallas_call x8 -> x4, Pallas kernels: 782 us -> 677 us  [reach(): pl.pallas_call(kernel, out_shape=[jax.ShapeDtypeStruct(shape, dtype) for...]
  transfers between devices with their start and end apart: 1 -> 1, of which waited for: 0 -> 0; matrix products, arithmetic and copies ran while one was open for 2% -> 1% of each run, Pallas kernels for 35% -> 34%
where the time goes in v3:
time: 710 us; the launch traced here: 701 us
  Pallas kernels  677 us (95%)
  other arithmetic  12.7 us (2%)
  local copies, waits for them, and re-layouts  8.88 us (1%)
    pallas_call x4, Pallas kernels, reach(): pl.pallas_call(kernel, out_shape=[jax.ShapeDtypeStruct(shape, dtype) for...  677 us
  transfers between devices with their start and end apart: 1, of which 0 were waited for; matrix products, arithmetic and copies ran while one was open for 1% of the time, Pallas kernels for 34%

profile of v3, /device:TPU:0, one launch (start us, length us, event | category | flops | bytes accessed | tf_op | source)
XLA Modules:
  0.0 700.6 jit_solution(4589726117957571997)
XLA Ops:
  0.6 0.0 copy-start.14
  0.7 0.0 copy-start.15
  0.7 0.0 copy-start.10
  0.7 0.0 copy-start.11
  0.7 0.0 copy-start.12
  0.7 0.0 copy-start.13
  0.7 1.2 dynamic-slice_bitcast_fusion
  1.9 0.0 copy-start.7
  1.9 0.0 copy-start.8
  1.9 0.0 copy-start.9
  1.9 0.8 collective-permute-start
  2.8 0.7 fusion.3
  3.5 0.2 reduce-window.4
  3.7 0.7 fusion.2
  4.3 0.1 convert_reduce_fusion.1
  4.5 0.1 select_reduce_fusion
  4.6 2.8 multiply_sine_fusion
  7.4 0.0 copy-done.14
  7.4 0.0 copy-done.15
  7.4 0.0 copy-done.10
  7.4 0.1 copy.41
  7.5 0.0 copy-done.11
  7.5 0.1 copy.42
  7.7 0.0 copy-done.12
  7.7 0.1 copy.43
  7.8 0.0 copy-done.13
  7.8 0.9 pad_maximum_fusion.1.a_ref
  8.6 0.0 copy-done.7
  8.6 0.0 copy-done.8
  8.7 0.0 copy-done.9
  8.7 1.1 pad_maximum_fusion.f_ref
  9.8 0.0 copy-start.3
  9.8 240.1 %first.1 = (bf16[192,4096]{1,0:T(8,128)(2,1)}, f32[64,4096]{1,0:T(8,128)}, f32[1,4096]{1,0:T(1,128)S(1)}, bf16[16,64,256]{2,1,0:T(8,128)(2,1)}, bf16[16,64,1024]...) custom-call(f32[32,4096]{1,0:T(8,128)} %get-tuple-element.144.cos_re, ...), custom_call_target="tpu_custom_call" | custom-call | tf_op jit(solution)/shard_map/first/pallas_call | solution.py:1646
  249.9 0.0 collective-permute-done
  249.9 0.0 copy-done.3
  249.9 0.9 bitcast_select_fusion.2.top_ref
  250.8 134.3 %turn.1 = (f32[64,4096]{1,0:T(8,128)}, f32[1,4096]{1,0:T(1,128)S(1)}, bf16[16,64,256]{2,1,0:T(8,128)(2,1)S(1)}, f32[256,1024]{1,0:T(8,128)}, f32[1,1024]{1,0:T(1...) custom-call(bf16[192,4096]{1,0:T(8,128)(2,1)} %get-tuple-element.60., ...), custom_call_target="tpu_custom_call" | custom-call | tf_op jit(solution)/shard_map/turn/pallas_call | solution.py:1646
  385.0 0.0 copy-start
  385.0 0.8 copy-done
  385.8 194.1 %lower.1 = (f32[64,4096]{1,0:T(8,128)}, f32[1,1024]{1,0:T(1,128)S(1)}, f32[256,1024]{1,0:T(8,128)}, f32[1,1024]{1,0:T(1,128)S(1)}, bf16[64,4096]{1,0:T(8,128)(2,...) custom-call(bf16[4,64,1024]{2,1,0:T(8,128)(2,1)} %get-tuple-element., ...), custom_call_target="tpu_custom_call" | custom-call | tf_op jit(solution)/shard_map/lower/pallas_call | solution.py:1646
  579.9 108.5 %last.1 = (bf16[2,256,1024]{2,1,0:T(8,128)(2,1)}, bf16[2,4,3,176,256]{4,3,2,1,0:T(8,128)(2,1)}, bf16[4,3,176,256]{3,2,1,0:T(8,128)(2,1)}, bf16[2,4,4,64,256]{4,3...) custom-call(bf16[192,4096]{1,0:T(8,128)(2,1)} %get-tuple-element.80.qkv_ref, ...), custom_call_target="tpu_custom_call" | custom-call | tf_op jit(solution)/shard_map/last/pallas_call | solution.py:1646
  688.5 0.1 constant_dynamic-slice_fusion
  688.6 0.5 fusion.1
  689.1 0.0 copy-start.2
  689.1 1.8 convert_reduce_fusion
  690.9 0.0 copy-start.1
  690.9 0.9 fusion.5
  691.8 1.8 copy.46
  693.6 0.0 copy-done.2
  693.6 0.0 copy-done.1
  693.6 0.5 add_bitcast_fusion
  694.1 0.0 copy-start.4
  694.1 0.0 copy-start.6
  694.2 1.4 fusion.4
  695.5 0.0 copy-start.5
  695.5 0.0 copy-done.4
  695.5 0.8 copy.45
  696.4 0.8 copy.44
  697.2 0.0 copy-done.6
  697.2 0.0 copy-done.5
  697.2 3.1 bitcast_convert_fusion
  (6 shorter events, 0.1 us)
Async XLA Ops:
  0.6 6.7 copy-start.14
  0.7 6.7 copy-start.15
  0.7 6.8 copy-start.10
  0.7 6.9 copy-start.11
  0.7 7.0 copy-start.12
  0.7 7.1 %copy-start.13 = (bf16[1,256,256]{2,1,0:T(8,128)(2,1)S(1)}, bf16[1,256,256]{2,1,0:T(8,128)(2,1)}, u32[]{:S(2)}) copy-start(bf16[1,256,256]{2,1,0:T(8,128)(2,1)} %param.18) | copy-start | bytes 393220
  1.9 6.8 copy-start.7
  1.9 6.8 copy-start.8
  1.9 6.7 copy-start.9
  1.9 248.0 %collective-permute-start = (bf16[256,1024]{1,0:T(8,128)(2,1)S(1)}, bf16[256,1024]{1,0:T(8,128)(2,1)S(1)}, u32[]{:S(2)}, u32[]{:S(2)}) collective-permute-start(bf16[256,1024]{1,0:T(8,128)(2,1)S(1)} %dynamic-slice_bitcast_fusion), channel_id=1, source_target_pairs={{4,6},{5,7},{6,4},{7,5},{12,14},{13,15},{14,12},{15,13},{16,18},{1... | collective-permute-start | bytes 1572872 | tf_op jit(solution)/shard_map/ppermute | solution.py:1910
  9.8 240.1 %copy-start.3 = (bf16[2,256,1024]{2,1,0:T(8,128)(2,1)S(1)}, bf16[2,256,1024]{2,1,0:T(8,128)(2,1)}, u32[]{:S(2)}) copy-start(bf16[2,256,1024]{2,1,0:T(8,128)(2,1)} %param.13) | copy-start | bytes 3145732
  385.0 0.8 copy-start
  689.1 4.5 copy-start.2
  690.9 2.7 copy-start.1
  694.1 1.4 copy-start.4
  694.1 3.1 copy-start.6
  695.5 1.7 copy-start.5

commit v4 on v3

--- a/solution.py
+++ b/solution.py
@@ -519,7 +519,12 @@
 
 
 def far_role(at):
-    return flip(at[0], at[2])
+    return flip(flip(at[0], at[2]), at[3])
+
+
+def partner_of(at):
+    y, x, c, h, p = at
+    return (y, x, c, 1 - h, p)
 
 
 def lane_of(at):
@@ -776,7 +781,7 @@
     def copy(self, b):
         lane, (y, x, c, h, p) = b % 4, self.at
         x, c = b // 8, (b // 4) % 2
-        home = (flip(flip(h, lane // 2), c), x, c, h, lane % 2)
+        home = ((c + lane // 2) % 2, x, c, h, lane % 2)
         return remote(self.block(b), self.place(self.mine), self.send.at[b], self.recv.at[self.mine], home)
 
     def start(self, b):
@@ -816,9 +821,9 @@
 
 
 class ToHeads:
-    def __init__(self, at, layer, piece, place, relay, sems):
-        self.at, self.layer, self.piece, self.place, self.relay = at, layer, piece, place, relay
-        self.send, self.recv, self.local, self.relay_send, self.relay_recv = sems
+    def __init__(self, at, layer, piece, place, sems):
+        self.at, self.layer, self.piece, self.place = at, layer, piece, place
+        self.send, self.recv, self.local, self.forth = sems
         y, x, c, h, p = at
         self.s = 2 * x + c
         self.sends = same(y, layer)
@@ -828,100 +833,63 @@
         return self.sends * self.near * same(self.s, j)
 
     def greet(self):
-        y, x, c, h, p = self.at
-        source = self.near * self.layer + (1 - self.near) * y
+        h, p = self.at[3], self.at[4]
         for k in range(4):
 
-            @pl.when(self.is_me(k) == 0)
+            @pl.when(self.near - self.is_me(k) == 1)
             def _(k=k):
-                signal((source, k // 2, k % 2, flip(h, 1 - self.near), p))
-
-        return 2 + self.sends * (4 - self.near)
-
-    def near_copy(self, j):
+                signal((self.layer, k // 2, k % 2, h, p))
+
+        return self.sends * (4 - self.near)
+
+    def copy(self, j):
         h, p = self.at[3], self.at[4]
-        home = (j % 2, j // 2, j % 2, h, p)
+        home = (flip(h, j % 2), j // 2, j % 2, h, p)
         return remote(self.piece(j), self.place(self.s), self.send.at[j], self.recv.at[self.s], home)
 
-    def far_copy(self, src, i, j):
-        h, p = self.at[3], self.at[4]
-        home = (1 - j % 2, j // 2, j % 2, 1 - h, p)
-        return remote(src, self.place(self.s), self.send.at[4 + i], self.recv.at[self.s], home)
-
-    def direct(self, i):
-        j = 2 * i + 1 - self.layer
-        return self.far_copy(self.piece(j), i, j)
-
-    def relayed(self, i):
-        return self.far_copy(self.relay.at[i], i, 2 * i + self.layer)
-
-    def to_twin(self, i):
-        y, x, c, h, p = self.at
-        return remote(
-            self.piece(2 * i + self.layer),
-            self.relay.at[i],
-            self.relay_send.at[i],
-            self.relay_recv.at[i],
-            (1 - self.layer, x, c, h, p),
-        )
-
-    def start_relay(self):
-        @pl.when(self.sends == 1)
-        def _():
-            for i in range(2):
-                self.to_twin(i).start()
+    def on(self, k):
+        return remote(self.place(k), self.place(k), self.forth.at[k], self.recv.at[k], partner_of(self.at))
 
     def start(self):
-        @pl.when(self.sends == 1)
-        def _():
-            for i in range(2):
-                self.direct(i).start()
-
         for j in range(4):
 
             @pl.when(self.sends - self.is_me(j) == 1)
             def _(j=j):
-                self.near_copy(j).start()
+                self.copy(j).start()
 
             @pl.when(self.is_me(j) == 1)
             def _(j=j):
                 pltpu.make_async_copy(self.piece(j), self.place(j), self.local).start()
 
     def forward(self):
-        @pl.when(self.sends == 0)
-        def _():
-            for i in range(2):
-                self.to_twin(i).wait_recv()
-                self.relayed(i).start()
+        for k in range(4):
+
+            @pl.when(self.near - self.is_me(k) == 1)
+            def _(k=k):
+                self.on(k).wait_recv()
+
+            @pl.when(self.is_me(k) == 1)
+            def _(k=k):
+                pltpu.make_async_copy(self.piece(k), self.place(k), self.local).wait()
+
+            @pl.when(self.near == 1)
+            def _(k=k):
+                self.on(k).start()
 
     def finish(self):
         for k in range(4):
-            dst = self.place(k)
-
-            @pl.when(self.is_me(k) == 0)
-            def _(k=k, dst=dst):
-                remote(dst, dst, self.send.at[0], self.recv.at[k], self.at).wait_recv()
-
-            @pl.when(self.is_me(k) == 1)
-            def _(k=k, dst=dst):
-                pltpu.make_async_copy(self.piece(k), dst, self.local).wait()
-
-        @pl.when(self.sends == 0)
-        def _():
-            for i in range(2):
-                self.relayed(i).wait_send()
-
-        @pl.when(self.sends == 1)
-        def _():
-            for i in range(2):
-                self.direct(i).wait_send()
-                self.to_twin(i).wait_send()
-
-        for j in range(4):
-
-            @pl.when(self.sends - self.is_me(j) == 1)
-            def _(j=j):
-                self.near_copy(j).wait_send()
+
+            @pl.when(self.near == 0)
+            def _(k=k):
+                self.on(k).wait_recv()
+
+            @pl.when(self.near == 1)
+            def _(k=k):
+                self.on(k).wait_send()
+
+            @pl.when(self.sends - self.is_me(k) == 1)
+            def _(k=k):
+                self.copy(k).wait_send()
 
 
 class ToShards:
@@ -944,13 +912,13 @@
 
                 @pl.when(self.gets == 1)
                 def _(j=j):
-                    signal((1 - j % 2, j // 2, j % 2, 1 - h, p))
+                    signal((flip(h, j % 2), j // 2, j % 2, 1 - h, p))
 
             if 0 in self.roles:
 
                 @pl.when(self.gets - self.is_me(j) == 1)
                 def _(j=j):
-                    signal((j % 2, j // 2, j % 2, h, p))
+                    signal((flip(h, j % 2), j // 2, j % 2, h, p))
 
         return self.active * (4 - self.gets * (1 - self.role))
 
@@ -1003,8 +971,7 @@
 
     def holder(self, micro):
         y, x, c, h, p = self.at
-        role = flip(h, micro)
-        return (flip(role, c), x, c, micro, p), (1 - role) * self.is_me
+        return (flip(h, c), x, c, micro, p), (1 - flip(h, micro)) * self.is_me
 
     def greet(self):
         for micro in range(2):
@@ -1057,7 +1024,7 @@
 
 def head_sems():
     dma = pltpu.SemaphoreType.DMA
-    return (dma((6,)), dma((4,)), dma, dma((2,)), dma((2,)))
+    return (dma((4,)), dma((4,)), dma, dma((4,)))
 
 
 def shard_sems():
@@ -1252,50 +1219,42 @@
 def first_kernel(
     cos_ref, sin_ref, seg_ref, in_ref, a_ref, f_ref, gain_ref,
     qkv0_ref, att_ref, lse_ref, att_in, wo_all, x_here, middle_ref, out_ref, qkv1_ref,
-    normed0_far, nmid_far, normed1_far, hidden_far, one_far, two_far, home_ref, a0, a1, f0, f1, gains, a0_relay, a1_relay, f0_relay, f1_relay,
+    normed0_far, nmid_far, normed1_far, hidden_far, one_far, two_far, a0, a1, f0, f1, gains,
     buf, low_ref, a_here, f_here, gain_here, hidden_ref, one_ref, two_ref,
     key_x, query_x, val_x, scores, total, out_c, in_c, rin,
     ag_sems, wo_sems, rs_sems, share_sems, block_sems, a0_sems, a1_sems, f0_sems, f1_sems, swap, gain_sems, loads,
-    homing,
 ):
     at = spot()
     y, x, c, h, p = at
     rows = x_here.shape[0]
     far = far_role(at)
     stage = Stage(loads)
-    partner, above = (y, x, c, 1 - h, p), (1 - y, x, c, h, p)
+    partner, above = partner_of(at), (1 - y, x, c, h, p)
     size = f_ref.shape[1] // 4
     a_pushes = [
-        ToHeads(at, layer, slices(a_ref, HS), columns(into), relay, sems)
-        for layer, into, relay, sems in ((0, a0, a0_relay, a0_sems), (1, a1, a1_relay, a1_sems))
+        ToHeads(at, layer, slices(a_ref, HS), columns(into), sems)
+        for layer, into, sems in ((0, a0, a0_sems), (1, a1, a1_sems))
     ]
     f_pushes = [
-        ToHeads(at, layer, slices(f_ref, size), columns(into), relay, sems)
-        for layer, into, relay, sems in ((0, f0, f0_relay, f0_sems), (1, f1, f1_relay, f1_sems))
+        ToHeads(at, layer, slices(f_ref, size), columns(into), sems)
+        for layer, into, sems in ((0, f0, f0_sems), (1, f1, f1_sems))
     ]
-    home = ToHome(at, 0, out_ref, lambda m: home_ref.at[m], homing)
     share = ToRows(at, lambda b: low_ref.at[:, pl.ds(b * rows, rows)], lambda b: att_in.at[b], share_sems)
-    greet(at, *a_pushes, *f_pushes, home, peers=(partner,))
+    greet(at, *a_pushes, *f_pushes, peers=(partner,))
     swapped = remote(in_ref.at[1 - h], x_here, swap.at[0], swap.at[1], partner)
     stays = pltpu.make_async_copy(in_ref.at[h], x_here, swap.at[2])
 
-    @pl.when(far == 1)
+    @pl.when(far == 0)
     def _():
         swapped.start()
-
-    @pl.when(far == 0)
-    def _():
         stays.start()
 
     across = remote(gain_ref, gains.at[y], gain_sems.at[0], gain_sems.at[1], above)
     across.start()
     keeps = pltpu.make_async_copy(gain_ref, gains.at[y], gain_sems.at[2])
     keeps.start()
-    for push in a_pushes:
-        push.start_relay()
-    a_pushes[0].start()
-    for push in f_pushes:
-        push.start_relay()
+    for push in (a_pushes[0], f_pushes[0], a_pushes[1], f_pushes[1]):
+        push.start()
     a_pushes[0].forward()
     keeps.wait()
     across.wait_send()
@@ -1304,11 +1263,12 @@
 
     @pl.when(far == 1)
     def _():
-        swapped.wait()
+        swapped.wait_recv()
 
     @pl.when(far == 0)
     def _():
         stays.wait()
+        swapped.wait_send()
 
     gain_copy.wait()
     buf[block_of(at)] = (unit_of(x_here[...].astype(F32))[0] * gain_here[0, 0:1]).astype(LOW)
@@ -1316,14 +1276,12 @@
     def ready():
         a_pushes[0].finish()
         copy = stage.copy(a0, a_here)
-        for push in (a_pushes[1], f_pushes[0]):
-            push.start()
-            push.forward()
         copy.wait()
 
     keep = (normed0_far, block_sems)
     gather(at, buf, ag_sems, lambda b: project_block(b, buf, a_here, cos_ref, sin_ref, None, qkv0_ref), keep, ready)
     wo_all[block_of(at)] = a_here[3]
+    f_pushes[0].forward()
     attend_and_share(
         at, gathering(at, wo_all, wo_sems), share, lambda: kept(buf, keep),
         qkv0_ref, seg_ref, att_ref, low_ref, lse_ref, key_x, query_x, val_x, scores,
@@ -1336,7 +1294,7 @@
     def more():
         f_pushes[0].finish()
         copy = stage.copy(f0, f_here)
-        f_pushes[1].start()
+        a_pushes[1].forward()
         f_pushes[1].forward()
         copy.wait()
 
@@ -1348,7 +1306,6 @@
     )
     out = (middle_ref[...] + total[...]).astype(LOW)
     out_ref[...] = out
-    home.start()
     buf[block_of(at)] = (unit_of(out.astype(F32))[0] * gain_here[1, 0:1]).astype(LOW)
     keep = (normed1_far, block_sems)
 
@@ -1363,7 +1320,6 @@
     kept(buf, keep)
     for save in saves:
         save.wait()
-    home.finish()
     f_pushes[1].finish()
 
 
@@ -1428,7 +1384,8 @@
             return none
 
         lax.fori_loop(0, 16, one, 0)
-        after()
+        if after is not None:
+            after()
 
     def partial(b):
         return dot(dqkv_ref[:, span(b, rows)], a_ref[:3].reshape(3 * HS, width), TN)
@@ -1454,15 +1411,17 @@
     run(steps)
 
 
-def out_weight_steps(at, total, boxes, sems, att_in, dmid_ref, low_ref):
-    low_ref[...] = dmid_ref[...].astype(LOW)
-    return scattering(at, total, boxes, sems, lambda b: dot(att_in[b], low_ref[...]))
+def meet(at, sem):
+    for mask, core in ((1, 0), (2, 0), (4, 0), (0, 1)):
+        peer = device(moved(at, mask, core))
+        pl.semaphore_signal(sem, inc=1, device_id=peer, device_id_type=MESH_ID)
+    pl.semaphore_wait(sem, 4)
 
 
 def put_grads(a_grad_ref, in_sum_ref, out_total):
     for i in range(3):
         a_grad_ref[i] = in_sum_ref[i * HS : (i + 1) * HS].astype(LOW)
-    a_grad_ref[3] = out_total[...].astype(LOW)
+    a_grad_ref[3] = out_total.astype(LOW)
 
 
 def by_columns(ref):
@@ -1471,13 +1430,14 @@
 
 
 def lower_kernel(
-    a_ref, gain_in_ref, dmid_above, att_in, gain_mid_ref,
+    a_ref, gain_in_ref, dmid_above, gain_mid_ref,
     x_far, f_far, middle_far, qkv_far, seg_far, att_far, lse_far, dout_far, cos_far, sin_far,
     hidden_far, one_far, two_far, normed_far, nmid_far, wo_far, hidden_above, middle_above, f_above, f_grad_above,
-    send_ref, gain_in_grad_ref, dmid_ref, gain_mid_grad_ref, dout_ref, f_grad_ref, a_grad_ref, home_ref, out_home, f_in_far,
-    buf, wo_all, dqkv_ref, low_ref, out_ref, in_sum_ref, dout_block,
-    total, out_c, in_c, rin, out_total, out_c2, in_c2, rin2,
-    ag_sems, rs_sems, rs2_sems, back_sems, f_sems, homing, out_homing, loads, ring_sems,
+    out_below,
+    send_ref, gain_in_grad_ref, dmid_ref, gain_mid_grad_ref, dout_ref, f_grad_ref, in_grad_ref, low_ref, out_ref, out_home, f_heard,
+    buf, wo_all, dqkv_ref, in_sum_ref, dout_block,
+    total, out_c, in_c, rin,
+    ag_sems, rs_sems, back_sems, heard_sems, out_homing, loads, ring_sems, meeting,
 ):
     at = spot()
     rows = low_ref.shape[0]
@@ -1485,17 +1445,22 @@
     normed_copy = stage.copy(normed_far, buf)
     wo_copy = stage.copy(wo_far, wo_all)
     length = dqkv_ref.shape[1]
-    home = ToHome(at, 1, low_ref, lambda m: home_ref.at[m], homing)
-    out = ToHome(at, 1, out_ref, lambda m: out_home.at[m], out_homing)
+    home = ToHome(at, 0, out_below, lambda m: out_home.at[m], out_homing)
+    far = far_role(at)
+    push = remote(f_grad_above, f_heard, heard_sems.at[0], heard_sems.at[1], partner_of(at))
 
     def column(b):
         start = b * rows
         return dout_ref.at[:, pl.ds(start if isinstance(b, int) else pl.multiple_of(start, rows), rows)]
 
     back = ToRows(at, lambda b: dout_block.at[b], column, back_sems)
-    push = ToShards(at, 1, by_columns(f_grad_above), lambda role, j: f_in_far.at[j], f_sems, (1,))
-    greet(at, home, out, push)
-    push.start()
+    greet(at, home, peers=(partner_of(at),))
+
+    @pl.when(far == 1)
+    def _():
+        push.start()
+
+    home.start()
     boxes = (out_c, in_c, rin)
 
     def out_steps(hidden_ref, down_ref):
@@ -1503,12 +1468,6 @@
             at, total, boxes, rs_sems, lambda b: dot(hidden_ref[span(b, rows)], down_ref[...])
         )
         out_ref[...] = (dmid_ref[...] + total[...]).astype(LOW)
-        out.start()
-
-    def weight_steps():
-        for _ in range(5):
-            yield
-        yield from out_weight_steps(at, out_total, (out_c2, in_c2, rin2), rs2_sems, att_in, dmid_above, low_ref)
 
     def attention(hidden_ref, down_ref, *refs):
         copies = [
@@ -1517,7 +1476,7 @@
         ]
         for copy in copies:
             copy.wait()
-        steps = taking_turns(out_steps(hidden_ref, down_ref), weight_steps())
+        steps = out_steps(hidden_ref, down_ref)
         attend_back_staged(
             stage, (qkv_far, seg_far, att_far, lse_far, dout_far, cos_far, sin_far), (None, dqkv_ref, send_ref),
             steps, 3, *refs,
@@ -1531,8 +1490,7 @@
         *attend_back_scratch(length),
     )
 
-    def after():
-        put_grads(a_grad_ref, in_sum_ref, out_total)
+    meet(at, meeting)
 
     def rest(hidden_ref, one_ref, two_ref, sums_ref, x_ref, f_ref, middle_ref, ring):
         blocks = streamed(nmid_far, ring, ring_sems)
@@ -1548,11 +1506,11 @@
         copies.pop(0).wait()
         grad = input_back(
             at, dqkv_ref, a_ref, x_ref, gain_in_ref, dmid_above, gain_in_grad_ref, total, boxes, rs_sems, buf,
-            normed_copy, in_sum_ref, after,
+            normed_copy, in_sum_ref, None,
         )
         dmid_ref[...] = grad
         low_ref[...] = grad.astype(LOW)
-        home.start()
+        in_grad_ref[...] = in_sum_ref[...].astype(LOW)
         for copy in copies + [wo_copy]:
             copy.wait()
         down_back(
@@ -1564,45 +1522,93 @@
     ring_type = pltpu.VMEM((8, *nmid_far.shape[1:]), LOW)
     pl.run_scoped(rest, *feed_scratch(length, f_far), *staged_scratch((x_far, f_far, middle_far)), ring_type)
     home.finish()
-    out.finish()
-    push.finish()
+
+    @pl.when(far == 1)
+    def _():
+        push.wait_send()
+
+    @pl.when(far == 0)
+    def _():
+        push.wait_recv()
 
 
 def last_kernel(
     qkv_ref, seg_ref, att_ref, lse_ref, dout_in, cos_ref, sin_ref, extra_ref, x_ref, a_ref, gain_ref, dmid_ref,
-    att_in, gains_ref, f_grad, f_above, a_above, normed_far,
-    home_ref, f_in, f_in_above, a_in, a_in_above, gain_sum,
-    buf, dqkv_ref, low_ref, in_sum_ref, a_grad_ref, gain_grad_ref, heard,
+    att_in, att_in_above, dmid_above, in_grad_above, gains_ref, f_grad, f_above, f_heard, out_above, grad_above, normed_far,
+    home_ref, out_home, grad_home, f_in, f_in_above, a_in, a_in_above, gain_sum,
+    buf, dqkv_ref, low_ref, two_low, in_sum_ref, a_grad_ref, a_above, gain_grad_ref, heard, f_sum, f_sum_above, f_got,
     key_x, val_x, query_x, dout_x, dq, scores, along,
     total, out_c, in_c, rin, out_total, out_c2, in_c2, rin2,
-    rs_sems, rs2_sems, f_sems, f1_sems, a_sems, a1_sems, homing, gain_sems, loads,
+    rs_sems, rs2_sems, f_sems, f1_sems, a_sems, a1_sems, homing, out_homing, grad_homing, gain_sems, got_sems, loads,
 ):
     at = spot()
     y, x, c, h, p = at
-    copy = Stage(loads).copy(normed_far, buf)
+    stage = Stage(loads)
+    far = far_role(at)
+    copy = stage.copy(normed_far, buf)
     home = ToHome(at, 0, low_ref, lambda m: home_ref.at[m], homing)
-    early = [
-        ToShards(at, layer, by_columns(ref), place, sems, roles)
-        for layer, ref, place, sems, roles in (
-            (1, f_above, lambda role, j: f_in_above.at[j], f1_sems, (0,)),
-            (0, f_grad, lambda role, j: f_in.at[role, j], f_sems, (0, 1)),
-            (1, a_above, lambda role, j: a_in_above.at[role, j], a1_sems, (0, 1)),
-        )
+    homes = [
+        ToHome(at, 1, ref, lambda m, into=into: into.at[m], sems)
+        for ref, into, sems in ((out_above, out_home, out_homing), (grad_above, grad_home, grad_homing))
     ]
-    a_push = ToShards(at, 0, by_columns(a_grad_ref), lambda role, j: a_in.at[role, j], a_sems)
-    peers = [moved(at, 0, 1), moved(at, 1), moved(at, 2), moved(at, 4), (y, x, c, 1 - h, p)]
-    greet(at, home, a_push, *early, peers=peers[4:])
-    for push in early:
-        push.start()
-    steps = out_weight_steps(at, out_total, (out_c2, in_c2, rin2), rs2_sems, att_in, dmid_ref, low_ref)
+    f_push, f_push_above = (
+        ToShards(at, layer, by_columns(ref), lambda role, j, into=into: into.at[j], sems, (0,))
+        for layer, ref, into, sems in ((0, f_sum, f_in, f_sems), (1, f_sum_above, f_in_above, f1_sems))
+    )
+    a_push, a_push_above = (
+        ToShards(at, layer, by_columns(ref), lambda role, j, into=into: into.at[role, j], sems)
+        for layer, ref, into, sems in ((0, a_grad_ref, a_in, a_sems), (1, a_above, a_in_above, a1_sems))
+    )
+    peers = [moved(at, 0, 1), moved(at, 1), moved(at, 2), moved(at, 4), partner_of(at)]
+    greet(at, home, *homes, f_push, f_push_above, a_push, a_push_above, peers=peers[4:])
+    give = remote(f_grad, f_got, got_sems.at[0], got_sems.at[1], partner_of(at))
+
+    @pl.when(far == 1)
+    def _():
+        give.start()
+
+    @pl.when(far == 0)
+    def _():
+        pairs = ((f_above, f_sum_above), (f_heard, f_sum))
+        copies = [pltpu.make_async_copy(*pair, got_sems.at[2 + i]) for i, pair in enumerate(pairs)]
+        for one in copies:
+            one.start()
+        for one in copies:
+            one.wait()
+        f_sum_above[...] = (f_sum_above[...].astype(F32) + f_sum[...].astype(F32)).astype(LOW)
+        pltpu.make_async_copy(f_grad, f_sum, got_sems.at[2]).start()
+
+    f_push_above.start()
+    for one in homes:
+        one.start()
+    two_low[0] = dmid_ref[...].astype(LOW)
+    two_low[1] = dmid_above[...].astype(LOW)
+
+    def two_layers(b):
+        return jnp.concatenate([dot(att_in[b], two_low[0]), dot(att_in_above[b], two_low[1])])
+
+    steps = scattering(at, out_total, (out_c2, in_c2, rin2), rs2_sems, two_layers)
     attend_back_body(
         qkv_ref, seg_ref, att_ref, lse_ref, dout_in, cos_ref, sin_ref, extra_ref, dqkv_ref, None,
         key_x, val_x, query_x, dout_x, dq, scores, along, lambda ki: next(steps, None),
     )
     run(steps)
 
+    for i in range(3):
+        a_above[i] = in_grad_above[i * HS : (i + 1) * HS]
+    a_above[3] = out_total[HS:].astype(LOW)
+    a_push_above.start()
+
+    @pl.when(far == 0)
+    def _():
+        pltpu.make_async_copy(f_grad, f_sum, got_sems.at[2]).wait()
+        give.wait_recv()
+        f_sum[...] = (f_sum[...].astype(F32) + f_got[...].astype(F32)).astype(LOW)
+
+    f_push.start()
+
     def after():
-        put_grads(a_grad_ref, in_sum_ref, out_total)
+        put_grads(a_grad_ref, in_sum_ref, out_total[:HS])
         a_push.start()
 
     grad = input_back(
@@ -1618,10 +1624,13 @@
         copy.start()
         copy.wait()
         gain_sum[i + 1] = gain_sum[i] + heard[i]
-    for push in early:
+
+    @pl.when(far == 1)
+    def _():
+        give.wait_send()
+
+    for push in (*homes, f_push_above, f_push, a_push_above, a_push, home):
         push.finish()
-    a_push.finish()
-    home.finish()
 
 
 VMEM_SPEC = pl.BlockSpec(memory_space=pltpu.VMEM)
@@ -1850,7 +1859,7 @@
         for y in range(2)
         for s in range(4)
         for z in range(4)
-        if (y + s) % 2
+        if (y + s + z // 2) % 2 == 0
     ]
 
 
@@ -1888,7 +1897,7 @@
 
     buf = [vmem(16, rows, width)]
     boxes = sum_boxes(rows, width)
-    small_boxes = sum_boxes(HS, width)
+    small_boxes = sum_boxes(2 * HS, width)
     wo_buf = [vmem(16, HS, width)]
     low_head = [vmem(HS, length)]
     block, low_block = [vmem(rows, width, dtype=F32)], [vmem(rows, width)]
@@ -1912,7 +1921,7 @@
     )
     (
         qkv0, att0, lse0, att_in0, wo_all0, own_in, mid0, out0, qkv1,
-        normed0, nmid0, normed1, hid0, one0, two0, home_out0, a0, a1, f0, f1, gains, *_,
+        normed0, nmid0, normed1, hid0, one0, two0, a0, a1, f0, f1, gains,
     ) = reach(
         first_kernel,
         0,
@@ -1920,9 +1929,7 @@
         [turned_out, head_out, lse_out, att_in_out, near(16, HS, width), low_out, block_out, low_out, turned_out]
         + [every] * 3
         + [hidden_far] * 3
-        + [home_out, a_far, a_far, f_far, f_far, stays(2, 2, width, dtype=F32)]
-        + [stays(2, 4, HS, width // 4)] * 2
-        + [stays(2, 3, units, width // 4)] * 2,
+        + [a_far, a_far, f_far, f_far, stays(2, 2, width, dtype=F32)],
         buf
         + low_head
         + [vmem(4, HS, width), vmem(3, units, width), vmem(2, 2, width, dtype=F32)]
@@ -1931,7 +1938,7 @@
         + boxes
         + [links(), links(), links(), row_sems(), dma((16,))]
         + [head_sems()] * 4
-        + [dma((3,)), dma((3,)), dma((7,)), home_sems()],
+        + [dma((3,)), dma((3,)), dma((7,))],
         "first",
         [inputs, a_own, f_own, jnp.concatenate([attn_gain, mlp_gain])],
     )
@@ -1950,49 +1957,48 @@
         + [links(), links(), links(), row_sems(), row_sems(), dma((1,))],
         "turn",
     )
-    extra, gin1, dmid0, gmid0, dout0, f_grad0, a_grad1, home_grad1, home_out1, f_far1 = reach(
+    extra, gin1, dmid0, gmid0, dout0, f_grad0, in_grad1, grad1, out1, home_out0, f_heard1 = reach(
         lower_kernel,
         2,
-        [a1, gain_in[1], dmid1, att_in1, gain_mid[0]],
-        [head_out, gain_out, block_out, gain_out, dout_out, f_out, near(4, HS, width), home_out, home_out, f_half],
+        [a1, gain_in[1], dmid1, gain_mid[0]],
+        [head_out, gain_out, block_out, gain_out, dout_out, f_out, near(3 * HS, width), low_out, low_out, home_out, f_far],
         buf
         + wo_buf
         + [vmem(3 * HS, length)]
-        + low_block
-        + low_block
         + in_sum[:1]
         + dout_block
         + boxes
-        + small_boxes
-        + [links(), links(), links(), row_sems(), shard_sems(), home_sems(), home_sems()]
-        + [dma((18,)), dma((8,))],
+        + [links(), links(), row_sems(), dma((2,)), home_sems(), dma((18,)), dma((8,)), pltpu.SemaphoreType.REGULAR],
         "lower",
         [out0, f0, mid0, qkv1, segment, att1, lse1, dout1, *tables, hid0, one0, two0, normed1, nmid0, wo_all0]
-        + [hid1, mid1, f1, f_grad1],
-    )
-    home_grad0, f_in0, f_near1, a_in0, a_in1, gain_sums = reach(
+        + [hid1, mid1, f1, f_grad1, out0],
+    )
+    home_grad0, home_out1, home_grad1, f_in0, f_in1, a_in0, a_in1, gain_sums = reach(
         last_kernel,
         3,
-        [qkv0, segment, att0, lse0, dout0, *tables, extra, own_in, a0, gain_in[0], dmid0, att_in0]
-        + [jnp.concatenate([gin1, gmid0, gmid1])],
-        [home_out, f_shards, f_half, a_shards, a_shards, near(6, 4, width, dtype=F32)],
+        [qkv0, segment, att0, lse0, dout0, *tables, extra, own_in, a0, gain_in[0], dmid0, att_in0, att_in1, dmid1]
+        + [in_grad1, jnp.concatenate([gin1, gmid0, gmid1])],
+        [home_out] * 3 + [f_half, f_half, a_shards, a_shards, near(6, 4, width, dtype=F32)],
         buf
         + [vmem(3 * HS, length)]
         + low_block
+        + [vmem(2, rows, width)]
         + in_sum
-        + [vmem(1, width, dtype=F32), vmem(5, 4, width, dtype=F32)]
+        + [vmem(4, HS, width), vmem(1, width, dtype=F32), vmem(5, 4, width, dtype=F32)]
+        + [vmem(3, units, width)] * 3
         + attend_back_scratch(length)
         + boxes
         + small_boxes
         + [links(), links()]
         + [shard_sems()] * 4
-        + [home_sems(), dma((2, 5)), dma((1,))],
+        + [home_sems()] * 3
+        + [dma((2, 5)), dma((4,)), dma((1,))],
         "last",
-        [f_grad0, f_grad1, a_grad1, normed0],
+        [f_grad0, f_grad1, f_heard1, out1, grad1, normed0],
     )
     on_first = y == 0
     a_sum = jnp.sum(jnp.where(on_first, a_in0, a_in1).astype(F32), axis=0)
-    f_total = jnp.where(on_first, f_in0[0], f_near1).astype(F32) + jnp.where(on_first, f_in0[1], f_far1).astype(F32)
+    f_total = jnp.where(on_first, f_in0, f_in1).astype(F32)
     a_sum = jnp.transpose(a_sum, (1, 0, 2, 3)).reshape(4, 4 * HS, width // 4)
     f_total = jnp.transpose(f_total, (1, 0, 2, 3)).reshape(3, 4 * units, width // 4)
     layer_out = jnp.where(on_first, home_out0, home_out1)

time: 710 us -> 698 us (0.983)
  Pallas kernels: 677 us -> 662 us
    pallas_call x4, Pallas kernels: 677 us -> 662 us  [reach(): pl.pallas_call(kernel, out_shape=[jax.ShapeDtypeStruct(shape, dtype) for...]
  transfers between devices with their start and end apart: 1 -> 1, of which waited for: 0 -> 0; matrix products, arithmetic and copies ran while one was open for 1% -> 1% of each run, Pallas kernels for 34% -> 31%
where the time goes in v4:
time: 698 us; the launch traced here: 690 us
  Pallas kernels  662 us (95%)
  other arithmetic  11.1 us (2%)
  local copies, waits for them, and re-layouts  9.37 us (1%)
    pallas_call x4, Pallas kernels, reach(): pl.pallas_call(kernel, out_shape=[jax.ShapeDtypeStruct(shape, dtype) for...  662 us
  transfers between devices with their start and end apart: 1, of which 0 were waited for; matrix products, arithmetic and copies ran while one was open for 1% of the time, Pallas kernels for 31%

profile of v4, /device:TPU:0, one launch (start us, length us, event | category | flops | bytes accessed | tf_op | source)
XLA Modules:
  0.0 689.5 jit_solution(15671237000670458347)
XLA Ops:
  0.6 0.0 copy-start.15
  0.7 0.0 copy-start.16
  0.7 0.0 copy-start.11
  0.7 0.0 copy-start.12
  0.7 0.0 copy-start.13
  0.7 0.0 copy-start.14
  0.7 1.2 dynamic-slice_bitcast_fusion
  1.9 0.0 copy-start.8
  1.9 0.0 copy-start.9
  1.9 0.0 copy-start.10
  1.9 6.1 collective-permute-start
  8.1 0.7 fusion.3
  8.8 0.2 reduce-window.4
  8.9 0.7 fusion.2
  9.6 0.1 convert_reduce_fusion.1
  9.7 0.1 select_reduce_fusion
  9.9 2.8 multiply_sine_fusion
  12.7 0.0 copy-done.15
  12.7 0.0 copy-done.16
  12.7 0.0 copy-done.11
  12.7 0.1 copy.41
  12.8 0.0 copy-done.12
  12.8 0.1 copy.42
  12.9 0.0 copy-done.13
  12.9 0.1 copy.43
  13.1 0.0 copy-done.14
  13.1 0.9 pad_maximum_fusion.1.a_ref
  13.9 0.0 copy-done.8
  13.9 0.0 copy-done.9
  13.9 0.0 copy-done.10
  13.9 1.1 pad_maximum_fusion.f_ref
  15.0 0.0 copy-start.5
  15.0 215.4 %first.1 = (bf16[192,4096]{1,0:T(8,128)(2,1)}, f32[64,4096]{1,0:T(8,128)}, f32[1,4096]{1,0:T(1,128)S(1)}, bf16[16,64,256]{2,1,0:T(8,128)(2,1)S(1)}, bf16[16,64,1...) custom-call(f32[32,4096]{1,0:T(8,128)} %get-tuple-element.148.cos_re, ...), custom_call_target="tpu_custom_call" | custom-call | tf_op jit(solution)/shard_map/first/pallas_call | solution.py:1655
  230.5 0.0 copy-start
  230.5 0.8 copy-done
  231.3 0.0 collective-permute-done
  231.3 0.0 copy-done.5
  231.3 0.9 bitcast_select_fusion.top_ref
  232.2 135.0 %turn.1 = (f32[64,4096]{1,0:T(8,128)}, f32[1,4096]{1,0:T(1,128)S(1)}, bf16[16,64,256]{2,1,0:T(8,128)(2,1)S(1)}, f32[256,1024]{1,0:T(8,128)}, f32[1,1024]{1,0:T(1...) custom-call(bf16[192,4096]{1,0:T(8,128)(2,1)} %get-tuple-element.61., ...), custom_call_target="tpu_custom_call" | custom-call | tf_op jit(solution)/shard_map/turn/pallas_call | solution.py:1655
  367.2 0.0 copy-start.1
  367.2 0.8 copy-done.1
  368.0 174.6 %lower.1 = (f32[64,4096]{1,0:T(8,128)}, f32[1,1024]{1,0:T(1,128)S(1)}, f32[256,1024]{1,0:T(8,128)}, f32[1,1024]{1,0:T(1,128)S(1)}, bf16[64,4096]{1,0:T(8,128)(2,...) custom-call(bf16[4,64,1024]{2,1,0:T(8,128)(2,1)} %get-tuple-element., ...), custom_call_target="tpu_custom_call" | custom-call | tf_op jit(solution)/shard_map/lower/pallas_call | solution.py:1655
  542.6 0.0 copy-start.2
  542.6 0.8 copy-done.2
  543.4 136.8 %last.1 = (bf16[2,256,1024]{2,1,0:T(8,128)(2,1)}, bf16[2,256,1024]{2,1,0:T(8,128)(2,1)}, bf16[2,256,1024]{2,1,0:T(8,128)(2,1)}, bf16[4,3,176,256]{3,2,1,0:T(8,12...) custom-call(bf16[192,4096]{1,0:T(8,128)(2,1)} %get-tuple-element.80., ...), custom_call_target="tpu_custom_call" | custom-call | tf_op jit(solution)/shard_map/last/pallas_call | solution.py:1655
  680.2 0.1 constant_dynamic-slice_fusion
  680.3 0.5 fusion.1
  680.8 1.7 convert_reduce_fusion
  682.5 0.0 copy-start.3
  682.5 0.0 copy-start.4
  682.6 0.8 fusion.5
  683.3 0.8 copy.46
  684.2 0.0 copy-done.3
  684.2 0.0 copy-done.4
  684.2 0.1 convert_bitcast_fusion
  684.3 0.0 copy-start.7
  684.4 1.4 fusion.4
  685.7 0.0 copy-start.6
  685.7 0.8 copy.45
  686.6 0.8 copy.44
  687.4 0.0 copy-done.7
  687.4 0.0 copy-done.6
  687.4 1.9 bitcast_convert_fusion
  (6 shorter events, 0.1 us)
Async XLA Ops:
  0.6 12.0 %copy-start.15 = (f32[1,1024]{1,0:T(1,128)S(1)}, f32[1,1024]{1,0:T(1,128)}, u32[]{:S(2)}) copy-start(f32[1,1024]{1,0:T(1,128)} %param.23) | copy-start | bytes 12292
  0.7 12.0 %copy-start.16 = (f32[1,1024]{1,0:T(1,128)S(1)}, f32[1,1024]{1,0:T(1,128)}, u32[]{:S(2)}) copy-start(f32[1,1024]{1,0:T(1,128)} %param.22) | copy-start | bytes 12292
  0.7 12.0 %copy-start.11 = (bf16[1,256,256]{2,1,0:T(8,128)(2,1)S(1)}, bf16[1,256,256]{2,1,0:T(8,128)(2,1)}, u32[]{:S(2)}) copy-start(bf16[1,256,256]{2,1,0:T(8,128)(2,1)} %param.15) | copy-start | bytes 393220
  0.7 12.1 %copy-start.12 = (bf16[1,256,256]{2,1,0:T(8,128)(2,1)S(1)}, bf16[1,256,256]{2,1,0:T(8,128)(2,1)}, u32[]{:S(2)}) copy-start(bf16[1,256,256]{2,1,0:T(8,128)(2,1)} %param.16) | copy-start | bytes 393220
  0.7 12.3 %copy-start.13 = (bf16[1,256,256]{2,1,0:T(8,128)(2,1)S(1)}, bf16[1,256,256]{2,1,0:T(8,128)(2,1)}, u32[]{:S(2)}) copy-start(bf16[1,256,256]{2,1,0:T(8,128)(2,1)} %param.17) | copy-start | bytes 393220
  0.7 12.4 %copy-start.14 = (bf16[1,256,256]{2,1,0:T(8,128)(2,1)S(1)}, bf16[1,256,256]{2,1,0:T(8,128)(2,1)}, u32[]{:S(2)}) copy-start(bf16[1,256,256]{2,1,0:T(8,128)(2,1)} %param.18) | copy-start | bytes 393220
  1.9 12.0 %copy-start.8 = (bf16[1,704,256]{2,1,0:T(8,128)(2,1)S(1)}, bf16[1,704,256]{2,1,0:T(8,128)(2,1)}, u32[]{:S(2)}) copy-start(bf16[1,704,256]{2,1,0:T(8,128)(2,1)} %param.21) | copy-start | bytes 1081348
  1.9 12.0 %copy-start.9 = (bf16[1,256,704]{1,2,0:T(8,128)(2,1)S(1)}, bf16[1,256,704]{1,2,0:T(8,128)(2,1)}, u32[]{:S(2)}) copy-start(bf16[1,256,704]{1,2,0:T(8,128)(2,1)} %param.20) | copy-start | bytes 1081348
  1.9 12.0 %copy-start.10 = (bf16[1,256,704]{1,2,0:T(8,128)(2,1)S(1)}, bf16[1,256,704]{1,2,0:T(8,128)(2,1)}, u32[]{:S(2)}) copy-start(bf16[1,256,704]{1,2,0:T(8,128)(2,1)} %param.19) | copy-start | bytes 1081348
  1.9 229.3 %collective-permute-start = (bf16[256,1024]{1,0:T(8,128)(2,1)S(1)}, bf16[256,1024]{1,0:T(8,128)(2,1)S(1)}, u32[]{:S(2)}, u32[]{:S(2)}) collective-permute-start(bf16[256,1024]{1,0:T(8,128)(2,1)S(1)} %dynamic-slice_bitcast_fusion), channel_id=1, source_target_pairs={{0,2},{1,3},{6,4},{7,5},{8,10},{9,11},{14,12},{15,13},{18,16},{19,... | collective-permute-start | bytes 1572872 | tf_op jit(solution)/shard_map/ppermute | solution.py:1919
  15.0 216.2 %copy-start.5 = (bf16[2,256,1024]{2,1,0:T(8,128)(2,1)S(1)}, bf16[2,256,1024]{2,1,0:T(8,128)(2,1)}, u32[]{:S(2)}) copy-start(bf16[2,256,1024]{2,1,0:T(8,128)(2,1)} %param.13) | copy-start | bytes 3145732
  230.5 0.8 copy-start
  367.2 0.8 copy-start.1
  542.6 0.8 copy-start.2
  682.5 1.6 copy-start.3
  682.5 1.6 copy-start.4
  684.3 3.1 copy-start.7
  685.7 1.7 copy-start.6

commit v5 on v4

--- a/solution.py
+++ b/solution.py
@@ -566,8 +566,12 @@
     return [moved(at, mask, core) for mask in range(8) for core in range(2) if mask + core]
 
 
-def greet(at, *pushes, peers=()):
-    met = others(at) + list(peers)
+def neighbours(at):
+    return [moved(at, mask, core) for mask, core in ((1, 0), (2, 0), (4, 0), (0, 1))]
+
+
+def greet(at, *pushes, peers=(), all_rows=True):
+    met = (others(at) if all_rows else neighbours(at)) + list(peers)
     count = len(met)
     for peer in met:
         signal(peer)
@@ -1216,13 +1220,34 @@
     push.finish()
 
 
+def tables(lengths_ref, micro, cos_ref, sin_ref, seg_ref):
+    half, length = cos_ref.shape
+    index = lax.broadcasted_iota(jnp.int32, (half, 1), 0).astype(F32)
+    frequency = jnp.exp(index * (-math.log(10000.0) / half))
+    ends, end = [], 0
+    for i in range(lengths_ref.shape[1]):
+        end = end + lengths_ref[micro, i]
+        ends.append(end)
+    for part in tiles(length):
+        places = part.start + lax.broadcasted_iota(jnp.int32, (1, TILE), 1)
+        segment, start = jnp.zeros_like(places), jnp.zeros_like(places)
+        for end in ends:
+            past = places >= end
+            segment = segment + jnp.where(past, 1, 0)
+            start = jnp.where(past, end, start)
+        seg_ref[:, part] = segment
+        angles = (places - start).astype(F32) * frequency
+        cos_ref[:, part] = jnp.cos(angles)
+        sin_ref[:, part] = jnp.sin(angles)
+
+
 def first_kernel(
-    cos_ref, sin_ref, seg_ref, in_ref, a_ref, f_ref, gain_ref,
-    qkv0_ref, att_ref, lse_ref, att_in, wo_all, x_here, middle_ref, out_ref, qkv1_ref,
-    normed0_far, nmid_far, normed1_far, hidden_far, one_far, two_far, a0, a1, f0, f1, gains,
+    lengths_ref, in_ref, top_ref, a_ref, f_ref, gain_ref,
+    cos_ref, sin_ref, seg_ref, qkv0_ref, att_ref, lse_ref, att_in, wo_all, x_here, middle_ref, out_ref, qkv1_ref,
+    normed0_far, nmid_far, normed1_far, hidden_far, one_far, two_far, a0, a1, f0, f1, gains, top_here,
     buf, low_ref, a_here, f_here, gain_here, hidden_ref, one_ref, two_ref,
     key_x, query_x, val_x, scores, total, out_c, in_c, rin,
-    ag_sems, wo_sems, rs_sems, share_sems, block_sems, a0_sems, a1_sems, f0_sems, f1_sems, swap, gain_sems, loads,
+    ag_sems, wo_sems, rs_sems, share_sems, block_sems, a0_sems, a1_sems, f0_sems, f1_sems, swap, top_swap, gain_sems, loads,
 ):
     at = spot()
     y, x, c, h, p = at
@@ -1249,12 +1274,15 @@
         swapped.start()
         stays.start()
 
+    top_swapped = remote(top_ref.at[1 - h], top_here, top_swap.at[0], top_swap.at[1], partner)
+    top_stays = pltpu.make_async_copy(top_ref.at[h], top_here, top_swap.at[2])
     across = remote(gain_ref, gains.at[y], gain_sems.at[0], gain_sems.at[1], above)
     across.start()
     keeps = pltpu.make_async_copy(gain_ref, gains.at[y], gain_sems.at[2])
     keeps.start()
     for push in (a_pushes[0], f_pushes[0], a_pushes[1], f_pushes[1]):
         push.start()
+    tables(lengths_ref, h, cos_ref, sin_ref, seg_ref)
     a_pushes[0].forward()
     keeps.wait()
     across.wait_send()
@@ -1298,6 +1326,11 @@
         f_pushes[1].forward()
         copy.wait()
 
+        @pl.when(far == 0)
+        def _():
+            top_swapped.start()
+            top_stays.start()
+
     gather(at, buf, ag_sems, lambda b: up_block(b, buf, f_here, hidden_ref, one_ref, two_ref), keep, more)
     saves = [stage.copy(*pair) for pair in ((hidden_ref, hidden_far), (one_ref, one_far), (two_ref, two_far))]
     boxes = (out_c, in_c, rin)
@@ -1321,6 +1354,15 @@
     for save in saves:
         save.wait()
     f_pushes[1].finish()
+
+    @pl.when(far == 1)
+    def _():
+        top_swapped.wait_recv()
+
+    @pl.when(far == 0)
+    def _():
+        top_stays.wait()
+        top_swapped.wait_send()
 
 
 def turn_kernel(
@@ -1479,7 +1521,7 @@
         steps = out_steps(hidden_ref, down_ref)
         attend_back_staged(
             stage, (qkv_far, seg_far, att_far, lse_far, dout_far, cos_far, sin_far), (None, dqkv_ref, send_ref),
-            steps, 3, *refs,
+            steps, 1, *refs,
         )
 
     pl.run_scoped(
@@ -1521,6 +1563,7 @@
 
     ring_type = pltpu.VMEM((8, *nmid_far.shape[1:]), LOW)
     pl.run_scoped(rest, *feed_scratch(length, f_far), *staged_scratch((x_far, f_far, middle_far)), ring_type)
+
     home.finish()
 
     @pl.when(far == 1)
@@ -1535,32 +1578,35 @@
 def last_kernel(
     qkv_ref, seg_ref, att_ref, lse_ref, dout_in, cos_ref, sin_ref, extra_ref, x_ref, a_ref, gain_ref, dmid_ref,
     att_in, att_in_above, dmid_above, in_grad_above, gains_ref, f_grad, f_above, f_heard, out_above, grad_above, normed_far,
-    home_ref, out_home, grad_home, f_in, f_in_above, a_in, a_in_above, gain_sum,
+    out_home, grad_home, f_in, a_in, gain_sum,
     buf, dqkv_ref, low_ref, two_low, in_sum_ref, a_grad_ref, a_above, gain_grad_ref, heard, f_sum, f_sum_above, f_got,
     key_x, val_x, query_x, dout_x, dq, scores, along,
     total, out_c, in_c, rin, out_total, out_c2, in_c2, rin2,
-    rs_sems, rs2_sems, f_sems, f1_sems, a_sems, a1_sems, homing, out_homing, grad_homing, gain_sems, got_sems, loads,
+    rs_sems, rs2_sems, f_sems, f1_sems, a_sems, a1_sems, homing, out1_homing, grad_homing, gain_sems, got_sems, loads,
 ):
     at = spot()
     y, x, c, h, p = at
     stage = Stage(loads)
     far = far_role(at)
     copy = stage.copy(normed_far, buf)
-    home = ToHome(at, 0, low_ref, lambda m: home_ref.at[m], homing)
+    home = ToHome(at, 0, low_ref, lambda m: grad_home.at[m], homing)
     homes = [
-        ToHome(at, 1, ref, lambda m, into=into: into.at[m], sems)
-        for ref, into, sems in ((out_above, out_home, out_homing), (grad_above, grad_home, grad_homing))
+        ToHome(at, layer, ref, lambda m, into=into: into.at[m], sems)
+        for layer, ref, into, sems in (
+            (1, out_above, out_home, out1_homing),
+            (1, grad_above, grad_home, grad_homing),
+        )
     ]
     f_push, f_push_above = (
-        ToShards(at, layer, by_columns(ref), lambda role, j, into=into: into.at[j], sems, (0,))
-        for layer, ref, into, sems in ((0, f_sum, f_in, f_sems), (1, f_sum_above, f_in_above, f1_sems))
+        ToShards(at, layer, by_columns(ref), lambda role, j: f_in.at[j], sems, (0,))
+        for layer, ref, sems in ((0, f_sum, f_sems), (1, f_sum_above, f1_sems))
     )
     a_push, a_push_above = (
-        ToShards(at, layer, by_columns(ref), lambda role, j, into=into: into.at[role, j], sems)
-        for layer, ref, into, sems in ((0, a_grad_ref, a_in, a_sems), (1, a_above, a_in_above, a1_sems))
+        ToShards(at, layer, by_columns(ref), lambda role, j: a_in.at[role, j], sems)
+        for layer, ref, sems in ((0, a_grad_ref, a_sems), (1, a_above, a1_sems))
     )
     peers = [moved(at, 0, 1), moved(at, 1), moved(at, 2), moved(at, 4), partner_of(at)]
-    greet(at, home, *homes, f_push, f_push_above, a_push, a_push_above, peers=peers[4:])
+    greet(at, home, *homes, f_push, f_push_above, a_push, a_push_above, peers=peers[4:], all_rows=False)
     give = remote(f_grad, f_got, got_sems.at[0], got_sems.at[1], partner_of(at))
 
     @pl.when(far == 1)
@@ -1651,18 +1697,20 @@
     ]
 
 
-def reach(kernel, number, args, outs, scratch, name, far=()):
+def reach(kernel, number, args, outs, scratch, name, far=(), scalars=()):
     return pl.pallas_call(
         kernel,
         out_shape=[jax.ShapeDtypeStruct(shape, dtype) for shape, dtype, _ in outs],
-        in_specs=[VMEM_SPEC] * len(args) + [ANY_SPEC] * len(far),
+        in_specs=[pl.BlockSpec(memory_space=pltpu.SMEM)] * len(scalars)
+        + [VMEM_SPEC] * len(args)
+        + [ANY_SPEC] * len(far),
         out_specs=[ANY_SPEC if stays else VMEM_SPEC for _, _, stays in outs],
         scratch_shapes=scratch,
         compiler_params=pltpu.CompilerParams(
             collective_id=number, has_side_effects=number is not None, vmem_limit_bytes=VMEM_BYTES
         ),
         name=name,
-    )(*args, *far)
+    )(*scalars, *args, *far)
 
 
 TILE = 512
@@ -1849,39 +1897,14 @@
     ]
 
 
-def number_of(y, s, z):
-    return (y * 4 + s) * 4 + z
-
-
-def far_pairs():
-    return [
-        (number_of(y, s, z), number_of(y, s, (z + 2) % 4))
-        for y in range(2)
-        for s in range(4)
-        for z in range(4)
-        if (y + s + z // 2) % 2 == 0
-    ]
-
-
-AXES = ("section", "seq", "tensor")
-
-
 def on_grid(
     inputs, cotangent, lengths, w_query, w_key, w_value, w_out, w_gate, w_up, w_down, attn_gain, mlp_gain
 ):
     at = spot()
     y, x, c, half, p = at
-    far = far_role(at) == 1
     rows, width = inputs.shape[1:]
     length = 16 * rows
     units = w_gate.shape[2] // 4
-    length_row = lax.dynamic_index_in_dim(lengths, half, 0, keepdims=False)
-    places = jnp.arange(length, dtype=jnp.int32)
-    segment, within = doc_table(length_row, places)
-    segment = segment[None]
-    frequency = jnp.exp(jnp.arange(HS // 2, dtype=F32) * (-math.log(10000.0) / (HS // 2)))
-    angles = within.astype(F32)[None, :] * frequency[:, None]
-    tables = [jnp.cos(angles), jnp.sin(angles)]
     a_own = jnp.stack([w_query[0].T, w_key[0].T, w_value[0].T, w_out[0]])
     f_own = jnp.stack([w_gate[0].T, w_up[0].T, w_down[0]])
     dma = pltpu.SemaphoreType.DMA
@@ -1913,23 +1936,18 @@
     f_half = stays(4, 3, units, width // 4)
     a_shards, f_shards = stays(2, 4, 4, HS, width // 4), stays(2, 4, 3, units, width // 4)
 
-    both = lax.dynamic_index_in_dim(cotangent, 1 - half, 0, keepdims=False)
-    own_top = jnp.where(
-        far,
-        lax.ppermute(both, AXES, far_pairs()),
-        lax.dynamic_index_in_dim(cotangent, half, 0, keepdims=False),
-    )
+    table = near(HS // 2, length, dtype=F32)
     (
-        qkv0, att0, lse0, att_in0, wo_all0, own_in, mid0, out0, qkv1,
-        normed0, nmid0, normed1, hid0, one0, two0, a0, a1, f0, f1, gains,
+        cosine, sine, segment, qkv0, att0, lse0, att_in0, wo_all0, own_in, mid0, out0, qkv1,
+        normed0, nmid0, normed1, hid0, one0, two0, a0, a1, f0, f1, gains, own_top,
     ) = reach(
         first_kernel,
         0,
-        [*tables, segment],
-        [turned_out, head_out, lse_out, att_in_out, near(16, HS, width), low_out, block_out, low_out, turned_out]
+        [],
+        [table, table, near(1, length, dtype=jnp.int32), turned_out, head_out, lse_out, att_in_out, near(16, HS, width), low_out, block_out, low_out, turned_out]
         + [every] * 3
         + [hidden_far] * 3
-        + [a_far, a_far, f_far, f_far, stays(2, 2, width, dtype=F32)],
+        + [a_far, a_far, f_far, f_far, stays(2, 2, width, dtype=F32), stays(rows, width)],
         buf
         + low_head
         + [vmem(4, HS, width), vmem(3, units, width), vmem(2, 2, width, dtype=F32)]
@@ -1938,9 +1956,10 @@
         + boxes
         + [links(), links(), links(), row_sems(), dma((16,))]
         + [head_sems()] * 4
-        + [dma((3,)), dma((3,)), dma((7,))],
+        + [dma((3,)), dma((3,)), dma((3,)), dma((7,))],
         "first",
-        [inputs, a_own, f_own, jnp.concatenate([attn_gain, mlp_gain])],
+        [inputs, cotangent, a_own, f_own, jnp.concatenate([attn_gain, mlp_gain])],
+        [lengths],
     )
     gain_in, gain_mid = [gains[i, 0:1] for i in range(2)], [gains[i, 1:2] for i in range(2)]
     att1, lse1, att_in1, dmid1, gmid1, dout1, f_grad1, mid1, hid1 = reach(
@@ -1970,15 +1989,15 @@
         + boxes
         + [links(), links(), row_sems(), dma((2,)), home_sems(), dma((18,)), dma((8,)), pltpu.SemaphoreType.REGULAR],
         "lower",
-        [out0, f0, mid0, qkv1, segment, att1, lse1, dout1, *tables, hid0, one0, two0, normed1, nmid0, wo_all0]
+        [out0, f0, mid0, qkv1, segment, att1, lse1, dout1, cosine, sine, hid0, one0, two0, normed1, nmid0, wo_all0]
         + [hid1, mid1, f1, f_grad1, out0],
     )
-    home_grad0, home_out1, home_grad1, f_in0, f_in1, a_in0, a_in1, gain_sums = reach(
+    home_out1, grad_home, f_in, a_in, gain_sums = reach(
         last_kernel,
         3,
-        [qkv0, segment, att0, lse0, dout0, *tables, extra, own_in, a0, gain_in[0], dmid0, att_in0, att_in1, dmid1]
+        [qkv0, segment, att0, lse0, dout0, cosine, sine, extra, own_in, a0, gain_in[0], dmid0, att_in0, att_in1, dmid1]
         + [in_grad1, jnp.concatenate([gin1, gmid0, gmid1])],
-        [home_out] * 3 + [f_half, f_half, a_shards, a_shards, near(6, 4, width, dtype=F32)],
+        [home_out, home_out, f_half, a_shards, near(6, 4, width, dtype=F32)],
         buf
         + [vmem(3 * HS, length)]
         + low_block
@@ -1997,20 +2016,18 @@
         [f_grad0, f_grad1, f_heard1, out1, grad1, normed0],
     )
     on_first = y == 0
-    a_sum = jnp.sum(jnp.where(on_first, a_in0, a_in1).astype(F32), axis=0)
-    f_total = jnp.where(on_first, f_in0, f_in1).astype(F32)
+    a_sum = jnp.sum(a_in.astype(F32), axis=0)
+    f_total = f_in.astype(F32)
     a_sum = jnp.transpose(a_sum, (1, 0, 2, 3)).reshape(4, 4 * HS, width // 4)
     f_total = jnp.transpose(f_total, (1, 0, 2, 3)).reshape(3, 4 * units, width // 4)
-    layer_out = jnp.where(on_first, home_out0, home_out1)
-    input_grad = jnp.where(on_first, home_grad0, home_grad1).astype(F32)
     share = width // 16
     first_col = (4 * (2 * x + c) + 2 * half + p) * share
     gain_share = lax.dynamic_slice_in_dim(gain_sums[5], first_col, share, 1)
     gain_in_share = jnp.where(on_first, gain_share[0:1], gain_share[1:2])
     gain_mid_share = jnp.where(on_first, gain_share[2:3], gain_share[3:4])
     return (
-        layer_out[None],
-        input_grad[None],
+        jnp.where(on_first, home_out0, home_out1)[None],
+        grad_home.astype(F32)[None],
         a_sum[0].T[None],
         a_sum[1].T[None],
         a_sum[2].T[None],

time: 698 us -> 694 us (level)
  transfers between devices with their start and end apart: 1 -> 0, of which waited for: 0 -> 0; matrix products, arithmetic and copies ran while one was open for 1% -> 0% of each run, Pallas kernels for 31% -> 0%
where the time goes in v5:
time: 694 us; the launch traced here: 685 us
  Pallas kernels  668 us (96%)
  local copies, waits for them, and re-layouts  8.7 us (1%)
  other arithmetic  7.31 us (1%)
    pallas_call x4, Pallas kernels, reach(): pl.pallas_call(kernel, out_shape=[jax.ShapeDtypeStruct(shape, dtype) for...  668 us

profile of v5, /device:TPU:0, one launch (start us, length us, event | category | flops | bytes accessed | tf_op | source)
XLA Modules:
  0.0 685.2 jit_solution(5747692129981908020)
XLA Ops:
  0.6 0.0 copy-start.8
  0.7 0.0 copy-start.9
  0.7 0.0 copy-start.10
  0.7 0.0 copy-start.11
  0.7 0.0 copy-start.12
  0.7 0.0 copy-start.13
  0.7 0.0 copy-start.3
  0.7 2.4 pad_maximum_fusion.f_ref
  3.1 0.0 copy-done.8
  3.1 0.1 copy.35
  3.2 0.0 copy-done.9
  3.2 0.1 copy.36
  3.3 0.0 copy-done.10
  3.4 0.1 copy.37
  3.5 0.0 copy-done.11
  3.5 0.9 pad_maximum_fusion.1.a_ref
  4.3 0.0 copy-done.12
  4.3 0.0 copy-done.13
  4.3 0.0 copy-done.3
  4.4 222.9 %first.1 = (f32[32,4096]{1,0:T(8,128)S(1)}, f32[32,4096]{1,0:T(8,128)}, s32[1,4096]{1,0:T(1,128)S(1)}, bf16[192,4096]{1,0:T(8,128)(2,1)}, f32[64,4096]{1,0:T(8,1...) custom-call(s32[2,4]{1,0:T(2,128)S(1)} %copy-done.3, ...), custom_call_target="tpu_custom_call" | custom-call | tf_op jit(solution)/shard_map/first/pallas_call | solution.py:1701
  227.2 0.0 copy-start
  227.3 0.8 copy-done
  228.1 132.3 %turn.1 = (f32[64,4096]{1,0:T(8,128)}, f32[1,4096]{1,0:T(1,128)S(1)}, bf16[16,64,256]{2,1,0:T(8,128)(2,1)S(1)}, f32[256,1024]{1,0:T(8,128)}, f32[1,1024]{1,0:T(1...) custom-call(bf16[192,4096]{1,0:T(8,128)(2,1)} %get-tuple-element.62., ...), custom_call_target="tpu_custom_call" | custom-call | tf_op jit(solution)/shard_map/turn/pallas_call | solution.py:1701
  360.4 0.0 copy-start.1
  360.4 0.8 copy-done.1
  361.2 175.6 %lower.1 = (f32[64,4096]{1,0:T(8,128)}, f32[1,1024]{1,0:T(1,128)S(1)}, f32[256,1024]{1,0:T(8,128)}, f32[1,1024]{1,0:T(1,128)S(1)}, bf16[64,4096]{1,0:T(8,128)(2,...) custom-call(bf16[4,64,1024]{2,1,0:T(8,128)(2,1)} %get-tuple-element., ...), custom_call_target="tpu_custom_call" | custom-call | tf_op jit(solution)/shard_map/lower/pallas_call | solution.py:1701
  536.8 0.0 copy-start.2
  536.8 0.8 copy-done.2
  537.6 137.0 %last.1 = (bf16[2,256,1024]{2,1,0:T(8,128)(2,1)}, bf16[2,256,1024]{2,1,0:T(8,128)(2,1)}, bf16[4,3,176,256]{3,2,1,0:T(8,128)(2,1)}, bf16[2,4,4,64,256]{4,3,2,1,0:T(8,128)(2,1)}, f32[6,4,1024]{2,1,0:T(4,128)S(1)}) custom-call(bf16[192,4096]{1,0:T(8,128)(2,1)} %get-tuple-element.85.qkv_ref, s32[1,4096]{1,0:T(1,128)S(1)} %get-tuple-element.63.seg_ref.seg_far, ...), custom_call_target="tpu_custom_call" | custom-call | tf_op jit(solution)/shard_map/last/pallas_call | solution.py:1701
  674.6 1.4 convert_bitcast_fusion
  676.1 0.0 copy-start.4
  676.1 0.0 copy-start.5
  676.1 0.0 copy-start.6
  676.1 1.4 fusion.2
  677.5 0.3 copy-done.4
  677.8 0.6 copy-done.5
  678.4 0.3 copy-done.6
  678.7 0.0 copy-start.7
  678.7 1.9 bitcast_convert_fusion
  680.6 0.0 copy-done.7
  680.6 0.2 convert_reduce_fusion
  680.8 0.8 fusion.3
  681.6 0.8 copy.38
  682.4 0.8 copy.39
  683.3 0.8 copy.40
  684.1 0.1 constant_dynamic-slice_fusion
  684.2 0.5 fusion.1
  (4 shorter events, 0.0 us)
Async XLA Ops:
  0.6 2.5 copy-start.8
  0.7 2.6 copy-start.9
  0.7 2.7 copy-start.10
  0.7 2.8 copy-start.11
  0.7 3.6 copy-start.12
  0.7 3.6 copy-start.13
  0.7 3.6 copy-start.3
  227.2 0.8 copy-start
  360.4 0.8 copy-start.1
  536.8 0.8 copy-start.2
  676.1 1.7 copy-start.4
  676.1 2.3 copy-start.5
  676.1 2.6 copy-start.6
  678.7 1.9 copy-start.7
